TPU v7x, 32 devices: a whole 2x2x4 slice. The times are simulated.
32 devices in a mesh: section: 2 (over core), dp: 16 (over z, y, x).
Axes of the slice: x: 2, y: 2, z: 4, core: 2. Of those that a mesh axis runs over, the one named last changes fastest.
Arguments:
- byte_ids: int32 [2, 16, 512], P(None, 'dp'), may hold values from 0 to 258
- lengths: int32 [2, 16], P(None, 'dp'), may hold values from 33 to 512, as said below
- groups: int32 [2, 16], P(None, 'dp'), may hold values from 0 to 15
- embedding: float32 [259, 768], P(None, ('section', 'dp')), may hold values from -6 to 6
- language: float32 [16, 768], P(None, ('section', 'dp')), may hold values from -3 to 3
- scorer: float32 [768], P(('section', 'dp')), may hold values from -0.21875 to 0.21875
- prenorm: float32 [768], P(('section', 'dp')), may hold values from 0.5 to 1.5
- query_weight: float32 [768, 768], P(('section', 'dp')), may hold values from -0.109375 to 0.109375
- key_weight: float32 [768, 768], P(('section', 'dp')), may hold values from -0.109375 to 0.109375
- value_weight: float32 [768, 768], P(('section', 'dp')), may hold values from -0.21875 to 0.21875
- output_weight: float32 [768, 768], P(('section', 'dp')), may hold values from -1.75 to 1.75
- midnorm: float32 [768], P(('section', 'dp')), may hold values from 0.5 to 1.5
- gate_weight: float32 [768, 2048], P(('section', 'dp')), may hold values from -0.21875 to 0.21875
- up_weight: float32 [768, 2048], P(('section', 'dp')), may hold values from -0.21875 to 0.21875
- down_weight: float32 [2048, 768], P(('section', 'dp')), may hold values from -0.125 to 0.125
- relative: float32 [32, 12], replicated, may hold values from -4 to 4
- cotangent: bfloat16 [2, 16, 256, 768], P(None, 'dp'), may hold values from -6 to 6
Outputs:
- encoded: bfloat16 [2, 16, 256, 768], P(None, 'dp', None, 'section')
- embedding_grad: float32 [259, 768], P(None, ('section', 'dp'))
- language_grad: float32 [16, 768], P(None, ('section', 'dp'))
- scorer_grad: float32 [768], P(('section', 'dp'))
- prenorm_grad: float32 [768], P(('section', 'dp'))
- query_grad: float32 [768, 768], P(('section', 'dp'))
- key_grad: float32 [768, 768], P(('section', 'dp'))
- value_grad: float32 [768, 768], P(('section', 'dp'))
- output_grad: float32 [768, 768], P(('section', 'dp'))
- midnorm_grad: float32 [768], P(('section', 'dp'))
- gate_grad: float32 [768, 2048], P(('section', 'dp'))
- up_grad: float32 [768, 2048], P(('section', 'dp'))
- down_grad: float32 [2048, 768], P(('section', 'dp'))
- relative_grad: float32 [32, 12], replicated
Inputs may be any that keep to these rules, and one draw needn't show every extreme that they name: `lengths`: some row has 512 bytes.
All inputs are finite; a program needn't handle non-finite values.
Results may differ from a plain program's by a relative error of at most 0.014.
The roundings to bfloat16 on the way count: a program that leaves them out, or rounds other values in their place, can miss the bound.
Values may be sent and summed in bfloat16 or wider, within the bound.
A program may use at most 256 MiB of HBM per device.

v0:
```python
import jax
import jax.numpy as jnp
from jax import lax
from jax.sharding import PartitionSpec as P

HEAD_DIM = 64
BLOCKS = 4
DOWN = 2
MICRO = 2


HIGHEST = lax.Precision.HIGHEST
EPSILON = 1e-06
NEGATIVE = -1000000000.0
LIMITS = (12, 16, 23, 32, 46, 64, 91)


def from_behind(block, axis, distance):
    devices = range(lax.axis_size(axis))
    route = [(i - distance, i) for i in devices if i - distance in devices]
    return lax.ppermute(block, axis, route)


def bucket_ids(offsets):
    distance = jnp.abs(offsets)
    larger = 8 + sum(((distance >= limit).astype(jnp.int32) for limit in LIMITS))
    inside = jnp.where(distance < 8, distance, larger)
    return jnp.where(offsets > 0, 16, 0).astype(jnp.int32) + inside


def tokenize(table, language, scorer, symbols, length, group):
    count = symbols.shape[1]
    positions = jnp.arange(count)
    valid = positions[None, :] < length[:, None]
    gathered = jnp.take(table, symbols, axis=0) + jnp.take(language, group, axis=0)[:, None, :]
    embedded = jnp.where(valid[:, :, None], gathered, 0.0)
    means = []
    scores = []
    for size in range(1, BLOCKS + 1):
        extra = -count % size
        padded = jnp.pad(embedded, ((0, 0), (0, extra), (0, 0)))
        pooled = padded.reshape(padded.shape[0], -1, size, padded.shape[2]).sum(2) / size
        rated = jnp.einsum("rjd,d->rj", pooled, scorer, precision=HIGHEST)
        means.append(jnp.repeat(pooled, size, axis=1)[:, :count])
        scores.append(jnp.repeat(rated, size, axis=1)[:, :count])
    chosen = jax.nn.softmax(jnp.stack(scores, -1), axis=-1)
    latent = sum((chosen[..., index, None] * means[index] for index in range(BLOCKS)))
    return latent.reshape(latent.shape[0], count // DOWN, DOWN, latent.shape[2]).mean(2)


def rms_scale(values, gain):
    return values * lax.rsqrt(jnp.mean(values * values, -1, keepdims=True) + EPSILON) * gain


def gelu_tanh(values):
    return jax.nn.gelu(values, approximate=True)


def product_of(left, right):
    return jnp.dot(left, right, preferred_element_type=jnp.float32)


def outer_sum(left, right):
    return jnp.einsum("tf,tg->fg", left, right, preferred_element_type=jnp.float32)


def times_transposed(left, matrix):
    return jnp.einsum("tg,fg->tf", left, matrix, preferred_element_type=jnp.float32)


def relative_tables(relative, tokens):
    offsets = jnp.arange(tokens)[None, :] - jnp.arange(tokens)[:, None]
    flat_ids = bucket_ids(offsets).reshape(tokens * tokens)
    selector = (flat_ids[:, None] == jnp.arange(relative.shape[0])[None, :]).astype(jnp.float32)
    bias = jnp.dot(selector, relative, precision=HIGHEST).T.reshape(
        relative.shape[1], tokens, tokens
    )
    return (selector.astype(jnp.bfloat16), bias)


def block_scores(query, keys_row, valid_row, bias):
    scores = jnp.einsum("qhe,khe->hqk", query, keys_row, preferred_element_type=jnp.float32)
    scores = scores + bias
    return jnp.where(valid_row[None, None, :], scores, NEGATIVE)


def attend(queries, keys, values, valid, bias):
    rows, tokens, heads, depth = queries.shape
    width = min(512, tokens)
    blocks = tokens // width

    def one_block(index):
        row = index // blocks
        query = lax.dynamic_index_in_dim(queries, row, 0, False)
        keys_row = lax.dynamic_index_in_dim(keys, row, 0, False)
        values_row = lax.dynamic_index_in_dim(values, row, 0, False)
        valid_row = lax.dynamic_index_in_dim(valid, row, 0, False)
        scores = block_scores(query, keys_row, valid_row, bias)
        top = jnp.max(scores, -1, keepdims=True)
        raised = jnp.exp(scores - top)
        total = jnp.sum(raised, -1, keepdims=True)
        softmaxed = (raised / total).astype(jnp.bfloat16)
        mixed = jnp.einsum(
            "hqk,khe->qhe", softmaxed, values_row, preferred_element_type=jnp.float32
        )
        return (mixed.astype(jnp.bfloat16), (top + jnp.log(total))[..., 0])

    mixed, logsum = lax.map(one_block, jnp.arange(rows * blocks))
    return (mixed.reshape(rows, tokens, heads, depth), logsum)


def attend_back(queries, keys, values, valid, bias, selector, logsum, mixed_delta):
    rows, tokens, heads, depth = queries.shape
    width = min(512, tokens)
    blocks = tokens // width

    def one_block(carry, index):
        key_total, value_total, table_total = carry
        row = index // blocks
        query = lax.dynamic_index_in_dim(queries, row, 0, False)
        mixed_part = lax.dynamic_index_in_dim(mixed_delta, row, 0, False)
        keys_row = lax.dynamic_index_in_dim(keys, row, 0, False)
        values_row = lax.dynamic_index_in_dim(values, row, 0, False)
        valid_row = lax.dynamic_index_in_dim(valid, row, 0, False)
        scores = block_scores(query, keys_row, valid_row, bias)
        softmaxed = jnp.exp(scores - lax.dynamic_index_in_dim(logsum, index, 0, False)[..., None])
        weight_delta = jnp.einsum(
            "qhe,khe->hqk", mixed_part, values_row, preferred_element_type=jnp.float32
        )
        inner = jnp.sum(softmaxed * weight_delta, -1, keepdims=True)
        score_delta = jnp.where(
            valid_row[None, None, :], softmaxed * (weight_delta - inner), 0.0
        ).astype(jnp.bfloat16)
        query_part = jnp.einsum(
            "hqk,khe->qhe", score_delta, keys_row, preferred_element_type=jnp.float32
        ).astype(jnp.bfloat16)
        key_part = jnp.einsum(
            "hqk,qhe->khe", score_delta, query, preferred_element_type=jnp.float32
        )
        value_part = jnp.einsum(
            "hqk,qhe->khe",
            softmaxed.astype(jnp.bfloat16),
            mixed_part,
            preferred_element_type=jnp.float32,
        )
        key_total = lax.dynamic_update_index_in_dim(
            key_total, lax.dynamic_index_in_dim(key_total, row, 0, False) + key_part, row, 0
        )
        value_total = lax.dynamic_update_index_in_dim(
            value_total, lax.dynamic_index_in_dim(value_total, row, 0, False) + value_part, row, 0
        )
        table_total = table_total + jnp.dot(
            score_delta.reshape(heads, width * tokens), selector, preferred_element_type=jnp.float32
        )
        return ((key_total, value_total, table_total), query_part)

    empty = jnp.zeros(keys.shape, jnp.float32)
    start_carry = (empty, empty, jnp.zeros((heads, selector.shape[1]), jnp.float32))
    (key_total, value_total, table_total), query_parts = lax.scan(
        one_block, start_carry, jnp.arange(rows * blocks)
    )
    query_delta = query_parts.reshape(rows, tokens, heads, depth)
    return (
        query_delta,
        key_total.astype(jnp.bfloat16),
        value_total.astype(jnp.bfloat16),
        table_total,
    )


def encoder_step(received, upstream, valid, weights, selector, bias):
    prenorm, query_w, key_w, value_w, output_w, midnorm, gate_w, up_w, down_w = weights
    rows, tokens, width = received.shape
    heads = width // HEAD_DIM
    hidden = received.astype(jnp.float32).reshape(rows * tokens, width)
    normed, norm_back = jax.vjp(rms_scale, hidden, prenorm.astype(jnp.float32))
    normed_low = normed.astype(jnp.bfloat16)

    def heads_of(matrix):
        return (
            product_of(normed_low, matrix)
            .astype(jnp.bfloat16)
            .reshape(rows, tokens, heads, HEAD_DIM)
        )

    queries = heads_of(query_w)
    keys = heads_of(key_w)
    values = heads_of(value_w)
    mixed, logsum = attend(queries, keys, values, valid, bias)
    mixed_flat = mixed.reshape(rows * tokens, width)
    middle = hidden + product_of(mixed_flat, output_w)
    second, second_back = jax.vjp(rms_scale, middle, midnorm.astype(jnp.float32))
    second_low = second.astype(jnp.bfloat16)
    gate = product_of(second_low, gate_w)
    upper = product_of(second_low, up_w)
    activated, gelu_back = jax.vjp(gelu_tanh, gate)
    product = (activated * upper).astype(jnp.bfloat16)
    result = middle + product_of(product, down_w)
    outer = upstream.reshape(rows * tokens, width)
    down_grad = outer_sum(product, outer)
    product_delta = times_transposed(outer, down_w)
    gate_delta = gelu_back(product_delta * upper)[0].astype(jnp.bfloat16)
    upper_delta = (product_delta * activated).astype(jnp.bfloat16)
    gate_grad = outer_sum(second_low, gate_delta)
    up_grad = outer_sum(second_low, upper_delta)
    second_delta = times_transposed(gate_delta, gate_w) + times_transposed(upper_delta, up_w)
    middle_norm, midnorm_grad = second_back(second_delta)
    middle_delta = outer.astype(jnp.float32) + middle_norm
    attend_delta = middle_delta.astype(jnp.bfloat16)
    output_grad = outer_sum(mixed_flat, attend_delta)
    mixed_delta = (
        times_transposed(attend_delta, output_w)
        .astype(jnp.bfloat16)
        .reshape(rows, tokens, heads, HEAD_DIM)
    )
    query_delta, key_delta, value_delta, table_total = attend_back(
        queries, keys, values, valid, bias, selector, logsum, mixed_delta
    )
    query_flat = query_delta.reshape(rows * tokens, width)
    key_flat = key_delta.reshape(rows * tokens, width)
    value_flat = value_delta.reshape(rows * tokens, width)
    query_grad = outer_sum(normed_low, query_flat)
    key_grad = outer_sum(normed_low, key_flat)
    value_grad = outer_sum(normed_low, value_flat)
    normed_delta = (
        times_transposed(query_flat, query_w)
        + times_transposed(key_flat, key_w)
        + times_transposed(value_flat, value_w)
    )
    hidden_norm, prenorm_grad = norm_back(normed_delta)
    hidden_delta = (middle_delta + hidden_norm).astype(jnp.bfloat16).reshape(rows, tokens, width)
    table_part = table_total.T
    grads = (
        prenorm_grad,
        query_grad,
        key_grad,
        value_grad,
        output_grad,
        midnorm_grad,
        gate_grad,
        up_grad,
        down_grad,
    )
    return (
        hidden_delta,
        result.astype(jnp.bfloat16).reshape(rows, tokens, width),
        grads,
        table_part,
    )


def body(
    byte_ids,
    lengths,
    groups,
    embedding,
    language,
    scorer,
    prenorm,
    query_weight,
    key_weight,
    value_weight,
    output_weight,
    midnorm,
    gate_weight,
    up_weight,
    down_weight,
    relative,
    cotangent,
):
    masters = (
        embedding,
        language,
        scorer,
        prenorm,
        query_weight,
        key_weight,
        value_weight,
        output_weight,
        midnorm,
        gate_weight,
        up_weight,
        down_weight,
    )
    (
        embedding_low,
        language_low,
        scorer_low,
        prenorm_low,
        query_low,
        key_low,
        value_low,
        output_low,
        midnorm_low,
        gate_low,
        up_low,
        down_low,
    ) = tuple((item.astype(jnp.bfloat16) for item in masters))
    first = lax.axis_index("section") == 0
    sections = lax.axis_size("section")
    full = (
        lax.all_gather(embedding_low, ("section", "dp"), axis=1, tiled=True),
        lax.all_gather(language_low, ("section", "dp"), axis=1, tiled=True),
        lax.all_gather(scorer_low, ("section", "dp"), axis=0, tiled=True),
        lax.all_gather(prenorm_low, ("section", "dp"), axis=0, tiled=True),
        lax.all_gather(query_low, ("section", "dp"), axis=0, tiled=True),
        lax.all_gather(key_low, ("section", "dp"), axis=0, tiled=True),
        lax.all_gather(value_low, ("section", "dp"), axis=0, tiled=True),
        lax.all_gather(output_low, ("section", "dp"), axis=0, tiled=True),
        lax.all_gather(midnorm_low, ("section", "dp"), axis=0, tiled=True),
        lax.all_gather(gate_low, ("section", "dp"), axis=0, tiled=True),
        lax.all_gather(up_low, ("section", "dp"), axis=0, tiled=True),
        lax.all_gather(down_low, ("section", "dp"), axis=0, tiled=True),
    )
    full = tuple(full)
    tokenizer_set = (
        full[0].astype(jnp.float32),
        full[1].astype(jnp.float32),
        full[2].astype(jnp.float32),
    )
    encoder_set = full[3:]
    rows = byte_ids.shape[1]
    tokens = byte_ids.shape[2] // DOWN
    width = full[0].shape[1]
    half = width // sections
    selector, bias = relative_tables(relative, tokens)
    front_grads = tuple((jnp.zeros(item.shape, jnp.float32) for item in tokenizer_set))
    back_grads = tuple((jnp.zeros(item.shape, jnp.float32) for item in encoder_set))
    table_grad = jnp.zeros(relative.shape, jnp.float32)
    kept = []
    for micro in range(MICRO):
        symbols = byte_ids[micro]
        length = lengths[micro]
        group = groups[micro]
        valid = jnp.arange(tokens)[None, :] * DOWN < length[:, None]

        def tokenize_forward():
            return tokenize(
                tokenizer_set[0], tokenizer_set[1], tokenizer_set[2], symbols, length, group
            ).astype(jnp.bfloat16)

        def tokenize_skip():
            return jnp.zeros((rows, tokens, width), jnp.bfloat16)

        sent = lax.cond(first, tokenize_forward, tokenize_skip)
        received = from_behind(sent, "section", 1)
        upstream = cotangent[micro]

        def encoder_run():
            hidden_delta, encoded, grads, table_part = encoder_step(
                received, upstream, valid, encoder_set, selector, bias
            )
            summed = tuple((total + part for total, part in zip(back_grads, grads)))
            return (hidden_delta, encoded, summed, table_grad + table_part)

        def encoder_skip():
            blank = jnp.zeros((rows, tokens, width), jnp.bfloat16)
            return (blank, blank, back_grads, table_grad)

        hidden_delta, encoded, back_grads, table_grad = lax.cond(first, encoder_skip, encoder_run)
        returned, front_half = from_behind((hidden_delta, encoded[..., :half]), "section", -1)

        def tokenize_back():

            def local(table, lang_table, score_vector):
                return tokenize(table, lang_table, score_vector, symbols, length, group)

            latent_value, pullback = jax.vjp(
                local, tokenizer_set[0], tokenizer_set[1], tokenizer_set[2]
            )
            parts = pullback(returned.astype(jnp.float32))
            return tuple((total + part for total, part in zip(front_grads, parts)))

        def tokenize_keep():
            return front_grads

        front_grads = lax.cond(first, tokenize_back, tokenize_keep)
        kept.append(jnp.where(first, front_half, encoded[..., half:]))
    encoded_out = jnp.stack(kept)
    grads = tuple(front_grads) + tuple(back_grads)
    shards = (
        lax.psum_scatter(grads[0], ("section", "dp"), scatter_dimension=1, tiled=True),
        lax.psum_scatter(grads[1], ("section", "dp"), scatter_dimension=1, tiled=True),
        lax.psum_scatter(grads[2], ("section", "dp"), scatter_dimension=0, tiled=True),
        lax.psum_scatter(grads[3], ("section", "dp"), scatter_dimension=0, tiled=True),
        lax.psum_scatter(grads[4], ("section", "dp"), scatter_dimension=0, tiled=True),
        lax.psum_scatter(grads[5], ("section", "dp"), scatter_dimension=0, tiled=True),
        lax.psum_scatter(grads[6], ("section", "dp"), scatter_dimension=0, tiled=True),
        lax.psum_scatter(grads[7], ("section", "dp"), scatter_dimension=0, tiled=True),
        lax.psum_scatter(grads[8], ("section", "dp"), scatter_dimension=0, tiled=True),
        lax.psum_scatter(grads[9], ("section", "dp"), scatter_dimension=0, tiled=True),
        lax.psum_scatter(grads[10], ("section", "dp"), scatter_dimension=0, tiled=True),
        lax.psum_scatter(grads[11], ("section", "dp"), scatter_dimension=0, tiled=True),
    )
    relative_grad = lax.psum(table_grad, ("section", "dp"))
    return (
        encoded_out,
        shards[0],
        shards[1],
        shards[2],
        shards[3],
        shards[4],
        shards[5],
        shards[6],
        shards[7],
        shards[8],
        shards[9],
        shards[10],
        shards[11],
        relative_grad,
    )


def solution(mesh):
    return jax.shard_map(
        body,
        mesh=mesh,
        in_specs=(
            P(None, "dp", None),
            P(None, "dp"),
            P(None, "dp"),
            P(None, ("section", "dp")),
            P(None, ("section", "dp")),
            P(("section", "dp")),
            P(("section", "dp")),
            P(("section", "dp"), None),
            P(("section", "dp"), None),
            P(("section", "dp"), None),
            P(("section", "dp"), None),
            P(("section", "dp")),
            P(("section", "dp"), None),
            P(("section", "dp"), None),
            P(("section", "dp"), None),
            P(),
            P(None, "dp", None, None),
        ),
        out_specs=(
            P(None, "dp", None, "section"),
            P(None, ("section", "dp")),
            P(None, ("section", "dp")),
            P(("section", "dp")),
            P(("section", "dp")),
            P(("section", "dp"), None),
            P(("section", "dp"), None),
            P(("section", "dp"), None),
            P(("section", "dp"), None),
            P(("section", "dp")),
            P(("section", "dp"), None),
            P(("section", "dp"), None),
            P(("section", "dp"), None),
            P(),
        ),
        check_vma=False,
    )
```

profile of v0, /device:TPU:1, one launch (start us, length us, event | category | flops | bytes accessed | tf_op | source)
XLA Modules:
  0.0 1628.6 jit_solution(11734710712734050515)
XLA Ops:
  19.5 41.6 %all-reduce.25 = (bf16[768]{0:T(1024)(128)(2,1)S(1)}, bf16[768]{0:T(1024)(128)(2,1)}, bf16[768]{0:T(1024)(128)(2,1)}) all-reduce(bf16[768]{0:T(1024)(128)(2,1)S(1)} %dynamic-update-slice.9, bf16[768]{0:T(1024)(128)(2,1)S(1)} %dynamic-update-slice.10, ...), channel_id=1, replica_groups=mesh['section'=2,'dp'=16] {'section','dp'}, use_global_device_ids=true, to_apply=%add.16 | all-reduce | flops 2304 | bytes 9216
  61.9 71.6 %all_gather.37 = bf16[259,768]{0,1:T(8,128)(2,1)S(1)} all-gather(bf16[259,24]{0,1:T(8,128)(2,1)S(1)} %convert_element_type.372), channel_id=1, replica_groups=mesh['section'=2,'dp'=16] {'section','dp'}, dimensions={1}, use_global_device_ids=true | all-gather | bytes 410256 | tf_op jit(solution)/shard_map/all_gather | solution.py:302
  133.6 64.1 %all-gather = bf16[32,24,16]{1,2,0:T(8,128)(2,1)S(1)} all-gather(bf16[1,24,16]{1,2,0:T(8,128)(2,1)S(1)} %convert_bitcast_fusion.2), channel_id=1, replica_groups=mesh['section'=2,'dp'=16] {'section','dp'}, dimensions={0}, use_global_device_ids=true | all-gather | bytes 25344 | tf_op jit(solution)/shard_map/all_gather | solution.py:303
  200.7 10.6 conditional.6
  212.6 10.2 conditional.8
  226.3 29.6 %convert_convert_fusion = bf16[65536,32]{1,0:T(8,128)(2,1)} fusion(s32[65536]{0:T(1024)S(1)} %fusion.209), kind=kLoop, calls=%fused_computation.383 | loop fusion | flops 6291456 | bytes 4456448 | tf_op jit(solution)/shard_map/convert_element_type | solution.py:78
  255.9 29.6 %fusion.207 = f32[65536,12]{0,1:T(8,128)S(1)} fusion(f32[32,12]{0,1:T(8,128)S(1)} %copy-done, s32[65536]{0:T(1024)S(1)} %fusion.209), kind=kOutput, calls=%fused_computation.385 | convolution fusion | flops 304087040 | bytes 3409408 | tf_op jit(solution)/shard_map/dot_general | solution.py:75
  286.8 2.1 slice.196
  289.5 10.6 all-gather.19.cloned.1.call-done
  300.1 61.2 %all-gather.21.cloned.1.call-done = bf16[768,2048]{1,0:T(8,128)(2,1)} async-done(((bf16[24,2048]{1,0:T(8,128)(2,1)}), bf16[768,2048]{1,0:T(8,128)(2,1)}) %all-gather.21.cloned.1.call-update) | async-done | bytes 3145744 | tf_op jit(solution)/shard_map/all_gather | solution.py:311
  361.3 61.4 %all-gather.9.cloned.1.call-done = bf16[2048,768]{1,0:T(8,128)(2,1)} async-done(((bf16[64,768]{1,0:T(8,128)(2,1)}), bf16[2048,768]{1,0:T(8,128)(2,1)}) %all-gather.9.cloned.1.call-update) | async-done | bytes 3145744 | tf_op jit(solution)/shard_map/all_gather | solution.py:313
  422.6 82.2 %conditional.7 = (bf16[1,256,768]{2,1,0:T(8,128)(2,1)}, bf16[1,256,768]{2,1,0:T(8,128)(2,1)S(1)}, f32[768]{0:T(1024)}, f32[768,768]{1,0:T(8,128)}, f32[768,768]{...) conditional(s32[]{:T(128)} %convert_element_type.370, ...), branch_computations={%region_7.19_spmd, %region_17.20_spmd} | conditional | flops 11668754432 | bytes 269540512 | solution.py:360
  423.4 1.8 convolution_convert_fusion.4
  428.9 3.5 copy.215
  432.5 2.9 fusion.215
  438.4 1.9 copy.185
  440.3 1.8 fusion.19
  448.2 3.5 multiply_convert_fusion
  451.8 3.7 fusion.226
  455.4 3.7 fusion.227
  460.1 1.8 multiply_reduce_fusion.1
  462.2 1.9 fusion.49
  465.4 1.9 copy.189
  468.6 4.3 select_convert_fusion
  473.0 2.6 copy.193
  478.4 7.3 convolution_bitcast_fusion
  486.4 2.1 fusion.54
  496.5 2.0 fusion.56
  498.6 2.1 fusion.58
  500.6 3.8 fusion.41
  504.9 2.1 collective-permute-start.4
  506.9 91.6 %conditional.9 = (bf16[1,256,768]{2,1,0:T(8,128)(2,1)}, bf16[1,256,768]{2,1,0:T(8,128)(2,1)S(1)}, f32[768]{0:T(1024)}, f32[768,768]{1,0:T(8,128)S(1)}, f32[768,7...) conditional(s32[]{:T(128)} %convert_element_type.370, ...), branch_computations={%region_25.37_spmd, %region_35.38_spmd} | conditional | flops 11675833344 | bytes 331094080 | solution.py:360
  509.4 1.9 convolution_convert_fusion.10
  514.8 3.6 copy.218
  518.4 2.7 fusion.216
  525.0 2.7 fusion.82
  527.8 1.7 multiply_reduce_fusion.7
  533.8 3.5 multiply_convert_fusion.3
  537.3 6.4 convolution_add_fusion.6
  543.7 6.5 convolution_add_fusion.7
  551.2 1.8 multiply_reduce_fusion.5
  555.0 1.9 convolution_add_fusion.8
  558.2 4.7 select_convert_fusion.1
  567.3 7.4 fusion.87
  575.4 2.5 convolution_add_fusion.9
  583.7 1.8 fusion.95
  585.4 2.0 fusion.103
  587.5 2.4 convolution_add_fusion.10
  591.2 2.5 convolution_add_fusion.11
  593.7 3.9 convolution_add_fusion.5
  598.6 2.6 collective-permute-start.5
  603.6 8.6 conditional.10
  612.8 9.6 conditional.11
  622.4 2.5 copy.221
  630.0 128.7 %collective-permute-start.3 = (bf16[1,256,384]{2,1,0:T(8,128)(2,1)S(1)}, bf16[1,256,384]{2,1,0:T(8,128)(2,1)S(1)}, u32[]{:S(2)}, u32[]{:S(2)}) collective-permute-start(bf16[1,256,384]{2,1,0:T(8,128)(2,1)S(1)} %slice.148), channel_id=1, source_target_pairs={{16,0},{17,1},{18,2},{19,3},{20,4},{21,5},{22,6},{23,7},{24,8},{25... | collective-permute-start | bytes 589832 | tf_op jit(solution)/shard_map/ppermute | solution.py:21
  761.9 38.1 %all-reduce.24 = (f32[16,768]{1,0:T(8,128)S(1)}, f32[768]{0:T(1024)S(1)}, f32[768]{0:T(1024)S(1)}, f32[768]{0:T(1024)S(1)}, f32[32,12]{0,1:T(8,128)}) all-reduce(f32[16,768]{1,0:T(8,128)} %get-tuple-element.479, f32[768]{0:T(1024)S(1)} %copy-done.120, ...), channel_id=3, replica_groups=mesh['section'=2,'dp'=16] {'section','dp'}, use_global_device_ids=true, to_apply=%region_79.84.clone | all-reduce | flops 14976 | bytes 119808
  802.5 42.1 %reduce-scatter.26.cloned.1.call-done = f32[259,24]{0,1:T(8,128)} async-done(((f32[259,768]{0,1:T(8,128)}), f32[259,24]{0,1:T(8,128)}) %reduce-scatter.26.cloned.1.call-update) | async-done | bytes 24880
  844.6 104.1 %reduce-scatter.12.cloned.1.call-done = f32[24,768]{1,0:T(8,128)} async-done(((f32[768,768]{1,0:T(8,128)}), f32[24,768]{1,0:T(8,128)}) %reduce-scatter.12.cloned.1.call-update) | async-done | bytes 73744 | tf_op jit(solution)/shard_map/reduce_scatter | solution.py:386
  948.7 104.7 %reduce-scatter.14.cloned.1.call-done = f32[24,768]{1,0:T(8,128)} async-done(((f32[768,768]{1,0:T(8,128)}), f32[24,768]{1,0:T(8,128)}) %reduce-scatter.14.cloned.1.call-update) | async-done | bytes 73744 | tf_op jit(solution)/shard_map/reduce_scatter | solution.py:387
  1053.4 103.9 %reduce-scatter.16.cloned.1.call-done = f32[24,768]{1,0:T(8,128)} async-done(((f32[768,768]{1,0:T(8,128)}), f32[24,768]{1,0:T(8,128)}) %reduce-scatter.16.cloned.1.call-update) | async-done | bytes 73744 | tf_op jit(solution)/shard_map/reduce_scatter | solution.py:388
  1157.4 104.6 %reduce-scatter.18.cloned.1.call-done = f32[24,768]{1,0:T(8,128)} async-done(((f32[768,768]{1,0:T(8,128)}), f32[24,768]{1,0:T(8,128)}) %reduce-scatter.18.cloned.1.call-update) | async-done | bytes 73744 | tf_op jit(solution)/shard_map/reduce_scatter | solution.py:389
  1262.0 119.6 %reduce-scatter.20.cloned.1.call-done = f32[24,2048]{1,0:T(8,128)} async-done(((f32[768,2048]{1,0:T(8,128)}), f32[24,2048]{1,0:T(8,128)}) %reduce-scatter.20.cloned.1.call-update) | async-done | bytes 196624 | tf_op jit(solution)/shard_map/reduce_scatter | solution.py:391
  1381.6 120.5 %reduce-scatter.22.cloned.1.call-done = f32[24,2048]{1,0:T(8,128)} async-done(((f32[768,2048]{1,0:T(8,128)}), f32[24,2048]{1,0:T(8,128)}) %reduce-scatter.22.cloned.1.call-update) | async-done | bytes 196624 | tf_op jit(solution)/shard_map/reduce_scatter | solution.py:392
  1502.1 119.5 %reduce-scatter.24.cloned.1.call-done = f32[64,768]{1,0:T(8,128)} async-done(((f32[2048,768]{1,0:T(8,128)}), f32[64,768]{1,0:T(8,128)}) %reduce-scatter.24.cloned.1.call-update) | async-done | bytes 196624 | tf_op jit(solution)/shard_map/reduce_scatter | solution.py:393
  (334 shorter events, 98.9 us)
Async XLA Ops:
  7.2 248.8 %copy-start = (f32[32,12]{0,1:T(8,128)S(1)}, f32[32,12]{0,1:T(8,128)}, u32[]{:S(2)}) copy-start(f32[32,12]{0,1:T(8,128)} %param.56) | copy-start | bytes 4612
  7.2 282.3 %all-gather.11.cloned.1.call-start = ((), (), s32[]{:S(2)}) async-start(), calls=%async_computation.9 | async-start | bytes 1216512 | tf_op jit(solution)/shard_map/all_gather | solution.py:308
  8.8 280.7 %all-gather.13.cloned.1.call-start = ((), (), s32[]{:S(2)}) async-start(), calls=%async_computation.10 | async-start | bytes 1216512 | tf_op jit(solution)/shard_map/all_gather | solution.py:306
  10.4 279.1 %all-gather.15.cloned.1.call-start = ((), (), s32[]{:S(2)}) async-start(), calls=%async_computation.11 | async-start | bytes 1216512 | tf_op jit(solution)/shard_map/all_gather | solution.py:307
  11.9 277.6 %all-gather.17.cloned.1.call-start = ((), (), s32[]{:S(2)}) async-start(), calls=%async_computation.12 | async-start | bytes 1216512 | tf_op jit(solution)/shard_map/all_gather | solution.py:309
  13.5 120.1 %copy-start.161 = (f32[16,24]{1,0:T(8,128)S(1)}, f32[16,24]{1,0:T(8,128)}, u32[]{:S(2)}) copy-start(f32[16,24]{1,0:T(8,128)} %param.45) | copy-start | bytes 4612
  13.5 286.6 %all-gather.19.cloned.1.call-start = ((), (), s32[]{:S(2)}) async-start(), calls=%async_computation.13 | async-start | bytes 3244032 | tf_op jit(solution)/shard_map/all_gather | solution.py:312
  15.2 346.1 %all-gather.21.cloned.1.call-start = ((), (), s32[]{:S(2)}) async-start(), calls=%async_computation.14 | async-start | bytes 3244032 | tf_op jit(solution)/shard_map/all_gather | solution.py:311
  16.8 405.8 %all-gather.9.cloned.1.call-start = ((), (), s32[]{:S(2)}) async-start(), calls=%async_computation.8 | async-start | bytes 3244032 | tf_op jit(solution)/shard_map/all_gather | solution.py:313
  61.1 151.5 %copy-start.74 = (f32[768]{0:T(1024)}, f32[768]{0:T(1024)S(1)}, u32[]{:S(2)}) copy-start(f32[768]{0:T(1024)S(1)} %convert_element_type.377) | copy-start | bytes 9220
  61.9 137.0 %copy-start.178 = (s32[2,1]{0,1:T(1,128)S(1)}, s32[2,1]{0,1:T(1,128)}, u32[]{:S(2)}) copy-start(s32[2,1]{0,1:T(1,128)} %param.42) | copy-start | bytes 28
  61.9 137.5 %copy-start.179 = (s32[2,1]{0,1:T(1,128)S(1)}, s32[2,1]{0,1:T(1,128)}, u32[]{:S(2)}) copy-start(s32[2,1]{0,1:T(1,128)} %param.43) | copy-start | bytes 28
  61.9 138.2 %copy-start.173 = (s32[2,1,512]{2,1,0:T(1,128)S(1)}, s32[2,1,512]{2,1,0:T(1,128)}, u32[]{:S(2)}) copy-start(s32[2,1,512]{2,1,0:T(1,128)} %param.41) | copy-start | bytes 12292
  133.6 79.0 %copy-start.2 = (f32[259,768]{0,1:T(8,128)}, f32[259,768]{0,1:T(8,128)S(1)}, u32[]{:S(2)}) copy-start(f32[259,768]{0,1:T(8,128)S(1)} %convert_element_type.373) | copy-start | bytes 2386948
  211.3 78.2 %collective-permute-start = (bf16[1,256,768]{2,1,0:T(8,128)(2,1)}, bf16[1,256,768]{2,1,0:T(8,128)(2,1)S(1)}, u32[]{:S(2)}, u32[]{:S(2)}) collective-permute-start(bf16[1,256,768]{2,1,0:T(8,128)(2,1)} %get-tuple-element.1035), channel_id=1, source_target_pairs={{0,16},{1,17},{2,18},{3,19},{4,20},{5,21},{6,22},{7,23},{8,24},{9,... | collective-permute-start | bytes 1179656 | tf_op jit(solution)/shard_map/ppermute | solution.py:21
  222.8 284.1 %collective-permute-start.2 = (bf16[1,256,768]{2,1,0:T(8,128)(2,1)}, bf16[1,256,768]{2,1,0:T(8,128)(2,1)}, u32[]{:S(2)}, u32[]{:S(2)}) collective-permute-start(bf16[1,256,768]{2,1,0:T(8,128)(2,1)} %get-tuple-element.1036), channel_id=1, source_target_pairs={{0,16},{1,17},{2,18},{3,19},{4,20},{5,21},{6,22},{7,23},{8,24},{9,... | collective-permute-start | bytes 1179656 | tf_op jit(solution)/shard_map/ppermute | solution.py:21
  225.7 618.9 %reduce-scatter.26.cloned.1.call-start = ((), (), s32[]{:S(2)}) async-start(), calls=%async_computation.22 | async-start | bytes 1216512
  286.8 135.9 %copy-start.155 = (bf16[768]{0:T(1024)(128)(2,1)S(1)}, bf16[768]{0:T(1024)(128)(2,1)}, u32[]{:S(2)}) copy-start(bf16[768]{0:T(1024)(128)(2,1)} %get-tuple-element.895) | copy-start | bytes 4612
  286.8 135.8 %copy-start.156 = (bf16[768]{0:T(1024)(128)(2,1)S(1)}, bf16[768]{0:T(1024)(128)(2,1)}, u32[]{:S(2)}) copy-start(bf16[768]{0:T(1024)(128)(2,1)} %get-tuple-element.896) | copy-start | bytes 4612
  422.8 3.3 copy-start.56
  423.4 13.7 copy-start.108
  442.7 19.3 %copy-start.24 = (f32[256,768]{1,0:T(8,128)}, f32[256,768]{1,0:T(8,128)S(1)}, u32[]{:S(2)}) copy-start(f32[256,768]{1,0:T(8,128)S(1)} %get-tuple-element.915) | copy-start | bytes 2359300 | tf_op jit(solution)/shard_map/cond
  478.3 7.3 copy-start.71
  478.3 7.3 copy-start.94
  485.7 2.7 copy-start.31
  504.9 96.4 %collective-permute-start.4 = (bf16[1,256,768]{2,1,0:T(8,128)(2,1)}, bf16[1,256,768]{2,1,0:T(8,128)(2,1)}, u32[]{:S(2)}, u32[]{:S(2)}) collective-permute-start(bf16[1,256,768]{2,1,0:T(8,128)(2,1)} %get-tuple-element.473), channel_id=1, source_target_pairs={{16,0},{17,1},{18,2},{19,3},{20,4},{21,5},{22,6},{23,7},{24,8},{25... | collective-permute-start | bytes 1179656 | tf_op jit(solution)/shard_map/ppermute | solution.py:21
  506.9 94.3 %copy-start.3 = (f32[259,768]{0,1:T(8,128)S(1)}, f32[259,768]{0,1:T(8,128)}, u32[]{:S(2)}) copy-start(f32[259,768]{0,1:T(8,128)} %copy-done.2) | copy-start | bytes 2386948
  506.9 94.3 %copy-start.75 = (f32[768]{0:T(1024)S(1)}, f32[768]{0:T(1024)}, u32[]{:S(2)}) copy-start(f32[768]{0:T(1024)} %copy-done.74) | copy-start | bytes 9220
  508.2 3.3 copy-start.58
  508.8 14.5 copy-start.121
  511.5 6.8 copy-start.62
  513.4 5.0 copy-start.65
  514.8 3.6 copy-start.177
  521.1 3.9 copy-start.83
  523.3 4.5 copy-start.91
  525.0 2.8 copy-start.76
  525.0 2.8 copy-start.10
  529.5 23.5 %copy-start.22 = (f32[256,768]{1,0:T(8,128)}, f32[256,768]{1,0:T(8,128)S(1)}, u32[]{:S(2)}) copy-start(f32[256,768]{1,0:T(8,128)S(1)} %get-tuple-element.924) | copy-start | bytes 2359300 | tf_op jit(solution)/shard_map/cond
  553.3 3.6 copy-start.34
  567.2 7.4 copy-start.5
  567.3 7.4 copy-start.93
  575.4 3.0 copy-start.33
  575.4 3.2 copy-start.73
  593.7 3.9 copy-start.114
  593.7 3.9 copy-start.132
  598.6 2.8 copy-start.6
  598.6 3.4 copy-start.36
  598.6 4.2 copy-start.37
  598.6 4.9 copy-start.38
  598.6 5.0 copy-start.78
  598.6 13.6 collective-permute-start.5
  625.0 323.7 %reduce-scatter.12.cloned.1.call-start = ((), (), s32[]{:S(2)}) async-start(), calls=%async_computation.15 | async-start | bytes 2433024 | tf_op jit(solution)/shard_map/reduce_scatter | solution.py:386
  625.7 427.7 %reduce-scatter.14.cloned.1.call-start = ((), (), s32[]{:S(2)}) async-start(), calls=%async_computation.16 | async-start | bytes 2433024 | tf_op jit(solution)/shard_map/reduce_scatter | solution.py:387
  626.3 531.0 %reduce-scatter.16.cloned.1.call-start = ((), (), s32[]{:S(2)}) async-start(), calls=%async_computation.17 | async-start | bytes 2433024 | tf_op jit(solution)/shard_map/reduce_scatter | solution.py:388
  627.0 634.9 %reduce-scatter.18.cloned.1.call-start = ((), (), s32[]{:S(2)}) async-start(), calls=%async_computation.18 | async-start | bytes 2433024 | tf_op jit(solution)/shard_map/reduce_scatter | solution.py:389
  627.6 753.9 %reduce-scatter.20.cloned.1.call-start = ((), (), s32[]{:S(2)}) async-start(), calls=%async_computation.19 | async-start | bytes 6488064 | tf_op jit(solution)/shard_map/reduce_scatter | solution.py:391
  628.4 873.7 %reduce-scatter.22.cloned.1.call-start = ((), (), s32[]{:S(2)}) async-start(), calls=%async_computation.20 | async-start | bytes 6488064 | tf_op jit(solution)/shard_map/reduce_scatter | solution.py:392
  628.9 992.7 %reduce-scatter.24.cloned.1.call-start = ((), (), s32[]{:S(2)}) async-start(), calls=%async_computation.21 | async-start | bytes 6488064 | tf_op jit(solution)/shard_map/reduce_scatter | solution.py:393
  629.0 129.7 %copy-start.81 = (bf16[1,256,768]{2,1,0:T(8,128)(2,1)S(1)}, bf16[1,256,768]{2,1,0:T(8,128)(2,1)}, u32[]{:S(2)}) copy-start(bf16[1,256,768]{2,1,0:T(8,128)(2,1)} %copy-done.80) | copy-start | bytes 1179652
  629.5 132.4 %copy-start.116 = (f32[768]{0:T(1024)S(1)}, f32[768]{0:T(1024)}, u32[]{:S(2)}) copy-start(f32[768]{0:T(1024)} %get-tuple-element.486) | copy-start | bytes 9220
  629.5 132.4 %copy-start.120 = (f32[768]{0:T(1024)S(1)}, f32[768]{0:T(1024)}, u32[]{:S(2)}) copy-start(f32[768]{0:T(1024)} %get-tuple-element.480) | copy-start | bytes 9220
  629.6 992.1 %copy-start.1 = (f32[32,12]{0,1:T(8,128)S(1)}, f32[32,12]{0,1:T(8,128)}, u32[]{:S(2)}) copy-start(f32[32,12]{0,1:T(8,128)} %param.56) | copy-start | bytes 4612
  630.0 130.1 %collective-permute-start.3 = (bf16[1,256,384]{2,1,0:T(8,128)(2,1)S(1)}, bf16[1,256,384]{2,1,0:T(8,128)(2,1)S(1)}, u32[]{:S(2)}, u32[]{:S(2)}) collective-permute-start(bf16[1,256,384]{2,1,0:T(8,128)(2,1)S(1)} %slice.148), channel_id=1, source_target_pairs={{16,0},{17,1},{18,2},{19,3},{20,4},{21,5},{22,6},{23,7},{24,8},{25... | collective-permute-start | bytes 589832 | tf_op jit(solution)/shard_map/ppermute | solution.py:21
  758.8 2.4 collective-permute-start.1
  (47 other events, 70.6 us)
Sparse Core Ops, SparseCore 0:
  11.5 56.7 all-gather.10
  71.8 53.5 all-gather.12
  128.8 53.2 all-gather.14
  185.5 53.1 all-gather.16
  242.0 58.0 all-gather.18
  303.4 57.8 all-gather.20
  364.7 57.8 all-gather.8
  625.1 219.4 reduce-scatter.25
  850.5 98.1 reduce-scatter.11
  955.3 98.1 reduce-scatter.13
  1059.3 98.0 reduce-scatter.15
  1163.9 97.9 reduce-scatter.17
  1268.2 113.3 reduce-scatter.19
  1388.6 113.4 reduce-scatter.21
  1508.1 113.4 reduce-scatter.23
where the time goes:
time: 1640 us; the launch traced here: 1630 us
  waiting for transfers between devices  958 us (58%)
  blocking collectives  215 us (13%)
  matrix products  148 us (9%)
  starting transfers between devices  138 us (8%)
  local copies, waits for them, and re-layouts  58.6 us (4%)
  other arithmetic  58.3 us (4%)
  loops' own time  37.6 us (2%)
    ppermute x6, starting transfers between devices, from_behind(): return lax.ppermute(block, axis, route)  137 us
    reduce_scatter x1, waiting for transfers between devices, body(): lax.psum_scatter(grads[10], ('section', 'dp'), scatter_dimension=0, tiled...  121 us
    reduce_scatter x1, waiting for transfers between devices, body(): lax.psum_scatter(grads[9], ('section', 'dp'), scatter_dimension=0, tiled=...  120 us
    reduce_scatter x1, waiting for transfers between devices, body(): lax.psum_scatter(grads[11], ('section', 'dp'), scatter_dimension=0, tiled...  120 us
    reduce_scatter x1, waiting for transfers between devices, body(): lax.psum_scatter(grads[5], ('section', 'dp'), scatter_dimension=0, tiled=...  105 us
    reduce_scatter x1, waiting for transfers between devices, body(): lax.psum_scatter(grads[7], ('section', 'dp'), scatter_dimension=0, tiled=...  105 us
    reduce_scatter x1, waiting for transfers between devices, body(): lax.psum_scatter(grads[4], ('section', 'dp'), scatter_dimension=0, tiled=...  104 us
    reduce_scatter x1, waiting for transfers between devices, body(): lax.psum_scatter(grads[6], ('section', 'dp'), scatter_dimension=0, tiled=...  104 us
  transfers between devices with their start and end apart: 21, of which 12 were waited for; matrix products, arithmetic and copies ran while one was open for 15% of the time, Pallas kernels for 0%

commit v1 on v0

v1 whole, which is shorter than its diff:
```python
import functools

import jax
import jax.numpy as jnp
from jax import lax
from jax.experimental import pallas as pl
from jax.experimental.pallas import tpu as pltpu
from jax.sharding import PartitionSpec as P

BLOCKS = 4
DOWN = 2
MICRO = 2
OUTER = 16
EPSILON = 1e-06
NEGATIVE = -1000000000.0
LIMITS = (12, 16, 23, 32, 46, 64, 91)
MESH = pl.DeviceIdType.MESH
BF = jnp.bfloat16
F32 = jnp.float32
I32 = jnp.int32

ELT, QKV, WO, GATE, UP, DOWNW = range(6)
ALL = (ELT, QKV, WO, GATE, UP, DOWNW)
VOC = 288
SCORER = 19


def dot(a, b):
    return lax.dot_general(a, b, (((1,), (0,)), ((), ())), preferred_element_type=F32)


def dot_nt(a, b):
    return lax.dot_general(a, b, (((1,), (1,)), ((), ())), preferred_element_type=F32)


def dot_tn(a, b):
    return lax.dot_general(a, b, (((0,), (0,)), ((), ())), preferred_element_type=F32)


def split3(x):
    hi = x.astype(BF)
    rest = x - hi.astype(F32)
    mid = rest.astype(BF)
    return hi, mid, (rest - mid.astype(F32)).astype(BF)


def iota(shape, axis):
    return lax.broadcasted_iota(I32, shape, axis)


def bucket_ids(offsets):
    distance = jnp.abs(offsets)
    larger = 8 + sum(((distance >= limit).astype(I32) for limit in LIMITS))
    inside = jnp.where(distance < 8, distance, larger)
    return jnp.where(offsets > 0, 16, 0).astype(I32) + inside


class Net:
    def __init__(self, inner, w, g, sb, x1, y1, zi, ch, tmp, fo, sems):
        self.w, self.g, self.sb, self.x1, self.y1 = w, g, sb, x1, y1
        self.zi, self.ch, self.tmp, self.fo = zi, ch, tmp, fo
        self.ag_s, self.ag_r, self.rs_s, self.rs_r, self.mi_s, self.mi_r = sems
        self.s = lax.axis_index("section")
        self.d = lax.axis_index("dp")
        outer = self.d // inner
        self.z = outer // 4
        self.yx = outer % 4
        y, x = self.yx // 2, self.yx % 2
        self.sib = (1 - self.s, self.d)
        self.yx_x = self.yx + 1 - 2 * x
        self.yx_y = self.yx + 2 - 4 * y
        self.yx_d = 3 - self.yx
        self.xn = (self.s, self.d + (1 - 2 * x) * inner)
        self.yn = (self.s, self.d + (1 - 2 * y) * 2 * inner)
        self.zz = [(self.z + k) % 4 for k in (1, 2, 3)]
        self.zn = [(self.s, self.d + (zz - self.z) * 4 * inner) for zz in self.zz]
        self.sent = []

    def barrier(self):
        barrier = pltpu.get_barrier_semaphore()
        for device in (self.sib, self.xn, self.yn, *self.zn):
            pl.semaphore_signal(barrier, inc=1, device_id=device, device_id_type=MESH)
        pl.semaphore_wait(barrier, 6)

    def copy(self, src, dst, send, recv, device):
        return pltpu.make_async_remote_copy(
            src_ref=src, dst_ref=dst, send_sem=send, recv_sem=recv,
            device_id=device, device_id_type=MESH,
        )

    def start(self, copy):
        copy.start()
        self.sent.append(copy)

    def finish(self):
        for copy in self.sent:
            copy.wait_send()
        self.sent = []

    def blk(self, ref, m, h, z, yx):
        return ref.at[h, :, z, yx] if m == DOWNW else ref.at[h, z, yx]

    def grp(self, ref, m, h, yx):
        return ref.at[h, :, :, yx] if m == DOWNW else ref.at[h, :, yx]

    def part(self, ref, m, h, z0, yx):
        return ref.at[h, :, pl.ds(z0, 2), yx] if m == DOWNW else ref.at[h, pl.ds(z0, 2), yx]

    def xy2(self, m):
        if m == DOWNW:
            return self.sb[m].at[0, pl.ds(0, 2)], self.sb[m].at[0, pl.ds(2, 2)]
        return self.sb[m].at[0], self.sb[m].at[1]

    def ag(self, m, slot):
        w, s = self.w[m], self.s
        pair = lambda src, dst, dev: self.copy(src, dst, self.ag_s.at[m, slot], self.ag_r.at[m, slot], dev)
        if slot == 0:
            if m == DOWNW:
                dst = self.ch[m].at[s]
            else:
                rows = self.tmp[m].shape[0]
                dst = self.ch[m].at[pl.ds(s * rows, rows)]
            return pair(self.tmp[m], dst, self.sib)
        if slot <= 3:
            ref = self.blk(w, m, s, self.z, self.yx)
            return pair(ref, ref, self.zn[slot - 1])
        if slot <= 5:
            ref = self.grp(w, m, s, self.yx)
            return pair(ref, ref, self.xn if slot == 4 else self.yn)
        if slot == 6:
            ref = self.part(w, m, s, 0, self.yx_x)
            return pair(ref, ref, self.yn)
        if slot == 7:
            ref = self.part(w, m, s, 2, self.yx_y)
            return pair(ref, ref, self.xn)
        ref = self.grp(w, m, s, (self.yx, self.yx_x, self.yx_y, self.yx_d)[slot - 8])
        return pair(ref, ref, self.sib)

    def ag0(self, m):
        self.start(self.ag(m, 0))

    def ag1(self, m):
        self.ag(m, 0).wait_recv()
        chunk = self.ch[m][...].astype(BF)
        if m == DOWNW:
            for sec in (0, 1):
                self.w[m][self.s, sec, self.z, self.yx] = chunk[sec]
        else:
            self.w[m][self.s, self.z, self.yx] = chunk
        for slot in (1, 2, 3):
            self.start(self.ag(m, slot))

    def ag2(self, m):
        for slot in (1, 2, 3):
            self.ag(m, slot).wait_recv()
        for slot in (4, 5, 8):
            self.start(self.ag(m, slot))

    def ag3(self, m):
        self.ag(m, 4).wait_recv()
        for slot in (6, 9):
            self.start(self.ag(m, slot))
        self.ag(m, 5).wait_recv()
        for slot in (7, 10):
            self.start(self.ag(m, slot))

    def ag4(self, m):
        for slot in (6, 7):
            self.ag(m, slot).wait_recv()
        self.start(self.ag(m, 11))

    def ag5(self, m):
        for slot in (8, 9, 10, 11):
            self.ag(m, slot).wait_recv()

    def rs(self, m, slot):
        g, s = self.g[m], self.s
        pair = lambda src, dst, dev: self.copy(src, dst, self.rs_s.at[m, slot], self.rs_r.at[m, slot], dev)
        if slot == 0:
            return pair(g.at[1 - s], self.sb[m], self.sib)
        if slot == 1:
            return pair(self.part(g, m, s, 0, self.yx_d), self.x1[m], self.xn)
        if slot == 2:
            return pair(self.part(g, m, s, 2, self.yx_d), self.y1[m], self.yn)
        if slot == 3:
            return pair(self.grp(g, m, s, self.yx_x), self.xy2(m)[0], self.xn)
        if slot == 4:
            return pair(self.grp(g, m, s, self.yx_y), self.xy2(m)[1], self.yn)
        if slot <= 7:
            k = slot - 5
            return pair(self.blk(g, m, s, self.zz[k], self.yx), self.zi[m].at[k], self.zn[k])
        if m == DOWNW:
            src = self.ch[m].at[1 - s]
        else:
            rows = self.fo[m].shape[0]
            src = self.ch[m].at[pl.ds((1 - s) * rows, rows)]
        return pair(src, self.fo[m], self.sib)

    def rs0(self, m):
        self.start(self.rs(m, 0))

    def rs1(self, m):
        self.rs(m, 0).wait_recv()
        g, sb, s = self.g[m], self.sb[m], self.s

        def add(i, carry):
            if m == DOWNW:
                at = (i // 4, i % 4)
                g[s, at[0], at[1]] = (g[s, at[0], at[1]].astype(F32) + sb[at[0], at[1]].astype(F32)).astype(BF)
            else:
                g[s, i // 4, i % 4] = (g[s, i // 4, i % 4].astype(F32) + sb[i // 4, i % 4].astype(F32)).astype(BF)
            return carry

        lax.fori_loop(0, 8 if m == DOWNW else 16, add, 0)
        self.start(self.rs(m, 1))
        self.start(self.rs(m, 2))

    def rs2(self, m):
        g, s = self.g[m], self.s
        for slot, ref, z0, yx in ((1, self.x1[m], 0, self.yx_y), (2, self.y1[m], 2, self.yx_x)):
            self.rs(m, slot).wait_recv()
            for j in (0, 1):
                if m == DOWNW:
                    for sec in (0, 1):
                        mine = g[s, sec, z0 + j, yx].astype(F32)
                        g[s, sec, z0 + j, yx] = (mine + ref[sec, j].astype(F32)).astype(BF)
                else:
                    mine = g[s, z0 + j, yx].astype(F32)
                    g[s, z0 + j, yx] = (mine + ref[j].astype(F32)).astype(BF)
        self.start(self.rs(m, 3))
        self.start(self.rs(m, 4))

    def rs3(self, m):
        self.rs(m, 3).wait_recv()
        self.rs(m, 4).wait_recv()
        g, s, yx = self.g[m], self.s, self.yx
        a, b = self.xy2(m)

        def total(sec, z):
            if m == DOWNW:
                return g[s, sec, z, yx].astype(F32) + a[sec, z].astype(F32) + b[sec, z].astype(F32)
            return g[s, z, yx].astype(F32) + a[z].astype(F32) + b[z].astype(F32)

        for slot in (5, 6, 7):
            zz = self.zz[slot - 5]
            if m == DOWNW:
                for sec in (0, 1):
                    g[s, sec, zz, yx] = total(sec, zz).astype(BF)
            else:
                g[s, zz, yx] = total(0, zz).astype(BF)
            self.start(self.rs(m, slot))
        if m == DOWNW:
            for sec in (0, 1):
                self.ch[m][sec] = total(sec, self.z)
        else:
            self.ch[m][...] = total(0, self.z)

    def rs4(self, m):
        for slot in (5, 6, 7):
            self.rs(m, slot).wait_recv()
        zi = self.zi[m]
        self.ch[m][...] += zi[0].astype(F32) + zi[1].astype(F32) + zi[2].astype(F32)
        self.start(self.rs(m, 8))

    def rs5(self, m):
        if m == DOWNW:
            mine = self.ch[m][self.s]
        else:
            rows = self.fo[m].shape[0]
            mine = self.ch[m][pl.ds(self.s * rows, rows)]
        self.rs(m, 8).wait_recv()
        return mine, self.fo[m][...]


def kernel(inner, sizes, *refs):
    (ints, rel, elt, wq, wk, wv, wo, wi0, wi1, wd, cot) = refs[:11]
    (enc_out, g_elt, g_q, g_k, g_v, g_o, g_0, g_1, g_d, g_rel) = refs[11:21]
    rest = refs[21:]
    take = lambda k: rest[6 * k : 6 * k + 6]
    w, g, sb, x1, y1, zi, ch, tmp, fo = (take(k) for k in range(9))
    rest = rest[54:]
    sems, rest = rest[:6], rest[6:]
    (pi, cb, prow, gthi, gtlo, rows_ref, hid, nrm, qs, ks, vs, bvec, pmat, mixed, mixp, mid, sec_ref,
     acc, encb, dq, dk, dv, dvec, relbuf, relin, cp) = rest
    tokens, width, half, ffh = sizes
    net = Net(inner, w, g, sb, x1, y1, zi, ch, tmp, fo, sems)
    s = net.s
    net.barrier()

    def lanes(ref, h, n):
        return ref[:, pl.ds(pl.multiple_of(h * n, 128), n)]

    pi[...] = jnp.where(iota((width, width), 0) == ints[3:4, :], 1.0, 0.0).astype(BF)

    wo_p = dot(wo[...].astype(BF), pi[...])
    wd_p = dot(wd[...].astype(BF), pi[...])
    rows_d, rows_f = elt.shape[0], wd.shape[0]
    fo_wo, fo_wd = fo[WO], fo[DOWNW]

    def halves(m, h):
        if m == ELT:
            return lanes(elt, h, 256)
        if m == QKV:
            return jnp.concatenate([lanes(r, h, half) for r in (wq, wk, wv)], axis=1)
        if m == GATE:
            return lanes(wi0, h, ffh)
        if m == UP:
            return lanes(wi1, h, ffh)
        value = wo_p if m == WO else wd_p
        return jnp.where(h == 0, value[:, :half], value[:, half:])

    for m in ALL:
        tmp[m][...] = halves(m, 1 - s)
        net.ag0(m)
        own = halves(m, s)
        if m == DOWNW:
            ch[m][s] = own
        else:
            ch[m][pl.ds(s * rows_d, rows_d)] = own
    for m in ALL:
        net.ag1(m)
    steps = (net.ag2, net.ag3, net.ag4, net.ag5)
    for t in range(len(ALL) + 3):
        for k, step in enumerate(steps):
            if 0 <= t - k < len(ALL):
                step(ALL[t - k])

    def wmat(m, h):
        return w[m][h].reshape(width, w[m].shape[-1])

    def gput(m, h, value):
        g[m][h] = value.astype(BF).reshape(g[m].shape[1:])

    cp[...] = dot(cot[s], pi[...]).astype(BF)

    span = 2 * tokens
    ohb = jnp.where(iota((128, span), 0) == bucket_ids(iota((128, span), 1) - (tokens - 1)), 1.0, 0.0).astype(BF)
    bv = sum(dot(part, ohb) for part in split3(rel[...]))
    heads = bvec.shape[0]
    for h in range(heads):
        bvec[h] = bv[h : h + 1, :]

    count = span
    ids, length, group = ints[0:1, :count], ints[1:2, :count], ints[2:3, :count]
    col = iota((1, count), 1)
    pos = jnp.where(col < tokens, 2 * col, 2 * (col - tokens) + 1)
    valid = pos < length
    symbol = iota((VOC, count), 0)
    onehot = jnp.where(((symbol == ids) | (symbol == group + 259)) & valid, 1.0, 0.0)
    cb[0] = onehot.astype(BF)

    def block_of(p, size):
        return p if size == 1 else p >> 1 if size == 2 else (p * 21846) >> 16 if size == 3 else p >> 2

    rowi = iota((count, 1), 0)
    posc = jnp.where(rowi < tokens, 2 * rowi, 2 * (rowi - tokens) + 1)
    for size in (2, 3, 4):
        pool = jnp.where(block_of(posc, size) == block_of(pos, size), 1.0, 0.0).astype(BF)
        cb[size - 1] = dot(cb[0], pool).astype(BF)

    e0, e1 = wmat(ELT, 0), wmat(ELT, 1)[:, :128]
    picks = jnp.where(iota((8, 128), 1) == iota((8, 128), 0) + SCORER, 1.0, 0.0).astype(BF)
    rows_ref[...] = dot_nt(picks, e1)
    g1, g2 = rows_ref[1:2, :], rows_ref[2:3, :]
    ew = jnp.concatenate([dot_tn(e0, e1), dot_tn(e1, e1)[: VOC - 256]], axis=0)[:, SCORER : SCORER + 1]
    ratings = [jnp.sum(cb[b].astype(F32) * ew, axis=0, keepdims=True) / (b + 1) for b in range(BLOCKS)]
    top = functools.reduce(jnp.maximum, ratings)
    raised = [jnp.exp(r - top) for r in ratings]
    total = sum(raised)
    chosen = [r / total for r in raised]
    mixw = 0.0
    for b in range(BLOCKS):
        prow[b : b + 1, :] = chosen[b]
        mixw = mixw + cb[b].astype(F32) * (chosen[b] / (2.0 * (b + 1)))
    gt = mixw[:, :tokens] + mixw[:, tokens:]
    gt = jnp.concatenate([gt, jnp.zeros((384 - VOC, tokens), F32)], axis=0).T
    gthi[...] = gt.astype(BF)
    gtlo[...] = (gt - gt.astype(BF).astype(F32)).astype(BF)
    latent = (
        dot_nt(gthi[:, :256], e0) + dot_nt(gthi[:, 256:], e1)
        + dot_nt(gtlo[:, :256], e0) + dot_nt(gtlo[:, 256:], e1)
    )
    hid[...] = latent.astype(BF)

    hidden = hid[...].astype(F32)
    r1 = lax.rsqrt(jnp.mean(hidden * hidden, -1, keepdims=True) + EPSILON)
    nrm[...] = (hidden * r1 * g1).astype(BF)
    for h in (0, 1):
        for j, ref in enumerate((qs, ks, vs)):
            out = dot(nrm[...], w[QKV][h, :, :, :, j * half : (j + 1) * half].reshape(width, half)).astype(BF)
            for i in range(half // 128):
                ref[h * (half // 128) + i] = out[:, i * 128 : (i + 1) * 128]

    tcol = iota((1, tokens), 1)
    valid_key = DOWN * tcol < ints[1:2, :tokens]
    lane = iota((1, 128), 1)
    masks = [jnp.where(lane < 64, 1.0 - e, float(e)).astype(BF) for e in (0, 1)]

    def forward_pair(i, carry):
        q2, k2, v2 = qs[i], ks[i], vs[i]
        out = 0.0
        for e in (0, 1):
            h = 2 * i + e
            line = jnp.broadcast_to(bvec[h], (tokens, span))
            bias = pltpu.roll(line, tokens + 1, 1, stride=1, stride_axis=0)[:, :tokens]
            scores = jnp.where(valid_key, dot_nt(q2, k2 * masks[e]) + bias, NEGATIVE)
            up = jnp.exp(scores - jnp.max(scores, -1, keepdims=True))
            prob = up * (1.0 / jnp.sum(up, -1, keepdims=True))
            pmat[h] = prob
            out = out + dot(prob.astype(BF), v2 * masks[e])
        mixed[:, pl.ds(pl.multiple_of(i * 128, 128), 128)] = out.astype(BF)
        return carry

    lax.fori_loop(0, width // 128, forward_pair, 0)
    mixp[...] = dot(mixed[...], pi[...]).astype(BF)
    for h in (0, 1):
        cols = slice(h * half, (h + 1) * half)
        mid[:, cols] = hid[:, cols].astype(F32) + dot(mixp[...], wmat(WO, h))
    middle = mid[...]
    r2 = lax.rsqrt(jnp.mean(middle * middle, -1, keepdims=True) + EPSILON)
    sec_ref[...] = (middle * r2 * g2).astype(BF)

    acc[...] = jnp.zeros_like(acc)
    encb[...] = mid[...]

    def feed(i, carry):
        h = i // 4
        cols = pl.ds(pl.multiple_of((i % 4) * 256, 256), 256)
        wg = w[GATE][h, :, :, :, cols].reshape(width, 256)
        wu = w[UP][h, :, :, :, cols].reshape(width, 256)
        wdn = [w[DOWNW][j, h, i % 4].reshape(256, half) for j in (0, 1)]
        gate, upper = dot(sec_ref[...], wg), dot(sec_ref[...], wu)
        pdelta = dot_nt(cp[:, :half], wdn[0]) + dot_nt(cp[:, half:], wdn[1])
        square = gate * gate
        tanh = jnp.tanh(0.7978845608 * (gate + 0.044715 * square * gate))
        act = 0.5 * gate * (1.0 + tanh)
        slope = 0.5 * (1.0 + tanh) + 0.5 * gate * (1.0 - tanh * tanh) * 0.7978845608 * (1.0 + 0.134145 * square)
        product = (act * upper).astype(BF)
        gdelta = (pdelta * upper * slope).astype(BF)
        udelta = (pdelta * act).astype(BF)
        g[GATE][h, :, :, :, cols] = dot_tn(sec_ref[...], gdelta).astype(BF).reshape(4, 4, -1, 256)
        g[UP][h, :, :, :, cols] = dot_tn(sec_ref[...], udelta).astype(BF).reshape(4, 4, -1, 256)
        for j in (0, 1):
            out = slice(j * half, (j + 1) * half)
            g[DOWNW][j, h, i % 4] = dot_tn(product, cp[:, out]).astype(BF).reshape(4, -1, half)
            encb[:, out] += dot(product, wdn[j])
        acc[...] += dot_nt(gdelta, wg) + dot_nt(udelta, wu)
        return carry

    lax.fori_loop(0, 8, feed, 0)

    encoded = dot_nt(encb[...].astype(BF), pi[...]).astype(BF)
    for h in (0, 1):
        mixed[:, h * half : (h + 1) * half] = encoded[:, h * half : (h + 1) * half]
    enc_out[s] = lanes(mixed, s, half)
    enc_copy = net.copy(
        mixed.at[:, pl.ds(pl.multiple_of((1 - s) * half, 128), half)], enc_out.at[s],
        net.mi_s.at[0], net.mi_r.at[0], net.sib,
    )
    net.start(enc_copy)

    middle = mid[...]
    r2 = lax.rsqrt(jnp.mean(middle * middle, -1, keepdims=True) + EPSILON)
    n2 = middle * r2
    sdelta = acc[...]
    scaled = sdelta * g2
    mid_grad = jnp.sum(sdelta * n2, axis=0, keepdims=True)
    mdel = encb
    mdel[...] = cp[...].astype(F32) + r2 * (scaled - n2 * jnp.mean(scaled * n2, -1, keepdims=True))
    adel = mdel[...].astype(BF)
    sec_ref[...] = adel
    for h in (0, 1):
        gput(WO, h, dot_tn(mixp[...], sec_ref[:, h * half : (h + 1) * half]))
    back = dot_nt(sec_ref[:, :half], wmat(WO, 0)) + dot_nt(sec_ref[:, half:], wmat(WO, 1))
    mixp[...] = dot_nt(back.astype(BF), pi[...]).astype(BF)

    flip = jnp.where(iota((tokens, tokens), 0) + iota((tokens, tokens), 1) == tokens - 1, 1.0, 0.0).astype(BF)

    def backward_pair(i, carry):
        cols = pl.ds(pl.multiple_of(i * 128, 128), 128)
        q2, k2, v2, m2 = qs[i], ks[i], vs[i], mixp[:, cols]
        outq = outk = outv = 0.0
        for e in (0, 1):
            h = 2 * i + e
            prob = pmat[h]
            wdelta = dot_nt(m2, v2 * masks[e])
            lean = jnp.sum(prob * wdelta, -1, keepdims=True)
            sd = jnp.where(valid_key, prob * (wdelta - lean), 0.0).astype(BF)
            outq = outq + dot(sd, k2 * masks[e])
            outk = outk + dot_tn(sd, q2 * masks[e])
            outv = outv + dot_tn(prob.astype(BF), m2 * masks[e])
            turned = jnp.concatenate([dot(sd, flip), jnp.zeros((tokens, tokens), F32)], axis=1)
            skew = pltpu.roll(turned, 0, 1, stride=1, stride_axis=0)
            dvec[h] = jnp.sum(skew, axis=0, keepdims=True)
        dq[:, cols], dk[:, cols], dv[:, cols] = outq.astype(BF), outk.astype(BF), outv.astype(BF)
        return carry

    lax.fori_loop(0, width // 128, backward_pair, 0)

    norm_delta = 0.0
    for h in (0, 1):
        for j, ref in enumerate((dq, dk, dv)):
            part = ref[:, h * half : (h + 1) * half]
            cols = slice(j * half, (j + 1) * half)
            g[QKV][h, :, :, :, cols] = dot_tn(nrm[...], part).astype(BF).reshape(4, 4, -1, half)
            norm_delta = norm_delta + dot_nt(part, w[QKV][h, :, :, :, cols].reshape(width, half))
    hidden = hid[...].astype(F32)
    r1 = lax.rsqrt(jnp.mean(hidden * hidden, -1, keepdims=True) + EPSILON)
    n1 = hidden * r1
    scaled = norm_delta * g1
    pre_grad = jnp.sum(norm_delta * n1, axis=0, keepdims=True)
    hdel = (mdel[...] + r1 * (scaled - n1 * jnp.mean(scaled * n1, -1, keepdims=True))).astype(BF)

    back = jnp.concatenate([dot(hdel, e0), dot(hdel, e1)], axis=1).T[:VOC]
    back = jnp.concatenate([back, back], axis=1)
    pdel = [jnp.sum(cb[b].astype(F32) * back, axis=0, keepdims=True) / (2.0 * (b + 1)) for b in range(BLOCKS)]
    lean = sum(prow[b : b + 1, :] * pdel[b] for b in range(BLOCKS))
    flow = 0.0
    for b in range(BLOCKS):
        flow = flow + cb[b].astype(F32) * (prow[b : b + 1, :] * (pdel[b] - lean) / (b + 1))
    gs = jnp.sum(flow, axis=1, keepdims=True)
    lane_v = iota((VOC, 128), 1)
    parts = [p.astype(F32) for p in split3(gs)]
    gs3 = jnp.where(lane_v == 0, parts[0], jnp.where(lane_v == 1, parts[1], jnp.where(lane_v == 2, parts[2], 0.0)))
    gs3 = gs3.astype(BF)
    lane_w = iota((width, 128), 1)
    wcol = jnp.where(lane_w < 3, e1.astype(F32)[:, SCORER : SCORER + 1], 0.0).astype(BF)
    gput(ELT, 0, dot_tn(hdel, gthi[:, :256]) + dot_tn(hdel, gtlo[:, :256]) + dot_nt(wcol, gs3[:256]))
    gs_tail = jnp.concatenate([gs3[256:], jnp.zeros((128 + 256 - VOC, 128), BF)], axis=0)
    tail = dot_tn(hdel, gthi[:, 256:]) + dot_tn(hdel, gtlo[:, 256:]) + dot_nt(wcol, gs_tail)
    scorer_grad = jnp.sum(dot(e0, gs3[:256]) + dot(e1, gs_tail), axis=1, keepdims=True)
    gains = [p.astype(F32) for p in (*split3(pre_grad), *split3(mid_grad))]
    gains = jnp.concatenate([*gains, jnp.zeros((10, width), F32)], axis=0).astype(BF)
    place_row, place_col = iota((16, 128), 0), iota((16, 128), 1)
    place = (place_row < 6) & (place_col == jnp.where(place_row < 3, SCORER + 1, SCORER + 2))
    tail = tail + dot_tn(gains, jnp.where(place, 1.0, 0.0).astype(BF))
    tail = jnp.where(lane_w == SCORER, scorer_grad, tail)
    gput(ELT, 1, jnp.concatenate([tail, jnp.zeros((width, 128), F32)], axis=1))

    ohr = jnp.where(iota((128, span), 0) == bucket_ids((tokens - 1) - iota((128, span), 1)), 1.0, 0.0).astype(BF)
    lines = jnp.concatenate([dvec[h] for h in range(heads)] + [jnp.zeros((16 - heads, span), F32)], axis=0)
    relbuf[0] = sum(dot_nt(part, ohr) for part in split3(lines))

    def rel_copy(slot, level, device):
        return net.copy(relbuf.at[level], relin.at[slot], net.mi_s.at[1 + slot], net.mi_r.at[1 + slot], device)

    for level, partners in enumerate((((0, net.sib),), ((1, net.xn),), ((2, net.yn),), ((3, net.zn[0]), (4, net.zn[1]), (5, net.zn[2])))):
        for slot, device in partners:
            net.start(rel_copy(slot, level, device))
        for slot, device in partners:
            rel_copy(slot, level, device).wait_recv()
        if level < 3:
            relbuf[level + 1] = relbuf[level] + relin[level]
    place = [jnp.where(net.z == k, 1.0, 0.0) for k in range(4)]
    level = [relbuf[3], relin[3], relin[4], relin[5]]
    summed = 0.0
    for k in range(4):
        summed = summed + sum(place[z] * level[(z - k) % 4] for z in range(4))
    g_rel[...] = summed

    order = (DOWNW, UP, GATE, WO, QKV, ELT)
    for m in order:
        net.rs0(m)
    results = {}

    def last(m):
        results[m] = True
        mine, other = net.rs5(m)
        n = mine.shape[1]
        if m in (WO, DOWNW):
            first = jnp.where(s == 0, mine, other)
            second = jnp.where(s == 0, other, mine)
            both = jnp.concatenate([first, second], axis=1)
            out = g_o if m == WO else g_d
            out[...] = sum(dot_nt(part, pi[...]) for part in split3(both))
            return
        targets = {ELT: (g_elt,), QKV: (g_q, g_k, g_v), GATE: (g_0,), UP: (g_1,)}[m]
        n = n // len(targets)
        for j, ref in enumerate(targets):
            ref[:, pl.ds(pl.multiple_of(s * n, 128), n)] = mine[:, j * n : (j + 1) * n]
            ref[:, pl.ds(pl.multiple_of((1 - s) * n, 128), n)] = other[:, j * n : (j + 1) * n]

    steps = (net.rs1, net.rs2, net.rs3, net.rs4, last)
    for t in range(len(order) + 4):
        for k, step in enumerate(steps):
            if 0 <= t - k < len(order):
                step(order[t - k])
    enc_copy.wait_recv()
    net.finish()


def call(inner, ints, rel, elt, wq, wk, wv, wo, wi0, wi1, wd, cot):
    rows_d, width = wq.shape
    rows_f = wd.shape[0]
    half, ffh = width // 2, wi0.shape[1] // 2
    tokens = cot.shape[1]
    span = 2 * tokens
    heads = width // 64
    wide = {ELT: 256, QKV: 3 * half, WO: half, GATE: ffh, UP: ffh, DOWNW: half}
    chip = {m: (2, rows_f) if m == DOWNW else (2 * rows_d,) for m in ALL}

    def shape(m, lead, sec, tail):
        return (*lead, *((2,) if m == DOWNW and sec else ()), *tail)

    def full(m):
        return (2, 4, 4, rows_f, wide[m]) if m == DOWNW else (4, 4, 2 * rows_d, wide[m])

    def part(m):
        return (2, 2, rows_f, wide[m]) if m == DOWNW else (2, 2 * rows_d, wide[m])

    scratch = []
    scratch += [pltpu.VMEM((2, *full(m)), BF) for m in ALL]
    scratch += [pltpu.VMEM((2, *full(m)), BF) for m in ALL]
    scratch += [pltpu.VMEM(full(m), BF) for m in ALL]
    scratch += [pltpu.VMEM(part(m), BF) for m in ALL]
    scratch += [pltpu.VMEM(part(m), BF) for m in ALL]
    scratch += [pltpu.VMEM((3, *chip[m], wide[m]), BF) for m in ALL]
    scratch += [pltpu.VMEM((*chip[m], wide[m]), F32) for m in ALL]
    scratch += [pltpu.VMEM((chip[m][-1] if m == DOWNW else rows_d, wide[m]), F32) for m in ALL]
    scratch += [pltpu.VMEM((chip[m][-1] if m == DOWNW else rows_d, wide[m]), F32) for m in ALL]
    dma = pltpu.SemaphoreType.DMA
    scratch += [dma((6, 12)), dma((6, 12)), dma((6, 9)), dma((6, 9)), dma((7,)), dma((7,))]
    act = (tokens, width)
    scratch += [
        pltpu.VMEM((width, width), BF),
        pltpu.VMEM((BLOCKS, VOC, span), BF),
        pltpu.VMEM((8, span), F32),
        pltpu.VMEM((tokens, 384), BF),
        pltpu.VMEM((tokens, 384), BF),
        pltpu.VMEM((8, width), F32),
        pltpu.VMEM(act, BF),
        pltpu.VMEM(act, BF),
        pltpu.VMEM((width // 128, tokens, 128), BF),
        pltpu.VMEM((width // 128, tokens, 128), BF),
        pltpu.VMEM((width // 128, tokens, 128), BF),
        pltpu.VMEM((heads, 1, span), F32),
        pltpu.VMEM((heads, tokens, tokens), F32),
        pltpu.VMEM(act, BF),
        pltpu.VMEM(act, BF),
        pltpu.VMEM(act, F32),
        pltpu.VMEM(act, BF),
        pltpu.VMEM(act, F32),
        pltpu.VMEM(act, F32),
        pltpu.VMEM(act, BF),
        pltpu.VMEM(act, BF),
        pltpu.VMEM(act, BF),
        pltpu.VMEM((heads, 1, span), F32),
        pltpu.VMEM((4, 16, 128), F32),
        pltpu.VMEM((6, 16, 128), F32),
        pltpu.VMEM(act, BF),
    ]
    outs = [
        jax.ShapeDtypeStruct((MICRO, tokens, half), BF),
        jax.ShapeDtypeStruct(elt.shape, F32),
        *[jax.ShapeDtypeStruct(item.shape, F32) for item in (wq, wk, wv, wo, wi0, wi1, wd)],
        jax.ShapeDtypeStruct((16, 128), F32),
    ]
    vmem = pl.BlockSpec(memory_space=pltpu.VMEM)
    return pl.pallas_call(
        functools.partial(kernel, inner, (tokens, width, half, ffh)),
        out_shape=outs,
        in_specs=[vmem] * 11,
        out_specs=[vmem] * len(outs),
        scratch_shapes=scratch,
        compiler_params=pltpu.CompilerParams(
            collective_id=0, has_side_effects=True, vmem_limit_bytes=63 * 2**20
        ),
    )(ints, rel, elt, wq, wk, wv, wo, wi0, wi1, wd, cot)


def body(
    byte_ids, lengths, groups, embedding, language, scorer, prenorm, query_weight, key_weight, value_weight,
    output_weight, midnorm, gate_weight, up_weight, down_weight, relative, cotangent,
):
    section = lax.axis_index("section")
    inner = lax.axis_size("dp") // OUTER
    vocab, langs = embedding.shape[0], language.shape[0]
    table = jnp.concatenate([embedding, language, scorer[None], prenorm[None], midnorm[None]], axis=0)
    elt = jnp.pad(table, ((0, 512 - table.shape[0]), (0, 0))).T
    shards = [elt, query_weight, key_weight, value_weight, output_weight, gate_weight, up_weight, down_weight]
    teams = [[o * inner + i for i in range(inner)] for o in range(OUTER)]
    if inner > 1:
        shards = [lax.all_gather(item, "dp", axis_index_groups=teams, axis=0, tiled=True) for item in shards]
    width = query_weight.shape[1]
    rows = shards[1].shape[0]
    count = byte_ids.shape[2]
    place = jnp.arange(width)
    natural = (place % (2 * rows)) // rows * (width // 2) + place // (2 * rows) * rows + place % rows
    pick = lambda item: lax.dynamic_index_in_dim(item, section, 0, False)
    ids = pick(byte_ids)[0].reshape(count // 2, 2).T.reshape(count)
    fill = jnp.zeros((width - count,), jnp.int32)
    ints = jnp.stack(
        [
            jnp.concatenate([ids, fill]),
            jnp.broadcast_to(pick(lengths), (width,)),
            jnp.broadcast_to(pick(groups), (width,)),
            natural.astype(jnp.int32),
        ]
        + [jnp.zeros((width,), jnp.int32)] * 4
    )
    rel = jnp.pad(relative.T, ((0, 16 - relative.shape[1]), (0, 128 - relative.shape[0])))
    encoded, *grads, rel_grad = call(inner, ints, rel, *shards, cotangent[:, 0])
    if inner > 1:
        grads = [
            lax.psum_scatter(item, "dp", axis_index_groups=teams, scatter_dimension=0, tiled=True) for item in grads
        ]
        rel_grad = lax.psum(rel_grad, "dp", axis_index_groups=teams)
    table = grads[0].T
    gains = table[vocab + langs : vocab + langs + 3]
    return (
        encoded[:, None],
        table[:vocab],
        table[vocab : vocab + langs],
        gains[0],
        gains[1],
        *grads[1:5],
        gains[2],
        *grads[5:8],
        rel_grad[: relative.shape[1], : relative.shape[0]].T,
    )


def solution(mesh):
    both = ("section", "dp")
    wide = P(both, None)
    return jax.shard_map(
        body,
        mesh=mesh,
        in_specs=(
            P(None, "dp", None), P(None, "dp"), P(None, "dp"), P(None, both), P(None, both), P(both), P(both),
            wide, wide, wide, wide, P(both), wide, wide, wide, P(), P(None, "dp", None, None),
        ),
        out_specs=(
            P(None, "dp", None, "section"), P(None, both), P(None, both), P(both), P(both),
            wide, wide, wide, wide, P(both), wide, wide, wide, P(),
        ),
        check_vma=False,
    )
```

time: 1640 us -> 230 us (0.14)
  waiting for transfers between devices: 958 us -> 0 us
  blocking collectives: 215 us -> 0 us
  Pallas kernels: 0 us -> 209 us
  matrix products: 148 us -> 0 us
  starting transfers between devices: 138 us -> 0 us
  other arithmetic: 58.3 us -> 0.05 us
  local copies, waits for them, and re-layouts: 58.6 us -> 19.1 us
  loops' own time: 37.6 us -> 0 us
    reduce_scatter x7 -> x0, waiting for transfers between devices: 777 us -> none  [the longest x1 121 us: body(): lax.psum_scatter(grads[10], ('section', 'dp'), scatter_dimension=0, tiled...]
    pallas_call x0 -> x1, Pallas kernels: none -> 209 us  [call(): pl.pallas_call(functools.partial(kernel, inner, (tokens, width, half, ffh...]
    dot_general x55 -> x0, matrix products: 139 us -> none  [the longest x14 45.2 us: outer_sum(): jnp.einsum('tf,tg->fg', left, right, preferred_element_type=jnp.float32)]
    ppermute x6 -> x0, starting transfers between devices: 137 us -> none  [from_behind(): return lax.ppermute(block, axis, route)]
    all_gather x2 -> x0, blocking collectives: 136 us -> none  [the longest x1 71.6 us: body(): lax.all_gather(embedding_low, ('section', 'dp'), axis=1, tiled=True)]
    all_gather x7 -> x0, waiting for transfers between devices: 133 us -> none  [the longest x1 61.4 us: body(): lax.all_gather(down_low, ('section', 'dp'), axis=0, tiled=True)]
    unnamed x2 -> x0, blocking collectives: 79.7 us -> none
    unnamed x16 -> x0, waiting for transfers between devices: 46.4 us -> none
  transfers between devices with their start and end apart: 21 -> 0, of which waited for: 12 -> 0; matrix products, arithmetic and copies ran while one was open for 15% -> 0% of each run, Pallas kernels for 0% -> 0%
where the time goes in v1:
time: 230 us; the launch traced here: 229 us
  Pallas kernels  209 us (91%)
  local copies, waits for them, and re-layouts  19.1 us (8%)
    pallas_call x1, Pallas kernels, call(): pl.pallas_call(functools.partial(kernel, inner, (tokens, width, half, ffh...  209 us
    unnamed x45, local copies, waits for them, and re-layouts  10.5 us

profile of v1, /device:TPU:1, one launch (start us, length us, event | category | flops | bytes accessed | tf_op | source)
XLA Modules:
  0.0 228.8 jit_solution(8735690045113519070)
XLA Ops:
  0.6 0.0 copy-start
  0.7 0.0 copy-start.12
  0.7 0.0 copy-start.13
  0.7 0.6 copy-done.12
  1.3 0.0 copy-done.13
  1.3 0.6 constant_dynamic-slice_fusion
  1.9 0.6 stack_broadcast_in_dim.4
  2.6 0.7 stack_broadcast_in_dim.5
  3.2 0.0 copy-done
  3.3 0.1 reshape_squeeze.3
  3.4 0.1 copy.37
  3.6 0.0 copy-start.9
  3.6 0.0 copy-start.14
  3.6 0.0 copy-start.15
  3.6 0.6 stack.12.refs_0_
  4.3 0.0 copy-done.9
  4.3 0.0 copy-start.8
  4.3 0.1 copy.38
  4.4 0.0 copy-done.14
  4.4 0.1 copy.39
  4.4 0.0 copy-done.15
  4.5 0.1 copy.40
  4.5 0.0 copy-start.16
  4.5 0.7 copy-done.16
  5.2 0.1 copy.41
  5.3 0.0 copy-done.8
  5.3 0.1 concatenate.7
  5.4 0.0 copy-start.10
  5.4 0.6 pad_bitcast_fusion.refs_2_
  6.0 0.1 copy-done.10
  6.1 0.6 pad.9.refs_1_
  6.7 208.8 %shard_map.272 = (bf16[2,256,384]{2,1,0:T(8,128)(2,1)}, f32[24,512]{1,0:T(8,128)}, f32[24,768]{1,0:T(8,128)}, f32[24,768]{1,0:T(8,128)}, f32[24,768]{1,0:T(8,128...) custom-call(s32[8,768]{1,0:T(8,128)} %stack.12.refs_0_, ...), custom_call_target="tpu_custom_call" | custom-call | tf_op jit(solution)/shard_map/pallas_call | solution.py:659
  215.5 1.6 slice_reduce_fusion
  217.1 1.4 slice.28
  218.5 0.8 slice.29
  219.2 0.7 copy.43
  219.9 0.0 copy-start.11
  219.9 0.7 copy-done.11
  220.6 0.6 slice_bitcast_fusion
  221.2 0.0 copy-start.7
  221.2 1.8 copy.53
  223.0 0.0 copy-done.7
  223.0 0.0 copy-start.6
  223.0 0.0 copy-start.5
  223.0 0.6 copy.54
  223.7 0.3 copy-done.6
  223.9 0.0 copy-start.3
  223.9 0.6 copy.55
  224.6 0.0 copy-done.5
  224.6 0.0 copy-start.4
  224.6 0.6 copy.56
  225.2 0.3 copy-done.4
  225.5 0.6 copy.57
  226.1 0.0 copy-done.3
  226.1 0.0 copy-start.2
  226.1 0.7 copy.58
  226.8 0.3 copy-done.2
  227.1 0.0 copy-start.1
  227.1 0.7 copy.59
  227.8 0.3 copy-done.1
  228.1 0.7 copy.60
  (6 shorter events, 0.1 us)
Async XLA Ops:
  0.6 2.6 %copy-start = (s32[2,1,512]{2,1,0:T(1,128)S(1)}, s32[2,1,512]{2,1,0:T(1,128)}, u32[]{:S(2)}) copy-start(s32[2,1,512]{2,1,0:T(1,128)} %param.17) | copy-start | bytes 12292
  0.7 0.7 copy-start.12
  0.7 0.7 copy-start.13
  3.6 0.7 copy-start.9
  3.6 0.8 copy-start.14
  3.6 0.8 copy-start.15
  4.3 1.0 copy-start.8
  4.5 0.7 copy-start.16
  5.4 0.7 copy-start.10
  219.9 0.7 copy-start.11
  221.2 1.8 copy-start.7
  223.0 0.9 copy-start.6
  223.0 1.5 copy-start.5
  223.9 2.2 copy-start.3
  224.6 0.9 copy-start.4
  226.1 1.0 copy-start.2
  227.1 1.0 copy-start.1

commit v2 on v1

--- a/solution.py
+++ b/solution.py
@@ -19,8 +19,10 @@
 F32 = jnp.float32
 I32 = jnp.int32
 
-ELT, QKV, WO, GATE, UP, DOWNW = range(6)
-ALL = (ELT, QKV, WO, GATE, UP, DOWNW)
+ELT, WQ, WK, WV, WO, DOWNW, GU0, GU1, GU2, GU3 = range(10)
+GU = (GU0, GU1, GU2, GU3)
+ALL = tuple(range(10))
+N = len(ALL)
 VOC = 288
 SCORER = 19
 
@@ -46,6 +48,10 @@
 
 def iota(shape, axis):
     return lax.broadcasted_iota(I32, shape, axis)
+
+
+def over(value, n):
+    return (value * (65536 // n + 1)) >> 16
 
 
 def bucket_ids(offsets):
@@ -76,7 +82,7 @@
         self.zn = [(self.s, self.d + (zz - self.z) * 4 * inner) for zz in self.zz]
         self.sent = []
 
-    def barrier(self):
+    def hello(self):
         barrier = pltpu.get_barrier_semaphore()
         for device in (self.sib, self.xn, self.yn, *self.zn):
             pl.semaphore_signal(barrier, inc=1, device_id=device, device_id_type=MESH)
@@ -139,7 +145,7 @@
     def ag0(self, m):
         self.start(self.ag(m, 0))
 
-    def ag1(self, m):
+    def own(self, m):
         self.ag(m, 0).wait_recv()
         chunk = self.ch[m][...].astype(BF)
         if m == DOWNW:
@@ -147,6 +153,8 @@
                 self.w[m][self.s, sec, self.z, self.yx] = chunk[sec]
         else:
             self.w[m][self.s, self.z, self.yx] = chunk
+
+    def ag1(self, m):
         for slot in (1, 2, 3):
             self.start(self.ag(m, slot))
 
@@ -273,90 +281,125 @@
 
 
 def kernel(inner, sizes, *refs):
-    (ints, rel, elt, wq, wk, wv, wo, wi0, wi1, wd, cot) = refs[:11]
-    (enc_out, g_elt, g_q, g_k, g_v, g_o, g_0, g_1, g_d, g_rel) = refs[11:21]
-    rest = refs[21:]
-    take = lambda k: rest[6 * k : 6 * k + 6]
+    (byte_ids, lengths, groups, emb, lang, scorer, prenorm, midnorm, rel, wq, wk, wv, wo, wi0, wi1, wd, cot) = refs[:17]
+    (enc_out, g_elt, g_q, g_k, g_v, g_o, g_0, g_1, g_d, g_rel) = refs[17:27]
+    rest = refs[27:]
+    take = lambda k: rest[N * k : N * k + N]
     w, g, sb, x1, y1, zi, ch, tmp, fo = (take(k) for k in range(9))
-    rest = rest[54:]
+    rest = rest[9 * N :]
     sems, rest = rest[:6], rest[6:]
-    (pi, cb, prow, gthi, gtlo, rows_ref, hid, nrm, qs, ks, vs, bvec, pmat, mixed, mixp, mid, sec_ref,
+    (pi, cb, prow, gthi, gtlo, rows_ref, hid, nrm, nrmt, qs, ks, vs, bvec, pmat, mixed, mixp, mid, sec_ref, sect,
      acc, encb, dq, dk, dv, dvec, relbuf, relin, cp) = rest
     tokens, width, half, ffh = sizes
+    quarter = ffh // 4
     net = Net(inner, w, g, sb, x1, y1, zi, ch, tmp, fo, sems)
     s = net.s
-    net.barrier()
+    net.hello()
 
     def lanes(ref, h, n):
         return ref[:, pl.ds(pl.multiple_of(h * n, 128), n)]
 
-    pi[...] = jnp.where(iota((width, width), 0) == ints[3:4, :], 1.0, 0.0).astype(BF)
-
-    wo_p = dot(wo[...].astype(BF), pi[...])
-    wd_p = dot(wd[...].astype(BF), pi[...])
-    rows_d, rows_f = elt.shape[0], wd.shape[0]
-    fo_wo, fo_wd = fo[WO], fo[DOWNW]
+    def wmat(m, h):
+        return w[m][h].reshape(width, w[m].shape[-1])
+
+    def gput(m, h, value):
+        g[m][h] = value.astype(BF).reshape(g[m].shape[1:])
+
+    rows_d = wq.shape[0]
+    vocab, langs = emb.shape[0], lang.shape[0]
+
+    def turned(value, at):
+        rows = value.shape[0]
+        more = -rows % 8
+        if more:
+            value = jnp.concatenate([value, jnp.zeros((more, rows_d), F32)], axis=0)
+        row = iota((rows + more, 512), 0)
+        spot = (row + at == iota((rows + more, 512), 1)) & (row < rows)
+        return dot_tn(value.astype(BF), jnp.where(spot, 1.0, 0.0).astype(BF))
+
+    vectors = jnp.concatenate([scorer[...], prenorm[...], midnorm[...]], axis=0)
+    elt = turned(emb[...], 0) + turned(lang[...], vocab) + turned(vectors, 256 + SCORER)
+    wide = {}
 
     def halves(m, h):
         if m == ELT:
-            return lanes(elt, h, 256)
-        if m == QKV:
-            return jnp.concatenate([lanes(r, h, half) for r in (wq, wk, wv)], axis=1)
-        if m == GATE:
-            return lanes(wi0, h, ffh)
-        if m == UP:
-            return lanes(wi1, h, ffh)
-        value = wo_p if m == WO else wd_p
+            return jnp.where(h == 0, elt[:, :256], elt[:, 256:])
+        if m in (WQ, WK, WV):
+            return lanes({WQ: wq, WK: wk, WV: wv}[m], h, half)
+        if m in GU:
+            cols = pl.ds(pl.multiple_of(h * ffh + (m - GU0) * quarter, 128), quarter)
+            return jnp.concatenate([wi0[:, cols], wi1[:, cols]], axis=1)
+        value = wide[m]
         return jnp.where(h == 0, value[:, :half], value[:, half:])
 
-    for m in ALL:
+    def exchange(m):
         tmp[m][...] = halves(m, 1 - s)
         net.ag0(m)
-        own = halves(m, s)
+        mine = halves(m, s)
         if m == DOWNW:
-            ch[m][s] = own
+            ch[m][s] = mine
         else:
-            ch[m][pl.ds(s * rows_d, rows_d)] = own
-    for m in ALL:
+            ch[m][pl.ds(s * rows_d, rows_d)] = mine
+
+    for m in (ELT, WQ, WK, WV, *GU):
+        exchange(m)
+    for m in (ELT, WQ, WK):
+        net.own(m)
         net.ag1(m)
-    steps = (net.ag2, net.ag3, net.ag4, net.ag5)
-    for t in range(len(ALL) + 3):
-        for k, step in enumerate(steps):
-            if 0 <= t - k < len(ALL):
-                step(ALL[t - k])
-
-    def wmat(m, h):
-        return w[m][h].reshape(width, w[m].shape[-1])
-
-    def gput(m, h, value):
-        g[m][h] = value.astype(BF).reshape(g[m].shape[1:])
-
+
+    col = iota((1, width), 1)
+    chip = over(col, 2 * rows_d)
+    inside = col - chip * (2 * rows_d)
+    natural = jnp.where(inside < rows_d, chip * rows_d + inside, half + (chip - 1) * rows_d + inside)
+    pi[...] = jnp.where(iota((width, width), 0) == natural, 1.0, 0.0).astype(BF)
+    wide[WO] = dot(wo[...].astype(BF), pi[...])
+    wide[DOWNW] = dot(wd[...].astype(BF), pi[...])
+    exchange(WO)
+    exchange(DOWNW)
+    for m in (WV, WO, DOWNW, *GU):
+        net.own(m)
+
+    gather = {"Z": net.ag2, "X": net.ag3, "D": net.ag4, "S": net.ag5, "A": net.ag1}
+    reduce = {"a": net.rs0, "b": net.rs1, "c": net.rs2, "d": net.rs3, "e": net.rs4}
+
+    def run(text):
+        for word in text.split():
+            m = int(word[1:])
+            if word[0] in gather:
+                gather[word[0]](m)
+                if word[0] == "Z" and m + 3 < N:
+                    net.ag1(m + 3)
+            elif word[0] == "f":
+                last(m)
+            else:
+                reduce[word[0]](m)
+
+    run("Z0")
     cp[...] = dot(cot[s], pi[...]).astype(BF)
 
     span = 2 * tokens
-    ohb = jnp.where(iota((128, span), 0) == bucket_ids(iota((128, span), 1) - (tokens - 1)), 1.0, 0.0).astype(BF)
-    bv = sum(dot(part, ohb) for part in split3(rel[...]))
-    heads = bvec.shape[0]
+    buckets, heads = rel.shape
+    ohb = jnp.where(iota((buckets, span), 0) == bucket_ids(iota((buckets, span), 1) - (tokens - 1)), 1.0, 0.0).astype(BF)
+    bv = sum(dot_tn(part, ohb) for part in split3(rel[...]))
     for h in range(heads):
         bvec[h] = bv[h : h + 1, :]
-
-    count = span
-    ids, length, group = ints[0:1, :count], ints[1:2, :count], ints[2:3, :count]
-    col = iota((1, count), 1)
+    run("X0 Z1")
+
+    length = jnp.where(s == 0, lengths[0:1, :], lengths[1:2, :])
+    group = jnp.where(s == 0, groups[0:1, :], groups[1:2, :])
+    col = iota((1, span), 1)
     pos = jnp.where(col < tokens, 2 * col, 2 * (col - tokens) + 1)
-    valid = pos < length
-    symbol = iota((VOC, count), 0)
-    onehot = jnp.where(((symbol == ids) | (symbol == group + 259)) & valid, 1.0, 0.0)
-    cb[0] = onehot.astype(BF)
+    symbol = iota((VOC, span), 0)
+    onehot = jnp.where(((symbol == byte_ids[s]) | (symbol == group + vocab)) & (col < length), 1.0, 0.0).astype(BF)
 
     def block_of(p, size):
-        return p if size == 1 else p >> 1 if size == 2 else (p * 21846) >> 16 if size == 3 else p >> 2
-
-    rowi = iota((count, 1), 0)
-    posc = jnp.where(rowi < tokens, 2 * rowi, 2 * (rowi - tokens) + 1)
-    for size in (2, 3, 4):
-        pool = jnp.where(block_of(posc, size) == block_of(pos, size), 1.0, 0.0).astype(BF)
-        cb[size - 1] = dot(cb[0], pool).astype(BF)
+        return p if size == 1 else p >> 1 if size == 2 else over(p, 3) if size == 3 else p >> 2
+
+    rowi = iota((span, 1), 0)
+    for size in range(1, BLOCKS + 1):
+        pool = jnp.where(block_of(rowi, size) == block_of(pos, size), 1.0, 0.0).astype(BF)
+        cb[size - 1] = dot(onehot, pool).astype(BF)
+    run("D0 Z2 S0 X1")
 
     e0, e1 = wmat(ELT, 0), wmat(ELT, 1)[:, :128]
     picks = jnp.where(iota((8, 128), 1) == iota((8, 128), 0) + SCORER, 1.0, 0.0).astype(BF)
@@ -376,6 +419,7 @@
     gt = jnp.concatenate([gt, jnp.zeros((384 - VOC, tokens), F32)], axis=0).T
     gthi[...] = gt.astype(BF)
     gtlo[...] = (gt - gt.astype(BF).astype(F32)).astype(BF)
+    run("Z3 D1 X2")
     latent = (
         dot_nt(gthi[:, :256], e0) + dot_nt(gthi[:, 256:], e1)
         + dot_nt(gtlo[:, :256], e0) + dot_nt(gtlo[:, 256:], e1)
@@ -384,15 +428,26 @@
 
     hidden = hid[...].astype(F32)
     r1 = lax.rsqrt(jnp.mean(hidden * hidden, -1, keepdims=True) + EPSILON)
-    nrm[...] = (hidden * r1 * g1).astype(BF)
-    for h in (0, 1):
-        for j, ref in enumerate((qs, ks, vs)):
-            out = dot(nrm[...], w[QKV][h, :, :, :, j * half : (j + 1) * half].reshape(width, half)).astype(BF)
+    normed = hidden * r1 * g1
+    nrm[...] = normed.astype(BF)
+    nrmt[...] = normed.T.astype(BF)
+
+    def project(m, ref):
+        for h in (0, 1):
+            out = dot(nrm[...], wmat(m, h)).astype(BF)
             for i in range(half // 128):
                 ref[h * (half // 128) + i] = out[:, i * 128 : (i + 1) * 128]
 
+    run("Z4 S1 D2 X3")
+    project(WQ, qs)
+    run("Z5 S2 D3 X4")
+    project(WK, ks)
+    run("S3 D4")
+    project(WV, vs)
+    run("Z6")
+
     tcol = iota((1, tokens), 1)
-    valid_key = DOWN * tcol < ints[1:2, :tokens]
+    valid_key = DOWN * tcol < length
     lane = iota((1, 128), 1)
     masks = [jnp.where(lane < 64, 1.0 - e, float(e)).astype(BF) for e in (0, 1)]
 
@@ -411,53 +466,56 @@
         mixed[:, pl.ds(pl.multiple_of(i * 128, 128), 128)] = out.astype(BF)
         return carry
 
-    lax.fori_loop(0, width // 128, forward_pair, 0)
+    pairs = width // 128
+    lax.fori_loop(0, pairs // 2, forward_pair, 0)
+    run("X5 S4 Z7")
+    lax.fori_loop(pairs // 2, pairs, forward_pair, 0)
+    run("D5 X6")
     mixp[...] = dot(mixed[...], pi[...]).astype(BF)
     for h in (0, 1):
         cols = slice(h * half, (h + 1) * half)
         mid[:, cols] = hid[:, cols].astype(F32) + dot(mixp[...], wmat(WO, h))
     middle = mid[...]
     r2 = lax.rsqrt(jnp.mean(middle * middle, -1, keepdims=True) + EPSILON)
-    sec_ref[...] = (middle * r2 * g2).astype(BF)
-
+    second = middle * r2 * g2
+    sec_ref[...] = second.astype(BF)
+    sect[...] = second.T.astype(BF)
     acc[...] = jnp.zeros_like(acc)
     encb[...] = mid[...]
-
-    def feed(i, carry):
-        h = i // 4
-        cols = pl.ds(pl.multiple_of((i % 4) * 256, 256), 256)
-        wg = w[GATE][h, :, :, :, cols].reshape(width, 256)
-        wu = w[UP][h, :, :, :, cols].reshape(width, 256)
-        wdn = [w[DOWNW][j, h, i % 4].reshape(256, half) for j in (0, 1)]
-        gate, upper = dot(sec_ref[...], wg), dot(sec_ref[...], wu)
-        pdelta = dot_nt(cp[:, :half], wdn[0]) + dot_nt(cp[:, half:], wdn[1])
-        square = gate * gate
-        tanh = jnp.tanh(0.7978845608 * (gate + 0.044715 * square * gate))
-        act = 0.5 * gate * (1.0 + tanh)
-        slope = 0.5 * (1.0 + tanh) + 0.5 * gate * (1.0 - tanh * tanh) * 0.7978845608 * (1.0 + 0.134145 * square)
-        product = (act * upper).astype(BF)
-        gdelta = (pdelta * upper * slope).astype(BF)
-        udelta = (pdelta * act).astype(BF)
-        g[GATE][h, :, :, :, cols] = dot_tn(sec_ref[...], gdelta).astype(BF).reshape(4, 4, -1, 256)
-        g[UP][h, :, :, :, cols] = dot_tn(sec_ref[...], udelta).astype(BF).reshape(4, 4, -1, 256)
-        for j in (0, 1):
-            out = slice(j * half, (j + 1) * half)
-            g[DOWNW][j, h, i % 4] = dot_tn(product, cp[:, out]).astype(BF).reshape(4, -1, half)
-            encb[:, out] += dot(product, wdn[j])
-        acc[...] += dot_nt(gdelta, wg) + dot_nt(udelta, wu)
-        return carry
-
-    lax.fori_loop(0, 8, feed, 0)
-
-    encoded = dot_nt(encb[...].astype(BF), pi[...]).astype(BF)
-    for h in (0, 1):
-        mixed[:, h * half : (h + 1) * half] = encoded[:, h * half : (h + 1) * half]
-    enc_out[s] = lanes(mixed, s, half)
-    enc_copy = net.copy(
-        mixed.at[:, pl.ds(pl.multiple_of((1 - s) * half, 128), half)], enc_out.at[s],
-        net.mi_s.at[0], net.mi_r.at[0], net.sib,
-    )
-    net.start(enc_copy)
+    run("Z8 S5 D6 X7 Z9")
+
+    def feed(c):
+        def one(h, carry):
+            wgu = w[GU0 + c][h].reshape(width, 2 * quarter)
+            wdn = [w[DOWNW][j, h, c].reshape(quarter, half) for j in (0, 1)]
+            both = dot(sec_ref[...], wgu)
+            gate, upper = both[:, :quarter], both[:, quarter:]
+            pdelta = dot_nt(cp[:, :half], wdn[0]) + dot_nt(cp[:, half:], wdn[1])
+            square = gate * gate
+            tanh = jnp.tanh(0.7978845608 * (gate + 0.044715 * square * gate))
+            act = 0.5 * gate * (1.0 + tanh)
+            slope = 0.5 * (1.0 + tanh) + 0.5 * gate * (1.0 - tanh * tanh) * 0.7978845608 * (1.0 + 0.134145 * square)
+            product = (act * upper).astype(BF)
+            delta = jnp.concatenate([(pdelta * upper * slope).astype(BF), (pdelta * act).astype(BF)], axis=1)
+            gput(GU0 + c, h, dot(sect[...], delta))
+            for j in (0, 1):
+                out = slice(j * half, (j + 1) * half)
+                g[DOWNW][j, h, c] = dot_tn(product, cp[:, out]).astype(BF).reshape(4, -1, half)
+                encb[:, out] += dot(product, wdn[j])
+            acc[...] += dot_nt(delta, wgu)
+            return carry
+
+        lax.fori_loop(0, 2, one, 0)
+
+    run("S6")
+    feed(0)
+    run("a6 D7 X8 S7")
+    feed(1)
+    run("a7 D8 X9 S8 b6")
+    feed(2)
+    run("a8 D9 b7 S9 c6")
+    feed(3)
+    run("a9 a5 b8 c7 d6")
 
     middle = mid[...]
     r2 = lax.rsqrt(jnp.mean(middle * middle, -1, keepdims=True) + EPSILON)
@@ -465,16 +523,17 @@
     sdelta = acc[...]
     scaled = sdelta * g2
     mid_grad = jnp.sum(sdelta * n2, axis=0, keepdims=True)
-    mdel = encb
+    mdel = acc
     mdel[...] = cp[...].astype(F32) + r2 * (scaled - n2 * jnp.mean(scaled * n2, -1, keepdims=True))
-    adel = mdel[...].astype(BF)
-    sec_ref[...] = adel
+    sec_ref[...] = mdel[...].astype(BF)
+    run("b9 b5")
     for h in (0, 1):
         gput(WO, h, dot_tn(mixp[...], sec_ref[:, h * half : (h + 1) * half]))
+    run("a4 c8 d7")
     back = dot_nt(sec_ref[:, :half], wmat(WO, 0)) + dot_nt(sec_ref[:, half:], wmat(WO, 1))
     mixp[...] = dot_nt(back.astype(BF), pi[...]).astype(BF)
-
     flip = jnp.where(iota((tokens, tokens), 0) + iota((tokens, tokens), 1) == tokens - 1, 1.0, 0.0).astype(BF)
+    run("b4 c9 c5 d8")
 
     def backward_pair(i, carry):
         cols = pl.ds(pl.multiple_of(i * 128, 128), 128)
@@ -489,27 +548,63 @@
             outq = outq + dot(sd, k2 * masks[e])
             outk = outk + dot_tn(sd, q2 * masks[e])
             outv = outv + dot_tn(prob.astype(BF), m2 * masks[e])
-            turned = jnp.concatenate([dot(sd, flip), jnp.zeros((tokens, tokens), F32)], axis=1)
-            skew = pltpu.roll(turned, 0, 1, stride=1, stride_axis=0)
+            reverse = jnp.concatenate([dot(sd, flip), jnp.zeros((tokens, tokens), F32)], axis=1)
+            skew = pltpu.roll(reverse, 0, 1, stride=1, stride_axis=0)
             dvec[h] = jnp.sum(skew, axis=0, keepdims=True)
         dq[:, cols], dk[:, cols], dv[:, cols] = outq.astype(BF), outk.astype(BF), outv.astype(BF)
         return carry
 
-    lax.fori_loop(0, width // 128, backward_pair, 0)
+    lax.fori_loop(0, pairs // 2, backward_pair, 0)
+    run("d9 d5 c4")
+    lax.fori_loop(pairs // 2, pairs, backward_pair, 0)
+    run("e6 e7")
+
+    ohr = jnp.where(iota((buckets, span), 0) == bucket_ids((tokens - 1) - iota((buckets, span), 1)), 1.0, 0.0).astype(BF)
+    lines = jnp.concatenate([dvec[h] for h in range(heads)] + [jnp.zeros((128 - heads, span), F32)], axis=0)
+    relbuf[0] = sum(dot_nt(ohr, part) for part in split3(lines))
+    levels = (
+        ((0, net.sib),), ((1, net.xn),), ((2, net.yn),), ((3, net.zn[0]), (4, net.zn[1]), (5, net.zn[2])),
+    )
+
+    def rel_copy(slot, level, device):
+        return net.copy(relbuf.at[level], relin.at[slot], net.mi_s.at[1 + slot], net.mi_r.at[1 + slot], device)
+
+    def rel_step(level):
+        if level:
+            for slot, device in levels[level - 1]:
+                rel_copy(slot, level - 1, device).wait_recv()
+        if level in (1, 2, 3):
+            relbuf[level] = relbuf[level - 1] + relin[level - 1]
+        if level < 4:
+            for slot, device in levels[level]:
+                net.start(rel_copy(slot, level, device))
+            return
+        place = [jnp.where(net.z == k, 1.0, 0.0) for k in range(4)]
+        level = [relbuf[3], relin[3], relin[4], relin[5]]
+        summed = 0.0
+        for k in range(4):
+            summed = summed + sum(place[z] * level[(z - k) % 4] for z in range(4))
+        g_rel[...] = summed
+
+    rel_step(0)
 
     norm_delta = 0.0
-    for h in (0, 1):
-        for j, ref in enumerate((dq, dk, dv)):
+    for m, ref in ((WQ, dq), (WK, dk), (WV, dv)):
+        for h in (0, 1):
             part = ref[:, h * half : (h + 1) * half]
-            cols = slice(j * half, (j + 1) * half)
-            g[QKV][h, :, :, :, cols] = dot_tn(nrm[...], part).astype(BF).reshape(4, 4, -1, half)
-            norm_delta = norm_delta + dot_nt(part, w[QKV][h, :, :, :, cols].reshape(width, half))
+            gput(m, h, dot(nrmt[...], part))
+            norm_delta = norm_delta + dot_nt(part, wmat(m, h))
+        run(f"a{m}")
+    rel_step(1)
+    run("d4 b1 e8")
     hidden = hid[...].astype(F32)
     r1 = lax.rsqrt(jnp.mean(hidden * hidden, -1, keepdims=True) + EPSILON)
     n1 = hidden * r1
     scaled = norm_delta * g1
     pre_grad = jnp.sum(norm_delta * n1, axis=0, keepdims=True)
     hdel = (mdel[...] + r1 * (scaled - n1 * jnp.mean(scaled * n1, -1, keepdims=True))).astype(BF)
+    rel_step(2)
+    run("b2 b3 e9 c1")
 
     back = jnp.concatenate([dot(hdel, e0), dot(hdel, e1)], axis=1).T[:VOC]
     back = jnp.concatenate([back, back], axis=1)
@@ -523,6 +618,8 @@
     parts = [p.astype(F32) for p in split3(gs)]
     gs3 = jnp.where(lane_v == 0, parts[0], jnp.where(lane_v == 1, parts[1], jnp.where(lane_v == 2, parts[2], 0.0)))
     gs3 = gs3.astype(BF)
+    rel_step(3)
+    run("c2 c3 d1 e5")
     lane_w = iota((width, 128), 1)
     wcol = jnp.where(lane_w < 3, e1.astype(F32)[:, SCORER : SCORER + 1], 0.0).astype(BF)
     gput(ELT, 0, dot_tn(hdel, gthi[:, :256]) + dot_tn(hdel, gtlo[:, :256]) + dot_nt(wcol, gs3[:256]))
@@ -536,37 +633,21 @@
     tail = tail + dot_tn(gains, jnp.where(place, 1.0, 0.0).astype(BF))
     tail = jnp.where(lane_w == SCORER, scorer_grad, tail)
     gput(ELT, 1, jnp.concatenate([tail, jnp.zeros((width, 128), F32)], axis=1))
-
-    ohr = jnp.where(iota((128, span), 0) == bucket_ids((tokens - 1) - iota((128, span), 1)), 1.0, 0.0).astype(BF)
-    lines = jnp.concatenate([dvec[h] for h in range(heads)] + [jnp.zeros((16 - heads, span), F32)], axis=0)
-    relbuf[0] = sum(dot_nt(part, ohr) for part in split3(lines))
-
-    def rel_copy(slot, level, device):
-        return net.copy(relbuf.at[level], relin.at[slot], net.mi_s.at[1 + slot], net.mi_r.at[1 + slot], device)
-
-    for level, partners in enumerate((((0, net.sib),), ((1, net.xn),), ((2, net.yn),), ((3, net.zn[0]), (4, net.zn[1]), (5, net.zn[2])))):
-        for slot, device in partners:
-            net.start(rel_copy(slot, level, device))
-        for slot, device in partners:
-            rel_copy(slot, level, device).wait_recv()
-        if level < 3:
-            relbuf[level + 1] = relbuf[level] + relin[level]
-    place = [jnp.where(net.z == k, 1.0, 0.0) for k in range(4)]
-    level = [relbuf[3], relin[3], relin[4], relin[5]]
-    summed = 0.0
-    for k in range(4):
-        summed = summed + sum(place[z] * level[(z - k) % 4] for z in range(4))
-    g_rel[...] = summed
-
-    order = (DOWNW, UP, GATE, WO, QKV, ELT)
-    for m in order:
-        net.rs0(m)
-    results = {}
+    run("a0")
+    rel_step(4)
+
+    encoded = dot_nt(encb[...].astype(BF), pi[...]).astype(BF)
+    for h in (0, 1):
+        mixed[:, h * half : (h + 1) * half] = encoded[:, h * half : (h + 1) * half]
+    enc_out[s] = lanes(mixed, s, half)
+    enc_copy = net.copy(
+        mixed.at[:, pl.ds(pl.multiple_of((1 - s) * half, 128), half)], enc_out.at[s],
+        net.mi_s.at[0], net.mi_r.at[0], net.sib,
+    )
+    net.start(enc_copy)
 
     def last(m):
-        results[m] = True
         mine, other = net.rs5(m)
-        n = mine.shape[1]
         if m in (WO, DOWNW):
             first = jnp.where(s == 0, mine, other)
             second = jnp.where(s == 0, other, mine)
@@ -574,33 +655,35 @@
             out = g_o if m == WO else g_d
             out[...] = sum(dot_nt(part, pi[...]) for part in split3(both))
             return
-        targets = {ELT: (g_elt,), QKV: (g_q, g_k, g_v), GATE: (g_0,), UP: (g_1,)}[m]
-        n = n // len(targets)
-        for j, ref in enumerate(targets):
-            ref[:, pl.ds(pl.multiple_of(s * n, 128), n)] = mine[:, j * n : (j + 1) * n]
-            ref[:, pl.ds(pl.multiple_of((1 - s) * n, 128), n)] = other[:, j * n : (j + 1) * n]
-
-    steps = (net.rs1, net.rs2, net.rs3, net.rs4, last)
-    for t in range(len(order) + 4):
-        for k, step in enumerate(steps):
-            if 0 <= t - k < len(order):
-                step(order[t - k])
+        for h, value in ((s, mine), (1 - s, other)):
+            if m in GU:
+                cols = pl.ds(pl.multiple_of(h * ffh + (m - GU0) * quarter, 128), quarter)
+                g_0[:, cols] = value[:, :quarter]
+                g_1[:, cols] = value[:, quarter:]
+            else:
+                n = value.shape[1]
+                target = {ELT: g_elt, WQ: g_q, WK: g_k, WV: g_v}[m]
+                target[:, pl.ds(pl.multiple_of(h * n, 128), n)] = value
+
+    run("b0 f6 f7 f8 c0 f9 f5 d2 d3 e4 f4 d0 e1 e2 e3 f1 e0 f2 f3 f0")
     enc_copy.wait_recv()
     net.finish()
 
 
-def call(inner, ints, rel, elt, wq, wk, wv, wo, wi0, wi1, wd, cot):
+VMEM = pl.BlockSpec(memory_space=pltpu.VMEM)
+
+
+def call(inner, *args):
+    wq, wi0, wd, cot = args[9], args[13], args[15], args[16]
     rows_d, width = wq.shape
     rows_f = wd.shape[0]
     half, ffh = width // 2, wi0.shape[1] // 2
     tokens = cot.shape[1]
     span = 2 * tokens
-    heads = width // 64
-    wide = {ELT: 256, QKV: 3 * half, WO: half, GATE: ffh, UP: ffh, DOWNW: half}
+    buckets, heads = args[8].shape
+    wide = {m: 256 if m == ELT else ffh // 2 if m in GU else half for m in ALL}
     chip = {m: (2, rows_f) if m == DOWNW else (2 * rows_d,) for m in ALL}
-
-    def shape(m, lead, sec, tail):
-        return (*lead, *((2,) if m == DOWNW and sec else ()), *tail)
+    mine = {m: rows_f if m == DOWNW else rows_d for m in ALL}
 
     def full(m):
         return (2, 4, 4, rows_f, wide[m]) if m == DOWNW else (4, 4, 2 * rows_d, wide[m])
@@ -616,10 +699,10 @@
     scratch += [pltpu.VMEM(part(m), BF) for m in ALL]
     scratch += [pltpu.VMEM((3, *chip[m], wide[m]), BF) for m in ALL]
     scratch += [pltpu.VMEM((*chip[m], wide[m]), F32) for m in ALL]
-    scratch += [pltpu.VMEM((chip[m][-1] if m == DOWNW else rows_d, wide[m]), F32) for m in ALL]
-    scratch += [pltpu.VMEM((chip[m][-1] if m == DOWNW else rows_d, wide[m]), F32) for m in ALL]
+    scratch += [pltpu.VMEM((mine[m], wide[m]), F32) for m in ALL]
+    scratch += [pltpu.VMEM((mine[m], wide[m]), F32) for m in ALL]
     dma = pltpu.SemaphoreType.DMA
-    scratch += [dma((6, 12)), dma((6, 12)), dma((6, 9)), dma((6, 9)), dma((7,)), dma((7,))]
+    scratch += [dma((N, 12)), dma((N, 12)), dma((N, 9)), dma((N, 9)), dma((7,)), dma((7,))]
     act = (tokens, width)
     scratch += [
         pltpu.VMEM((width, width), BF),
@@ -630,6 +713,7 @@
         pltpu.VMEM((8, width), F32),
         pltpu.VMEM(act, BF),
         pltpu.VMEM(act, BF),
+        pltpu.VMEM((width, tokens), BF),
         pltpu.VMEM((width // 128, tokens, 128), BF),
         pltpu.VMEM((width // 128, tokens, 128), BF),
         pltpu.VMEM((width // 128, tokens, 128), BF),
@@ -639,85 +723,89 @@
         pltpu.VMEM(act, BF),
         pltpu.VMEM(act, F32),
         pltpu.VMEM(act, BF),
+        pltpu.VMEM((width, tokens), BF),
         pltpu.VMEM(act, F32),
         pltpu.VMEM(act, F32),
         pltpu.VMEM(act, BF),
         pltpu.VMEM(act, BF),
         pltpu.VMEM(act, BF),
         pltpu.VMEM((heads, 1, span), F32),
-        pltpu.VMEM((4, 16, 128), F32),
-        pltpu.VMEM((6, 16, 128), F32),
+        pltpu.VMEM((4, buckets, 128), F32),
+        pltpu.VMEM((6, buckets, 128), F32),
         pltpu.VMEM(act, BF),
     ]
     outs = [
         jax.ShapeDtypeStruct((MICRO, tokens, half), BF),
-        jax.ShapeDtypeStruct(elt.shape, F32),
-        *[jax.ShapeDtypeStruct(item.shape, F32) for item in (wq, wk, wv, wo, wi0, wi1, wd)],
-        jax.ShapeDtypeStruct((16, 128), F32),
+        jax.ShapeDtypeStruct((rows_d, 512), F32),
+        *[jax.ShapeDtypeStruct(item.shape, F32) for item in args[9:16]],
+        jax.ShapeDtypeStruct((buckets, 128), F32),
     ]
-    vmem = pl.BlockSpec(memory_space=pltpu.VMEM)
     return pl.pallas_call(
         functools.partial(kernel, inner, (tokens, width, half, ffh)),
         out_shape=outs,
-        in_specs=[vmem] * 11,
-        out_specs=[vmem] * len(outs),
+        in_specs=[VMEM] * len(args),
+        out_specs=[VMEM] * len(outs),
         scratch_shapes=scratch,
         compiler_params=pltpu.CompilerParams(
             collective_id=0, has_side_effects=True, vmem_limit_bytes=63 * 2**20
         ),
-    )(ints, rel, elt, wq, wk, wv, wo, wi0, wi1, wd, cot)
+    )(*args)
+
+
+def settle(vocab, langs, heads, *refs):
+    ins, outs = refs[:10], refs[10:]
+    outs[0][:, 0] = ins[0][...]
+    rows = ins[1].shape[0]
+    table = ins[1][...]
+    table = jnp.concatenate([table, jnp.zeros((128 - rows, table.shape[1]), F32)], axis=0).T[:, :rows]
+    outs[1][...] = table[:vocab]
+    outs[2][...] = table[vocab : vocab + langs]
+    at = vocab + langs
+    for k, i in enumerate((3, 4, 9)):
+        outs[i][...] = table[at + k : at + k + 1]
+    for i, k in zip((5, 6, 7, 8, 10, 11, 12), range(2, 9)):
+        outs[i][...] = ins[k][...]
+    outs[13][...] = ins[9][:, :heads]
 
 
 def body(
     byte_ids, lengths, groups, embedding, language, scorer, prenorm, query_weight, key_weight, value_weight,
     output_weight, midnorm, gate_weight, up_weight, down_weight, relative, cotangent,
 ):
-    section = lax.axis_index("section")
     inner = lax.axis_size("dp") // OUTER
     vocab, langs = embedding.shape[0], language.shape[0]
-    table = jnp.concatenate([embedding, language, scorer[None], prenorm[None], midnorm[None]], axis=0)
-    elt = jnp.pad(table, ((0, 512 - table.shape[0]), (0, 0))).T
-    shards = [elt, query_weight, key_weight, value_weight, output_weight, gate_weight, up_weight, down_weight]
+    tables = [embedding, language, scorer[None], prenorm[None], midnorm[None]]
+    weights = [query_weight, key_weight, value_weight, output_weight, gate_weight, up_weight, down_weight]
     teams = [[o * inner + i for i in range(inner)] for o in range(OUTER)]
     if inner > 1:
-        shards = [lax.all_gather(item, "dp", axis_index_groups=teams, axis=0, tiled=True) for item in shards]
-    width = query_weight.shape[1]
-    rows = shards[1].shape[0]
-    count = byte_ids.shape[2]
-    place = jnp.arange(width)
-    natural = (place % (2 * rows)) // rows * (width // 2) + place // (2 * rows) * rows + place % rows
-    pick = lambda item: lax.dynamic_index_in_dim(item, section, 0, False)
-    ids = pick(byte_ids)[0].reshape(count // 2, 2).T.reshape(count)
-    fill = jnp.zeros((width - count,), jnp.int32)
-    ints = jnp.stack(
-        [
-            jnp.concatenate([ids, fill]),
-            jnp.broadcast_to(pick(lengths), (width,)),
-            jnp.broadcast_to(pick(groups), (width,)),
-            natural.astype(jnp.int32),
-        ]
-        + [jnp.zeros((width,), jnp.int32)] * 4
-    )
-    rel = jnp.pad(relative.T, ((0, 16 - relative.shape[1]), (0, 128 - relative.shape[0])))
-    encoded, *grads, rel_grad = call(inner, ints, rel, *shards, cotangent[:, 0])
+        tables = [lax.all_gather(item, "dp", axis_index_groups=teams, axis=1, tiled=True) for item in tables]
+        weights = [lax.all_gather(item, "dp", axis_index_groups=teams, axis=0, tiled=True) for item in weights]
+    results = call(inner, byte_ids, lengths, groups, *tables, relative, *weights, cotangent[:, 0])
     if inner > 1:
         grads = [
-            lax.psum_scatter(item, "dp", axis_index_groups=teams, scatter_dimension=0, tiled=True) for item in grads
+            lax.psum_scatter(item, "dp", axis_index_groups=teams, scatter_dimension=0, tiled=True)
+            for item in results[1:9]
         ]
-        rel_grad = lax.psum(rel_grad, "dp", axis_index_groups=teams)
-    table = grads[0].T
-    gains = table[vocab + langs : vocab + langs + 3]
-    return (
-        encoded[:, None],
-        table[:vocab],
-        table[vocab : vocab + langs],
-        gains[0],
-        gains[1],
-        *grads[1:5],
-        gains[2],
-        *grads[5:8],
-        rel_grad[: relative.shape[1], : relative.shape[0]].T,
-    )
+        results = [results[0], *grads, lax.psum(results[9], "dp", axis_index_groups=teams)]
+    buckets, heads = relative.shape
+    rows = results[1].shape[0]
+    line = jax.ShapeDtypeStruct((1, rows), F32)
+    like = [jax.ShapeDtypeStruct(item.shape, F32) for item in results[2:9]]
+    shapes = [
+        jax.ShapeDtypeStruct(cotangent.shape[:3] + (results[0].shape[2],), BF),
+        jax.ShapeDtypeStruct((vocab, rows), F32),
+        jax.ShapeDtypeStruct((langs, rows), F32),
+        line, line, *like[:4], line, *like[4:],
+        jax.ShapeDtypeStruct((buckets, heads), F32),
+    ]
+    outs = pl.pallas_call(
+        functools.partial(settle, vocab, langs, heads),
+        out_shape=shapes,
+        in_specs=[VMEM] * 10,
+        out_specs=[VMEM] * 14,
+        compiler_params=pltpu.CompilerParams(vmem_limit_bytes=24 * 2**20),
+    )(*results)
+    return tuple(item[0] if i in (3, 4, 9) else item for i, item in enumerate(outs))
 
 
 def solution(mesh):

time: 230 us -> 183 us (0.80)
  Pallas kernels: 209 us -> 168 us
  local copies, waits for them, and re-layouts: 19.1 us -> 14.4 us
    pallas_call x1, Pallas kernels: 209 us -> 166 us  [call(): pl.pallas_call(functools.partial(kernel, inner, (tokens, width, half, ffh...]
    unnamed x45 -> x30, local copies, waits for them, and re-layouts: 10.5 us -> 14.4 us
    slice x3 -> x0, local copies, waits for them, and re-layouts: 3.72 us -> none  [the longest x1 1.56 us: body(): gains[2]]
where the time goes in v2:
time: 183 us
  Pallas kernels  168 us (92%)
  local copies, waits for them, and re-layouts  14.4 us (8%)
    pallas_call x1, Pallas kernels, call(): pl.pallas_call(functools.partial(kernel, inner, (tokens, width, half, ffh...  166 us
    unnamed x30, local copies, waits for them, and re-layouts  14.4 us

profile of v2, /device:TPU:1, one launch (start us, length us, event | category | flops | bytes accessed | tf_op | source)
XLA Modules:
  0.0 182.6 jit_solution(15629864273725937011)
XLA Ops:
  0.6 0.0 copy-start.10
  0.7 0.0 copy-start.11
  0.7 1.3 copy.31.refs_1_
  2.0 0.0 copy-done.11
  2.0 0.6 copy.32.refs_2_
  2.6 0.0 copy-done.10
  2.6 0.7 copy.34.refs_8_
  3.3 1.5 copy.33.refs_3_
  4.8 166.5 %shard_map.272 = (bf16[2,256,384]{2,1,0:T(8,128)(2,1)}, f32[24,512]{1,0:T(8,128)}, f32[24,768]{1,0:T(8,128)}, f32[24,768]{1,0:T(8,128)}, f32[24,768]{1,0:T(8,128...) custom-call(s32[2,1,512]{2,1,0:T(1,128)} %refs_0_.1, ...), custom_call_target="tpu_custom_call" | custom-call | tf_op jit(solution)/shard_map/pallas_call | solution.py:743
  171.3 0.0 copy-start.9
  171.3 0.7 copy-done.9
  172.0 0.0 copy-start
  172.0 1.0 copy-done
  173.0 0.0 copy-start.1
  173.0 0.9 copy-done.1
  174.0 0.0 copy-start.2
  174.0 0.9 copy-done.2
  174.9 0.0 copy-start.3
  174.9 0.9 copy-done.3
  175.8 0.0 copy-start.4
  175.8 0.9 copy-done.4
  176.7 0.0 copy-start.5
  176.7 0.9 copy-done.5
  177.6 0.0 copy-start.6
  177.6 0.9 copy-done.6
  178.5 0.0 copy-start.7
  178.5 0.9 copy-done.7
  179.3 0.0 copy-start.8
  179.3 0.8 copy-done.8
  180.1 1.1 shard_map.273
  181.2 0.7 copy.36
  181.9 0.7 copy.35
Async XLA Ops:
  0.6 2.0 %copy-start.10 = (f32[32,12]{0,1:T(8,128)S(1)}, f32[32,12]{0,1:T(8,128)}, u32[]{:S(2)}) copy-start(f32[32,12]{0,1:T(8,128)} %param.32) | copy-start | bytes 4612
  0.7 1.3 copy-start.11
  171.3 0.7 copy-start.9
  172.0 1.0 copy-start
  173.0 0.9 copy-start.1
  174.0 0.9 copy-start.2
  174.9 0.9 copy-start.3
  175.8 0.9 copy-start.4
  176.7 0.9 copy-start.5
  177.6 0.9 copy-start.6
  178.5 0.9 copy-start.7
  179.3 0.8 copy-start.8

commit v3 on v2

v3 whole, which is shorter than its diff:
```python
import functools

import jax
import jax.numpy as jnp
from jax import lax
from jax.experimental import pallas as pl
from jax.experimental.pallas import tpu as pltpu
from jax.sharding import PartitionSpec as P

BLOCKS = 4
DOWN = 2
MICRO = 2
OUTER = 16
EPSILON = 1e-06
NEGATIVE = -1000000000.0
LIMITS = (12, 16, 23, 32, 46, 64, 91)
MESH = pl.DeviceIdType.MESH
BF = jnp.bfloat16
F32 = jnp.float32
I32 = jnp.int32

ELT, WQ, WK, WV, WO, DNA, DNB, GU0, GU1, GU2, GU3 = range(11)
DN = (DNA, DNB)
GU = (GU0, GU1, GU2, GU3)
ALL = tuple(range(11))
N = len(ALL)
PLANE_GATHER = ()
PLANE_REDUCE = ()
SCHEDULE = (
    ("A", 6), ("p", 0), ("p", 1), ("p", 2), ("Z", 0), ("A", 2), ("Z", 6), ("A", 1), ("X", 0), ("Z", 2), ("A", 3),
    ("D", 0), ("X", 6), ("Z", 1), ("A", 4), ("S", 0), ("p", 3), ("p", 4), ("Z", 3), ("A", 7), ("X", 2), ("D", 6),
    ("Z", 4), ("A", 5), ("X", 1), ("S", 6), ("D", 2), ("S", 2), ("Z", 7), ("D", 1), ("A", 8), ("X", 3), ("X", 4),
    ("Z", 5), ("A", 9), ("S", 1), ("p", 5), ("p", 6), ("D", 3), ("D", 4), ("Z", 8), ("A", 10), ("S", 3), ("p", 7),
    ("S", 4), ("Z", 9), ("X", 7), ("p", 8), ("X", 5), ("p", 9), ("p", 10), ("Z", 10), ("p", 11), ("D", 7), ("X", 8),
    ("S", 7), ("D", 5), ("X", 9), ("S", 5), ("p", 12), ("D", 8), ("a", 7), ("X", 10), ("D", 9), ("S", 8), ("p", 13),
    ("S", 9), ("D", 10), ("b", 7), ("a", 8), ("p", 14), ("c", 7), ("S", 10), ("b", 8), ("a", 9), ("p", 15), ("b", 9),
    ("a", 10), ("a", 6), ("a", 5), ("p", 16), ("c", 8), ("a", 4), ("p", 17), ("d", 7), ("p", 18), ("c", 9), ("b", 10),
    ("b", 6), ("b", 4), ("b", 5), ("d", 8), ("p", 19), ("e", 7), ("p", 20), ("p", 21), ("p", 22), ("e", 8), ("p", 23),
    ("c", 10), ("c", 4), ("p", 24), ("c", 6), ("c", 5), ("p", 25), ("p", 26), ("p", 27), ("p", 28), ("f", 7),
    ("f", 8), ("d", 9), ("r", 1), ("a", 3), ("a", 1), ("a", 0), ("a", 2), ("r", 2), ("b", 0), ("d", 4), ("r", 3),
    ("b", 3), ("b", 1), ("b", 2), ("e", 9), ("d", 10), ("r", 4), ("f", 9), ("c", 0), ("e", 4), ("d", 6), ("d", 5),
    ("c", 3), ("f", 4), ("c", 1), ("c", 2), ("e", 10), ("d", 0), ("f", 10), ("d", 3), ("d", 1), ("d", 2), ("e", 6),
    ("e", 0), ("e", 5), ("f", 6), ("f", 0), ("f", 5), ("e", 3), ("f", 3), ("e", 1), ("e", 2), ("f", 1), ("f", 2),
)
VOC = 288
SCORER = 19


def dot(a, b):
    return lax.dot_general(a, b, (((1,), (0,)), ((), ())), preferred_element_type=F32)


def dot_nt(a, b):
    return lax.dot_general(a, b, (((1,), (1,)), ((), ())), preferred_element_type=F32)


def dot_tn(a, b):
    return lax.dot_general(a, b, (((0,), (0,)), ((), ())), preferred_element_type=F32)


def split3(x):
    hi = x.astype(BF)
    rest = x - hi.astype(F32)
    mid = rest.astype(BF)
    return hi, mid, (rest - mid.astype(F32)).astype(BF)


def iota(shape, axis):
    return lax.broadcasted_iota(I32, shape, axis)


def over(value, n):
    return (value * (65536 // n + 1)) >> 16


def bucket_ids(offsets):
    distance = jnp.abs(offsets)
    larger = 8 + sum(((distance >= limit).astype(I32) for limit in LIMITS))
    inside = jnp.where(distance < 8, distance, larger)
    return jnp.where(offsets > 0, 16, 0).astype(I32) + inside


class Net:
    def __init__(self, inner, w, g, sb, x1, y1, zi, ch, tmp, fo, sems):
        self.w, self.g, self.sb, self.x1, self.y1 = w, g, sb, x1, y1
        self.zi, self.ch, self.tmp, self.fo = zi, ch, tmp, fo
        self.ag_s, self.ag_r, self.rs_s, self.rs_r, self.mi_s, self.mi_r = sems
        self.s = lax.axis_index("section")
        self.d = lax.axis_index("dp")
        outer = self.d // inner
        self.z = outer // 4
        self.yx = outer % 4
        y, x = self.yx // 2, self.yx % 2
        self.sib = (1 - self.s, self.d)
        self.yx_x = self.yx + 1 - 2 * x
        self.yx_y = self.yx + 2 - 4 * y
        self.yx_d = 3 - self.yx
        self.xn = (self.s, self.d + (1 - 2 * x) * inner)
        self.yn = (self.s, self.d + (1 - 2 * y) * 2 * inner)
        self.dn = (self.s, self.d + (1 - 2 * x) * inner + (1 - 2 * y) * 2 * inner)
        self.zz = [(self.z + k) % 4 for k in (1, 2, 3)]
        self.zn = [(self.s, self.d + (zz - self.z) * 4 * inner) for zz in self.zz]
        self.sent = []

    def hello(self):
        barrier = pltpu.get_barrier_semaphore()
        for device in (self.sib, self.xn, self.yn, self.dn, *self.zn):
            pl.semaphore_signal(barrier, inc=1, device_id=device, device_id_type=MESH)
        pl.semaphore_wait(barrier, 7)

    def copy(self, src, dst, send, recv, device):
        return pltpu.make_async_remote_copy(
            src_ref=src, dst_ref=dst, send_sem=send, recv_sem=recv,
            device_id=device, device_id_type=MESH,
        )

    def start(self, copy):
        copy.start()
        self.sent.append(copy)

    def finish(self):
        for copy in self.sent:
            copy.wait_send()
        self.sent = []

    def blk(self, ref, m, h, z, yx):
        return ref.at[h, :, z, yx] if m in DN else ref.at[h, z, yx]

    def grp(self, ref, m, h, yx):
        return ref.at[h, :, :, yx] if m in DN else ref.at[h, :, yx]

    def part(self, ref, m, h, z0, yx):
        return ref.at[h, :, pl.ds(z0, 2), yx] if m in DN else ref.at[h, pl.ds(z0, 2), yx]

    def plane(self, ref, m, h, z):
        return ref.at[h, :, z] if m in DN else ref.at[h, z]

    def xy2(self, m):
        if m in DN:
            return self.sb[m].at[0, pl.ds(0, 2)], self.sb[m].at[0, pl.ds(2, 2)]
        return self.sb[m].at[0], self.sb[m].at[1]

    def ag(self, m, slot):
        w, s = self.w[m], self.s
        pair = lambda src, dst, dev: self.copy(src, dst, self.ag_s.at[m, slot], self.ag_r.at[m, slot], dev)
        if slot == 0:
            if m in DN:
                dst = self.ch[m].at[s]
            else:
                rows = self.tmp[m].shape[0]
                dst = self.ch[m].at[pl.ds(s * rows, rows)]
            return pair(self.tmp[m], dst, self.sib)
        if m in PLANE_GATHER:
            if slot <= 3:
                ref = self.blk(w, m, s, self.z, self.yx)
                return pair(ref, ref, (self.xn, self.yn, self.dn)[slot - 1])
            ref = self.plane(w, m, s, (self.z, *self.zz)[(0, 0, 0, 0, 3, 2, 1)[slot - 4]] if slot > 7 else self.z)
            return pair(ref, ref, self.sib if slot >= 7 else self.zn[slot - 4])
        if slot <= 3:
            ref = self.blk(w, m, s, self.z, self.yx)
            return pair(ref, ref, self.zn[slot - 1])
        if slot <= 5:
            ref = self.grp(w, m, s, self.yx)
            return pair(ref, ref, self.xn if slot == 4 else self.yn)
        if slot == 6:
            ref = self.part(w, m, s, 0, self.yx_x)
            return pair(ref, ref, self.yn)
        if slot == 7:
            ref = self.part(w, m, s, 2, self.yx_y)
            return pair(ref, ref, self.xn)
        ref = self.grp(w, m, s, (self.yx, self.yx_x, self.yx_y, self.yx_d)[slot - 8])
        return pair(ref, ref, self.sib)

    def ag0(self, m):
        self.start(self.ag(m, 0))

    def own(self, m):
        self.ag(m, 0).wait_recv()
        chunk = self.ch[m][...].astype(BF)
        if m in DN:
            for sec in (0, 1):
                self.w[m][self.s, sec, self.z, self.yx] = chunk[sec]
        else:
            self.w[m][self.s, self.z, self.yx] = chunk

    def ag1(self, m):
        for slot in (1, 2, 3):
            self.start(self.ag(m, slot))

    def ag2(self, m):
        for slot in (1, 2, 3):
            self.ag(m, slot).wait_recv()
        for slot in (4, 5, 6, 7) if m in PLANE_GATHER else (4, 5, 8):
            self.start(self.ag(m, slot))

    def ag3(self, m):
        chain = ((4, (8,)), (5, (9,)), (6, (10,))) if m in PLANE_GATHER else ((4, (6, 9)), (5, (7, 10)))
        for slot, onward in chain:
            self.ag(m, slot).wait_recv()
            for then in onward:
                self.start(self.ag(m, then))

    def ag4(self, m):
        if m in PLANE_GATHER:
            return
        for slot in (6, 7):
            self.ag(m, slot).wait_recv()
        self.start(self.ag(m, 11))

    def ag5(self, m):
        for slot in (7, 8, 9, 10) if m in PLANE_GATHER else (8, 9, 10, 11):
            self.ag(m, slot).wait_recv()

    def rs(self, m, slot):
        g, s = self.g[m], self.s
        pair = lambda src, dst, dev: self.copy(src, dst, self.rs_s.at[m, slot], self.rs_r.at[m, slot], dev)
        if slot == 0:
            return pair(g.at[1 - s], self.sb[m], self.sib)
        if m in PLANE_REDUCE and slot <= 6:
            if slot <= 3:
                return pair(self.plane(g, m, s, self.zz[slot - 1]), self.zi[m].at[slot - 1], self.zn[slot - 1])
            k = slot - 4
            ref = self.blk(g, m, s, self.z, (self.yx_x, self.yx_y, self.yx_d)[k])
            return pair(ref, self.x1[m].at[k], (self.xn, self.yn, self.dn)[k])
        if slot == 1:
            return pair(self.part(g, m, s, 0, self.yx_d), self.x1[m], self.xn)
        if slot == 2:
            return pair(self.part(g, m, s, 2, self.yx_d), self.y1[m], self.yn)
        if slot == 3:
            return pair(self.grp(g, m, s, self.yx_x), self.xy2(m)[0], self.xn)
        if slot == 4:
            return pair(self.grp(g, m, s, self.yx_y), self.xy2(m)[1], self.yn)
        if slot <= 7:
            k = slot - 5
            return pair(self.blk(g, m, s, self.zz[k], self.yx), self.zi[m].at[k], self.zn[k])
        if m in DN:
            src = self.ch[m].at[1 - s]
        else:
            rows = self.fo[m].shape[0]
            src = self.ch[m].at[pl.ds((1 - s) * rows, rows)]
        return pair(src, self.fo[m], self.sib)

    def rs0(self, m):
        self.start(self.rs(m, 0))

    def rs1(self, m):
        self.rs(m, 0).wait_recv()
        g, sb, s = self.g[m], self.sb[m], self.s

        def add(i, carry):
            if m in DN:
                at = (i // 4, i % 4)
                g[s, at[0], at[1]] = (g[s, at[0], at[1]].astype(F32) + sb[at[0], at[1]].astype(F32)).astype(BF)
            else:
                g[s, i // 4, i % 4] = (g[s, i // 4, i % 4].astype(F32) + sb[i // 4, i % 4].astype(F32)).astype(BF)
            return carry

        lax.fori_loop(0, 8 if m in DN else 16, add, 0)
        for slot in (1, 2, 3) if m in PLANE_REDUCE else (1, 2):
            self.start(self.rs(m, slot))

    def rs2(self, m):
        g, s = self.g[m], self.s
        if m in PLANE_REDUCE:
            for slot in (1, 2, 3):
                self.rs(m, slot).wait_recv()
            zi = self.zi[m]

            def whole(yx):
                parts = [zi[k, yx].astype(F32) for k in (0, 1, 2)]
                return g[s, self.z, yx].astype(F32) + (parts[0] + parts[1] + parts[2])

            for slot, yx in ((4, self.yx_x), (5, self.yx_y), (6, self.yx_d)):
                g[s, self.z, yx] = whole(yx).astype(BF)
                self.start(self.rs(m, slot))
            self.ch[m][...] = whole(self.yx)
            return
        for slot, ref, z0, yx in ((1, self.x1[m], 0, self.yx_y), (2, self.y1[m], 2, self.yx_x)):
            self.rs(m, slot).wait_recv()
            for j in (0, 1):
                if m in DN:
                    for sec in (0, 1):
                        mine = g[s, sec, z0 + j, yx].astype(F32)
                        g[s, sec, z0 + j, yx] = (mine + ref[sec, j].astype(F32)).astype(BF)
                else:
                    mine = g[s, z0 + j, yx].astype(F32)
                    g[s, z0 + j, yx] = (mine + ref[j].astype(F32)).astype(BF)
        self.start(self.rs(m, 3))
        self.start(self.rs(m, 4))

    def rs3(self, m):
        if m in PLANE_REDUCE:
            for slot in (4, 5, 6):
                self.rs(m, slot).wait_recv()
            x1 = self.x1[m]
            self.ch[m][...] += x1[0].astype(F32) + x1[1].astype(F32) + x1[2].astype(F32)
            self.start(self.rs(m, 8))
            return
        self.rs(m, 3).wait_recv()
        self.rs(m, 4).wait_recv()
        g, s, yx = self.g[m], self.s, self.yx
        a, b = self.xy2(m)

        def total(sec, z):
            if m in DN:
                return g[s, sec, z, yx].astype(F32) + a[sec, z].astype(F32) + b[sec, z].astype(F32)
            return g[s, z, yx].astype(F32) + a[z].astype(F32) + b[z].astype(F32)

        for slot in (5, 6, 7):
            zz = self.zz[slot - 5]
            if m in DN:
                for sec in (0, 1):
                    g[s, sec, zz, yx] = total(sec, zz).astype(BF)
            else:
                g[s, zz, yx] = total(0, zz).astype(BF)
            self.start(self.rs(m, slot))
        if m in DN:
            for sec in (0, 1):
                self.ch[m][sec] = total(sec, self.z)
        else:
            self.ch[m][...] = total(0, self.z)

    def rs4(self, m):
        if m in PLANE_REDUCE:
            return
        for slot in (5, 6, 7):
            self.rs(m, slot).wait_recv()
        zi = self.zi[m]
        self.ch[m][...] += zi[0].astype(F32) + zi[1].astype(F32) + zi[2].astype(F32)
        self.start(self.rs(m, 8))

    def rs5(self, m):
        if m in DN:
            mine = self.ch[m][self.s]
        else:
            rows = self.fo[m].shape[0]
            mine = self.ch[m][pl.ds(self.s * rows, rows)]
        self.rs(m, 8).wait_recv()
        return mine, self.fo[m][...]


def kernel(inner, sizes, *refs):
    (byte_ids, lengths, groups, emb, lang, scorer, prenorm, midnorm, rel, wq, wk, wv, wo, wi0, wi1, wd, cot) = refs[:17]
    (enc_out, g_elt, g_q, g_k, g_v, g_o, g_0, g_1, g_d, g_rel) = refs[17:27]
    rest = refs[27:]
    take = lambda k: rest[N * k : N * k + N]
    w, g, sb, x1, y1, zi, ch, tmp, fo = (take(k) for k in range(9))
    rest = rest[9 * N :]
    sems, rest = rest[:6], rest[6:]
    (pi, cb, prow, gthi, gtlo, rows_ref, hid, nrm, nrmt, qs, ks, vs, bvec, pmat, mixed, mixp, mid, sec_ref, sect,
     acc, encb, dq, dk, dv, dvec, relbuf, relin, cp) = rest
    tokens, width, half, ffh = sizes
    quarter = ffh // 4
    net = Net(inner, w, g, sb, x1, y1, zi, ch, tmp, fo, sems)
    s = net.s
    net.hello()

    def lanes(ref, h, n):
        return ref[:, pl.ds(pl.multiple_of(h * n, 128), n)]

    def wmat(m, h):
        return w[m][h].reshape(width, w[m].shape[-1])

    def gput(m, h, value):
        g[m][h] = value.astype(BF).reshape(g[m].shape[1:])

    rows_d = wq.shape[0]
    vocab, langs = emb.shape[1], lang.shape[0]

    def turned(value, at):
        rows = value.shape[0]
        more = -rows % 8
        if more:
            value = jnp.concatenate([value, jnp.zeros((more, rows_d), F32)], axis=0)
        row = iota((rows + more, 512), 0)
        spot = (row + at == iota((rows + more, 512), 1)) & (row < rows)
        return dot_tn(value.astype(BF), jnp.where(spot, 1.0, 0.0).astype(BF))

    vectors = jnp.concatenate([scorer[...], prenorm[...], midnorm[...]], axis=0)
    spread = jnp.where(iota((vocab, 512), 0) == iota((vocab, 512), 1), 1.0, 0.0).astype(BF)
    elt = dot(emb[...].astype(BF), spread) + turned(lang[...], vocab) + turned(vectors, 256 + SCORER)
    wide = {}

    def halves(m, h):
        if m == ELT:
            return jnp.where(h == 0, elt[:, :256], elt[:, 256:])
        if m in (WQ, WK, WV):
            return lanes({WQ: wq, WK: wk, WV: wv}[m], h, half)
        if m in GU:
            cols = pl.ds(pl.multiple_of(h * ffh + (m - GU0) * quarter, 128), quarter)
            return jnp.concatenate([wi0[:, cols], wi1[:, cols]], axis=1)
        value = wide[m]
        return jnp.where(h == 0, value[:, :half], value[:, half:])

    def exchange(m):
        tmp[m][...] = halves(m, 1 - s)
        net.ag0(m)
        mine = halves(m, s)
        if m in DN:
            ch[m][s] = mine
        else:
            ch[m][pl.ds(s * rows_d, rows_d)] = mine

    for m in (ELT, WQ, WK, WV, *GU):
        exchange(m)
    first = (0,)
    for m in first:
        net.own(m)
        net.ag1(m)

    col = iota((1, width), 1)
    chip = over(col, 2 * rows_d)
    inside = col - chip * (2 * rows_d)
    natural = jnp.where(inside < rows_d, chip * rows_d + inside, half + (chip - 1) * rows_d + inside)
    pi[...] = jnp.where(iota((width, width), 0) == natural, 1.0, 0.0).astype(BF)
    wide[WO] = dot(wo[...].astype(BF), pi[...])
    down_p = dot(wd[...].astype(BF), pi[...])
    wide[DNA], wide[DNB] = down_p[: wd.shape[0] // 2], down_p[wd.shape[0] // 2 :]
    for m in (WO, *DN):
        exchange(m)
    for m in ALL:
        if m not in first:
            net.own(m)

    span = 2 * tokens
    heads, buckets = rel.shape
    pairs = width // 128
    keep = {}
    mdel = acc

    def turn_cotangent():
        cp[...] = dot(cot[s], pi[...]).astype(BF)


    def bias_lines():
        ohb = jnp.where(iota((buckets, span), 0) == bucket_ids(iota((buckets, span), 1) - (tokens - 1)), 1.0, 0.0)
        bv = sum(dot(part, ohb.astype(BF)) for part in split3(rel[...]))
        for h in range(heads):
            bvec[h] = bv[h : h + 1, :]

    length = jnp.where(s == 0, lengths[:, 0:1], lengths[:, 1:2])
    group = jnp.where(s == 0, groups[:, 0:1], groups[:, 1:2])

    def block_of(p, size):
        return p if size == 1 else p >> 1 if size == 2 else over(p, 3) if size == 3 else p >> 2

    def count_blocks():
        col = iota((1, span), 1)
        pos = jnp.where(col < tokens, 2 * col, 2 * (col - tokens) + 1)
        symbol = iota((VOC, span), 0)
        onehot = jnp.where(((symbol == byte_ids[s]) | (symbol == group + vocab)) & (col < length), 1.0, 0.0).astype(BF)
        rowi = iota((span, 1), 0)
        for size in range(1, BLOCKS + 1):
            pool = jnp.where(block_of(rowi, size) == block_of(pos, size), 1.0, 0.0).astype(BF)
            cb[size - 1] = dot(onehot, pool).astype(BF)

    def table():
        return wmat(ELT, 0), wmat(ELT, 1)[:, :128]

    def choose_blocks():
        e0, e1 = table()
        picks = jnp.where(iota((8, 128), 1) == iota((8, 128), 0) + SCORER, 1.0, 0.0).astype(BF)
        rows_ref[...] = dot_nt(picks, e1)
        ew = jnp.concatenate([dot_tn(e0, e1), dot_tn(e1, e1)[: VOC - 256]], axis=0)[:, SCORER : SCORER + 1]
        ratings = [jnp.sum(cb[b].astype(F32) * ew, axis=0, keepdims=True) / (b + 1) for b in range(BLOCKS)]
        top = functools.reduce(jnp.maximum, ratings)
        raised = [jnp.exp(r - top) for r in ratings]
        total = sum(raised)
        chosen = [r / total for r in raised]
        mixw = 0.0
        for b in range(BLOCKS):
            prow[b : b + 1, :] = chosen[b]
            mixw = mixw + cb[b].astype(F32) * (chosen[b] / (2.0 * (b + 1)))
        gt = mixw[:, :tokens] + mixw[:, tokens:]
        gt = jnp.concatenate([gt, jnp.zeros((384 - VOC, tokens), F32)], axis=0).T
        gthi[...] = gt.astype(BF)
        gtlo[...] = (gt - gt.astype(BF).astype(F32)).astype(BF)

    def make_hidden():
        e0, e1 = table()
        latent = (
            dot_nt(gthi[:, :256], e0) + dot_nt(gthi[:, 256:], e1)
            + dot_nt(gtlo[:, :256], e0) + dot_nt(gtlo[:, 256:], e1)
        )
        hid[...] = latent.astype(BF)

        hidden = hid[...].astype(F32)
        r1 = lax.rsqrt(jnp.mean(hidden * hidden, -1, keepdims=True) + EPSILON)
        normed = hidden * r1 * rows_ref[1:2, :]
        nrm[...] = normed.astype(BF)
        nrmt[...] = normed.T.astype(BF)

    def project(m, ref):
        for h in (0, 1):
            out = dot(nrm[...], wmat(m, h)).astype(BF)
            for i in range(half // 128):
                ref[h * (half // 128) + i] = out[:, i * 128 : (i + 1) * 128]

    tcol = iota((1, tokens), 1)
    valid_key = DOWN * tcol < length
    lane = iota((1, 128), 1)
    masks = [jnp.where(lane < 64, 1.0 - e, float(e)).astype(BF) for e in (0, 1)]

    def forward_pair(i, carry):
        q2, k2, v2 = qs[i], ks[i], vs[i]
        out = 0.0
        for e in (0, 1):
            h = 2 * i + e
            line = jnp.broadcast_to(bvec[h], (tokens, span))
            bias = pltpu.roll(line, tokens + 1, 1, stride=1, stride_axis=0)[:, :tokens]
            scores = jnp.where(valid_key, dot_nt(q2, k2 * masks[e]) + bias, NEGATIVE)
            up = jnp.exp(scores - jnp.max(scores, -1, keepdims=True))
            prob = up * (1.0 / jnp.sum(up, -1, keepdims=True))
            pmat[h] = prob
            out = out + dot(prob.astype(BF), v2 * masks[e])
        mixed[:, pl.ds(pl.multiple_of(i * 128, 128), 128)] = out.astype(BF)
        return carry

    def forward_pairs(k):
        lax.fori_loop(2 * k, 2 * k + 2, forward_pair, 0)

    def make_middle():
        mixp[...] = dot(mixed[...], pi[...]).astype(BF)
        for h in (0, 1):
            cols = slice(h * half, (h + 1) * half)
            mid[:, cols] = hid[:, cols].astype(F32) + dot(mixp[...], wmat(WO, h))
        middle = mid[...]
        r2 = lax.rsqrt(jnp.mean(middle * middle, -1, keepdims=True) + EPSILON)
        second = middle * r2 * rows_ref[2:3, :]
        sec_ref[...] = second.astype(BF)
        sect[...] = second.T.astype(BF)
        acc[...] = jnp.zeros_like(acc)
        encb[...] = mid[...]

    def feed(c):
        def one(h, carry):
            wgu = w[GU0 + c][h].reshape(width, 2 * quarter)
            wdn = [
                jnp.concatenate([w[m][j, h, c] for m in DN], axis=1).reshape(quarter, half) for j in (0, 1)
            ]
            both = dot(sec_ref[...], wgu)
            gate, upper = both[:, :quarter], both[:, quarter:]
            pdelta = dot_nt(cp[:, :half], wdn[0]) + dot_nt(cp[:, half:], wdn[1])
            square = gate * gate
            tanh = jnp.tanh(0.7978845608 * (gate + 0.044715 * square * gate))
            act = 0.5 * gate * (1.0 + tanh)
            slope = 0.5 * (1.0 + tanh) + 0.5 * gate * (1.0 - tanh * tanh) * 0.7978845608 * (1.0 + 0.134145 * square)
            product = (act * upper).astype(BF)
            delta = jnp.concatenate([(pdelta * upper * slope).astype(BF), (pdelta * act).astype(BF)], axis=1)
            gput(GU0 + c, h, dot(sect[...], delta))
            for j in (0, 1):
                out = slice(j * half, (j + 1) * half)
                grad = dot_tn(product, cp[:, out]).astype(BF).reshape(4, -1, half)
                few = grad.shape[1] // 2
                g[DNA][j, h, c], g[DNB][j, h, c] = grad[:, :few], grad[:, few:]
                encb[:, out] += dot(product, wdn[j])
            acc[...] += dot_nt(delta, wgu)
            return carry

        lax.fori_loop(0, 2, one, 0)

    def middle_back():
        middle = mid[...]
        r2 = lax.rsqrt(jnp.mean(middle * middle, -1, keepdims=True) + EPSILON)
        n2 = middle * r2
        sdelta = acc[...]
        scaled = sdelta * rows_ref[2:3, :]
        rows_ref[4:5, :] = jnp.sum(sdelta * n2, axis=0, keepdims=True)
        mdel[...] = cp[...].astype(F32) + r2 * (scaled - n2 * jnp.mean(scaled * n2, -1, keepdims=True))
        sec_ref[...] = mdel[...].astype(BF)
        for h in (0, 1):
            gput(WO, h, dot_tn(mixp[...], sec_ref[:, h * half : (h + 1) * half]))

    def mixed_back():
        back = dot_nt(sec_ref[:, :half], wmat(WO, 0)) + dot_nt(sec_ref[:, half:], wmat(WO, 1))
        mixp[...] = dot_nt(back.astype(BF), pi[...]).astype(BF)
        mid[...] = jnp.zeros_like(mid)

    flip = jnp.where(iota((tokens, tokens), 0) + iota((tokens, tokens), 1) == tokens - 1, 1.0, 0.0).astype(BF)

    def backward_pair(i, carry):
        cols = pl.ds(pl.multiple_of(i * 128, 128), 128)
        q2, k2, v2, m2 = qs[i], ks[i], vs[i], mixp[:, cols]
        outq = outk = outv = 0.0
        for e in (0, 1):
            h = 2 * i + e
            prob = pmat[h]
            wdelta = dot_nt(m2, v2 * masks[e])
            lean = jnp.sum(prob * wdelta, -1, keepdims=True)
            sd = jnp.where(valid_key, prob * (wdelta - lean), 0.0).astype(BF)
            outq = outq + dot(sd, k2 * masks[e])
            outk = outk + dot_tn(sd, q2 * masks[e])
            outv = outv + dot_tn(prob.astype(BF), m2 * masks[e])
            reverse = jnp.concatenate([dot(sd, flip), jnp.zeros((tokens, tokens), F32)], axis=1)
            skew = pltpu.roll(reverse, 0, 1, stride=1, stride_axis=0)
            dvec[h] = jnp.sum(skew, axis=0, keepdims=True)
        dq[:, cols], dk[:, cols], dv[:, cols] = outq.astype(BF), outk.astype(BF), outv.astype(BF)
        return carry

    def backward_pairs(k):
        lax.fori_loop(2 * k, 2 * k + 2, backward_pair, 0)

    def relative_back():
        ohr = jnp.where(iota((128, span), 0) == bucket_ids((tokens - 1) - iota((128, span), 1)), 1.0, 0.0).astype(BF)
        lines = jnp.concatenate([dvec[h] for h in range(heads)] + [jnp.zeros((16 - heads, span), F32)], axis=0)
        relbuf[0] = sum(dot_nt(part, ohr) for part in split3(lines))
        rel_step(0)

    levels = (
        ((0, net.sib),), ((1, net.xn),), ((2, net.yn),), ((3, net.zn[0]), (4, net.zn[1]), (5, net.zn[2])),
    )

    def rel_copy(slot, level, device):
        return net.copy(relbuf.at[level], relin.at[slot], net.mi_s.at[1 + slot], net.mi_r.at[1 + slot], device)

    def rel_step(level):
        if level:
            for slot, device in levels[level - 1]:
                rel_copy(slot, level - 1, device).wait_recv()
        if level in (1, 2, 3):
            relbuf[level] = relbuf[level - 1] + relin[level - 1]
        if level < 4:
            for slot, device in levels[level]:
                net.start(rel_copy(slot, level, device))
            return
        place = [jnp.where(net.z == k, 1.0, 0.0) for k in range(4)]
        level = [relbuf[3], relin[3], relin[4], relin[5]]
        summed = 0.0
        for k in range(4):
            summed = summed + sum(place[z] * level[(z - k) % 4] for z in range(4))
        g_rel[...] = summed

    def weight_back(k):
        m, ref = ((WQ, dq), (WK, dk), (WV, dv))[k]
        for h in (0, 1):
            part = ref[:, h * half : (h + 1) * half]
            gput(m, h, dot(nrmt[...], part))
            mid[...] += dot_nt(part, wmat(m, h))

    def hidden_back():
        hidden = hid[...].astype(F32)
        norm_delta = mid[...]
        r1 = lax.rsqrt(jnp.mean(hidden * hidden, -1, keepdims=True) + EPSILON)
        n1 = hidden * r1
        scaled = norm_delta * rows_ref[1:2, :]
        rows_ref[3:4, :] = jnp.sum(norm_delta * n1, axis=0, keepdims=True)
        delta = mdel[...] + r1 * (scaled - n1 * jnp.mean(scaled * n1, -1, keepdims=True))
        sec_ref[...] = delta.astype(BF)

    def choice_back():
        e0, e1 = table()
        hdel = sec_ref[...]
        back = jnp.concatenate([dot(hdel, e0), dot(hdel, e1)], axis=1).T[:VOC]
        back = jnp.concatenate([back, back], axis=1)
        pdel = [jnp.sum(cb[b].astype(F32) * back, axis=0, keepdims=True) / (2.0 * (b + 1)) for b in range(BLOCKS)]
        lean = sum(prow[b : b + 1, :] * pdel[b] for b in range(BLOCKS))
        flow = 0.0
        for b in range(BLOCKS):
            flow = flow + cb[b].astype(F32) * (prow[b : b + 1, :] * (pdel[b] - lean) / (b + 1))
        gs = jnp.sum(flow, axis=1, keepdims=True)
        lane_v = iota((VOC, 128), 1)
        parts = [p.astype(F32) for p in split3(gs)]
        gs3 = jnp.where(lane_v == 0, parts[0], jnp.where(lane_v == 1, parts[1], jnp.where(lane_v == 2, parts[2], 0.0)))
        gs3 = gs3.astype(BF)
        keep[0] = gs3

    def table_back():
        e0, e1 = table()
        hdel, gs3 = sec_ref[...], keep[0]
        lane_w = iota((width, 128), 1)
        wcol = jnp.where(lane_w < 3, e1.astype(F32)[:, SCORER : SCORER + 1], 0.0).astype(BF)
        gput(ELT, 0, dot_tn(hdel, gthi[:, :256]) + dot_tn(hdel, gtlo[:, :256]) + dot_nt(wcol, gs3[:256]))
        gs_tail = jnp.concatenate([gs3[256:], jnp.zeros((128 + 256 - VOC, 128), BF)], axis=0)
        tail = dot_tn(hdel, gthi[:, 256:]) + dot_tn(hdel, gtlo[:, 256:]) + dot_nt(wcol, gs_tail)
        scorer_grad = jnp.sum(dot(e0, gs3[:256]) + dot(e1, gs_tail), axis=1, keepdims=True)
        gains = [p.astype(F32) for p in (*split3(rows_ref[3:4, :]), *split3(rows_ref[4:5, :]))]
        gains = jnp.concatenate([*gains, jnp.zeros((10, width), F32)], axis=0).astype(BF)
        place_row, place_col = iota((16, 128), 0), iota((16, 128), 1)
        place = (place_row < 6) & (place_col == jnp.where(place_row < 3, SCORER + 1, SCORER + 2))
        tail = tail + dot_tn(gains, jnp.where(place, 1.0, 0.0).astype(BF))
        tail = jnp.where(lane_w == SCORER, scorer_grad, tail)
        gput(ELT, 1, jnp.concatenate([tail, jnp.zeros((width, 128), F32)], axis=1))


    enc_copy = net.copy(
        mixed.at[:, pl.ds(pl.multiple_of((1 - s) * half, 128), half)], enc_out.at[s],
        net.mi_s.at[0], net.mi_r.at[0], net.sib,
    )

    def send_encoded():
        encoded = dot_nt(encb[...].astype(BF), pi[...]).astype(BF)
        for h in (0, 1):
            mixed[:, h * half : (h + 1) * half] = encoded[:, h * half : (h + 1) * half]
        enc_out[s] = lanes(mixed, s, half)
        net.start(enc_copy)

    def last(m):
        mine, other = net.rs5(m)
        if m == WO or m in DN:
            first = jnp.where(s == 0, mine, other)
            second = jnp.where(s == 0, other, mine)
            both = jnp.concatenate([first, second], axis=1)
            value = sum(dot_nt(part, pi[...]) for part in split3(both))
            if m == WO:
                g_o[...] = value
            else:
                rows = value.shape[0]
                g_d[(m - DNA) * rows : (m - DNA + 1) * rows, :] = value
            return
        for h, value in ((s, mine), (1 - s, other)):
            if m in GU:
                cols = pl.ds(pl.multiple_of(h * ffh + (m - GU0) * quarter, 128), quarter)
                g_0[:, cols] = value[:, :quarter]
                g_1[:, cols] = value[:, quarter:]
            else:
                n = value.shape[1]
                target = {ELT: g_elt, WQ: g_q, WK: g_k, WV: g_v}[m]
                target[:, pl.ds(pl.multiple_of(h * n, 128), n)] = value

    pieces = (
        turn_cotangent, bias_lines, count_blocks, choose_blocks, make_hidden,
        *(functools.partial(project, *item) for item in ((WQ, qs), (WK, ks), (WV, vs))),
        *(functools.partial(forward_pairs, k) for k in range(pairs // 2)),
        make_middle,
        *(functools.partial(feed, c) for c in range(4)),
        middle_back, mixed_back,
        *(functools.partial(backward_pairs, k) for k in range(pairs // 2)),
        relative_back,
        *(functools.partial(weight_back, k) for k in range(3)),
        hidden_back, choice_back, table_back, send_encoded,
    )
    steps = {
        "A": net.ag1, "Z": net.ag2, "X": net.ag3, "D": net.ag4, "S": net.ag5,
        "a": net.rs0, "b": net.rs1, "c": net.rs2, "d": net.rs3, "e": net.rs4, "f": last,
        "p": lambda k: pieces[k](), "r": rel_step,
    }
    for kind, index in SCHEDULE:
        steps[kind](index)
    enc_copy.wait_recv()
    net.finish()


VMEM = pl.BlockSpec(memory_space=pltpu.VMEM)


def call(inner, *args):
    wq, wi0, wd, cot = args[9], args[13], args[15], args[16]
    rows_d, width = wq.shape
    rows_f = wd.shape[0] // 2
    half, ffh = width // 2, wi0.shape[1] // 2
    tokens = cot.shape[1]
    span = 2 * tokens
    heads, buckets = args[8].shape
    wide = {m: 256 if m == ELT else ffh // 2 if m in GU else half for m in ALL}
    chip = {m: (2, rows_f) if m in DN else (2 * rows_d,) for m in ALL}
    mine = {m: rows_f if m in DN else rows_d for m in ALL}

    def full(m):
        return (2, 4, 4, rows_f, wide[m]) if m in DN else (4, 4, 2 * rows_d, wide[m])

    def part(m):
        return (2, 2, rows_f, wide[m]) if m in DN else (2, 2 * rows_d, wide[m])

    scratch = []
    scratch += [pltpu.VMEM((2, *full(m)), BF) for m in ALL]
    scratch += [pltpu.VMEM((2, *full(m)), BF) for m in ALL]
    scratch += [pltpu.VMEM(full(m), BF) for m in ALL]
    scratch += [
        pltpu.VMEM((3, *part(m)[1:]) if m in PLANE_REDUCE else part(m), BF) for m in ALL
    ]
    scratch += [pltpu.VMEM((16, 128) if m in PLANE_REDUCE else part(m), BF) for m in ALL]
    scratch += [
        pltpu.VMEM((3, *((4,) if m in PLANE_REDUCE else ()), *chip[m], wide[m]), BF) for m in ALL
    ]
    scratch += [pltpu.VMEM((*chip[m], wide[m]), F32) for m in ALL]
    scratch += [pltpu.VMEM((mine[m], wide[m]), F32) for m in ALL]
    scratch += [pltpu.VMEM((mine[m], wide[m]), F32) for m in ALL]
    dma = pltpu.SemaphoreType.DMA
    scratch += [dma((N, 12)), dma((N, 12)), dma((N, 9)), dma((N, 9)), dma((7,)), dma((7,))]
    act = (tokens, width)
    scratch += [
        pltpu.VMEM((width, width), BF),
        pltpu.VMEM((BLOCKS, VOC, span), BF),
        pltpu.VMEM((8, span), F32),
        pltpu.VMEM((tokens, 384), BF),
        pltpu.VMEM((tokens, 384), BF),
        pltpu.VMEM((8, width), F32),
        pltpu.VMEM(act, BF),
        pltpu.VMEM(act, BF),
        pltpu.VMEM((width, tokens), BF),
        pltpu.VMEM((width // 128, tokens, 128), BF),
        pltpu.VMEM((width // 128, tokens, 128), BF),
        pltpu.VMEM((width // 128, tokens, 128), BF),
        pltpu.VMEM((heads, 1, span), F32),
        pltpu.VMEM((heads, tokens, tokens), F32),
        pltpu.VMEM(act, BF),
        pltpu.VMEM(act, BF),
        pltpu.VMEM(act, F32),
        pltpu.VMEM(act, BF),
        pltpu.VMEM((width, tokens), BF),
        pltpu.VMEM(act, F32),
        pltpu.VMEM(act, F32),
        pltpu.VMEM(act, BF),
        pltpu.VMEM(act, BF),
        pltpu.VMEM(act, BF),
        pltpu.VMEM((heads, 1, span), F32),
        pltpu.VMEM((4, 16, 128), F32),
        pltpu.VMEM((6, 16, 128), F32),
        pltpu.VMEM(act, BF),
    ]
    outs = [
        jax.ShapeDtypeStruct((MICRO, tokens, half), BF),
        jax.ShapeDtypeStruct((rows_d, 512), F32),
        *[jax.ShapeDtypeStruct(item.shape, F32) for item in args[9:16]],
        jax.ShapeDtypeStruct((16, 128), F32),
    ]
    return pl.pallas_call(
        functools.partial(kernel, inner, (tokens, width, half, ffh)),
        out_shape=outs,
        in_specs=[VMEM] * len(args),
        out_specs=[VMEM] * len(outs),
        scratch_shapes=scratch,
        compiler_params=pltpu.CompilerParams(
            collective_id=0, has_side_effects=True, vmem_limit_bytes=63 * 2**20
        ),
    )(*args)


def settle(vocab, langs, heads, buckets, *refs):
    ins, outs = refs[:10], refs[10:]
    outs[0][:, 0] = ins[0][...]
    rows = ins[1].shape[0]
    outs[1][...] = ins[1][:, :vocab]
    table = ins[1][:, 256:]
    table = jnp.concatenate([table, jnp.zeros((128 - rows, 256), F32)], axis=0).T[:, :rows]
    at = vocab - 256
    outs[2][...] = table[at : at + langs]
    at = at + langs
    for k, i in enumerate((3, 4, 9)):
        outs[i][...] = table[at + k : at + k + 1]
    for i, k in zip((5, 6, 7, 8, 10, 11, 12), range(2, 9)):
        outs[i][...] = ins[k][...]
    outs[13][...] = ins[9][:heads, :buckets]


def body(
    byte_ids, lengths, groups, embedding, language, scorer, prenorm, query_weight, key_weight, value_weight,
    output_weight, midnorm, gate_weight, up_weight, down_weight, relative, cotangent,
):
    inner = lax.axis_size("dp") // OUTER
    vocab, langs = embedding.shape[0], language.shape[0]
    tables = [embedding.T, language, scorer[None], prenorm[None], midnorm[None]]
    weights = [query_weight, key_weight, value_weight, output_weight, gate_weight, up_weight, down_weight]
    teams = [[o * inner + i for i in range(inner)] for o in range(OUTER)]
    if inner > 1:
        tables = [
            lax.all_gather(item, "dp", axis_index_groups=teams, axis=min(i, 1), tiled=True)
            for i, item in enumerate(tables)
        ]
        weights = [lax.all_gather(item, "dp", axis_index_groups=teams, axis=0, tiled=True) for item in weights]
    results = call(inner, byte_ids, lengths.T, groups.T, *tables, relative.T, *weights, cotangent[:, 0])
    if inner > 1:
        grads = [
            lax.psum_scatter(item, "dp", axis_index_groups=teams, scatter_dimension=0, tiled=True)
            for item in results[1:9]
        ]
        results = [results[0], *grads, lax.psum(results[9], "dp", axis_index_groups=teams)]
    buckets, heads = relative.shape
    rows = results[1].shape[0]
    line = jax.ShapeDtypeStruct((1, rows), F32)
    like = [jax.ShapeDtypeStruct(item.shape, F32) for item in results[2:9]]
    shapes = [
        jax.ShapeDtypeStruct(cotangent.shape[:3] + (results[0].shape[2],), BF),
        jax.ShapeDtypeStruct((rows, vocab), F32),
        jax.ShapeDtypeStruct((langs, rows), F32),
        line, line, *like[:4], line, *like[4:],
        jax.ShapeDtypeStruct((heads, buckets), F32),
    ]
    outs = pl.pallas_call(
        functools.partial(settle, vocab, langs, heads, buckets),
        out_shape=shapes,
        in_specs=[VMEM] * 10,
        out_specs=[VMEM] * 14,
        compiler_params=pltpu.CompilerParams(vmem_limit_bytes=60 * 2**20),
    )(*results)
    return tuple(item[0] if i in (3, 4, 9) else item.T if i in (1, 13) else item for i, item in enumerate(outs))


def solution(mesh):
    both = ("section", "dp")
    wide = P(both, None)
    return jax.shard_map(
        body,
        mesh=mesh,
        in_specs=(
            P(None, "dp", None), P(None, "dp"), P(None, "dp"), P(None, both), P(None, both), P(both), P(both),
            wide, wide, wide, wide, P(both), wide, wide, wide, P(), P(None, "dp", None, None),
        ),
        out_specs=(
            P(None, "dp", None, "section"), P(None, both), P(None, both), P(both), P(both),
            wide, wide, wide, wide, P(both), wide, wide, wide, P(),
        ),
        check_vma=False,
    )
```

time: 183 us -> 162 us (0.89)
  local copies, waits for them, and re-layouts: 14.4 us -> 0 us
  Pallas kernels: 168 us -> 161 us
    unnamed x30 -> x0, local copies, waits for them, and re-layouts: 14.4 us -> none
    pallas_call x1, Pallas kernels: 166 us -> 159 us  [call(): pl.pallas_call(functools.partial(kernel, inner, (tokens, width, half, ffh...]
where the time goes in v3:
time: 162 us
  Pallas kernels  161 us (99%)
    pallas_call x1, Pallas kernels, call(): pl.pallas_call(functools.partial(kernel, inner, (tokens, width, half, ffh...  159 us

profile of v3, /device:TPU:1, one launch (start us, length us, event | category | flops | bytes accessed | tf_op | source)
XLA Modules:
  0.0 161.8 jit_solution(17297879262117430079)
XLA Ops:
  0.7 158.5 %shard_map.272 = (bf16[2,256,384]{2,1,0:T(8,128)(2,1)}, f32[24,512]{1,0:T(8,128)}, f32[24,768]{1,0:T(8,128)}, f32[24,768]{1,0:T(8,128)}, f32[24,768]{1,0:T(8,128...) custom-call(s32[2,1,512]{2,1,0:T(1,128)} %refs_0_.1, ...), custom_call_target="tpu_custom_call" | custom-call | tf_op jit(solution)/shard_map/pallas_call | solution.py:817
  159.2 2.4 %shard_map.273 = (bf16[2,1,256,384]{3,2,1,0:T(8,128)(2,1)}, f32[24,259]{1,0:T(8,128)}, f32[16,24]{1,0:T(8,128)}, f32[1,24]{1,0:T(1,128)}, f32[1,24]{1,0:T(1,128)...) custom-call(bf16[2,256,384]{2,1,0:T(8,128)(2,1)} %get-tuple-element., ...), custom_call_target="tpu_custom_call" | custom-call | tf_op jit(solution)/shard_map/pallas_call | solution.py:879

commit v4 on v3

--- a/solution.py
+++ b/solution.py
@@ -24,23 +24,23 @@
 GU = (GU0, GU1, GU2, GU3)
 ALL = tuple(range(11))
 N = len(ALL)
-PLANE_GATHER = ()
+PLANE_GATHER = (10,)
 PLANE_REDUCE = ()
 SCHEDULE = (
-    ("A", 6), ("p", 0), ("p", 1), ("p", 2), ("Z", 0), ("A", 2), ("Z", 6), ("A", 1), ("X", 0), ("Z", 2), ("A", 3),
-    ("D", 0), ("X", 6), ("Z", 1), ("A", 4), ("S", 0), ("p", 3), ("p", 4), ("Z", 3), ("A", 7), ("X", 2), ("D", 6),
-    ("Z", 4), ("A", 5), ("X", 1), ("S", 6), ("D", 2), ("S", 2), ("Z", 7), ("D", 1), ("A", 8), ("X", 3), ("X", 4),
-    ("Z", 5), ("A", 9), ("S", 1), ("p", 5), ("p", 6), ("D", 3), ("D", 4), ("Z", 8), ("A", 10), ("S", 3), ("p", 7),
-    ("S", 4), ("Z", 9), ("X", 7), ("p", 8), ("X", 5), ("p", 9), ("p", 10), ("Z", 10), ("p", 11), ("D", 7), ("X", 8),
-    ("S", 7), ("D", 5), ("X", 9), ("S", 5), ("p", 12), ("D", 8), ("a", 7), ("X", 10), ("D", 9), ("S", 8), ("p", 13),
-    ("S", 9), ("D", 10), ("b", 7), ("a", 8), ("p", 14), ("c", 7), ("S", 10), ("b", 8), ("a", 9), ("p", 15), ("b", 9),
-    ("a", 10), ("a", 6), ("a", 5), ("p", 16), ("c", 8), ("a", 4), ("p", 17), ("d", 7), ("p", 18), ("c", 9), ("b", 10),
-    ("b", 6), ("b", 4), ("b", 5), ("d", 8), ("p", 19), ("e", 7), ("p", 20), ("p", 21), ("p", 22), ("e", 8), ("p", 23),
-    ("c", 10), ("c", 4), ("p", 24), ("c", 6), ("c", 5), ("p", 25), ("p", 26), ("p", 27), ("p", 28), ("f", 7),
-    ("f", 8), ("d", 9), ("r", 1), ("a", 3), ("a", 1), ("a", 0), ("a", 2), ("r", 2), ("b", 0), ("d", 4), ("r", 3),
-    ("b", 3), ("b", 1), ("b", 2), ("e", 9), ("d", 10), ("r", 4), ("f", 9), ("c", 0), ("e", 4), ("d", 6), ("d", 5),
-    ("c", 3), ("f", 4), ("c", 1), ("c", 2), ("e", 10), ("d", 0), ("f", 10), ("d", 3), ("d", 1), ("d", 2), ("e", 6),
-    ("e", 0), ("e", 5), ("f", 6), ("f", 0), ("f", 5), ("e", 3), ("f", 3), ("e", 1), ("e", 2), ("f", 1), ("f", 2),
+    ("A", 10), ("Z", 0), ("A", 2), ("p", 0), ("p", 1), ("Z", 1), ("A", 3), ("X", 0), ("p", 2), ("Z", 2), ("A", 4),
+    ("X", 1), ("D", 0), ("S", 0), ("p", 3), ("Z", 3), ("A", 5), ("X", 2), ("D", 1), ("p", 4), ("S", 1), ("p", 5),
+    ("Z", 4), ("A", 6), ("X", 3), ("D", 2), ("S", 2), ("p", 6), ("Z", 5), ("A", 7), ("X", 4), ("D", 3), ("S", 3),
+    ("p", 7), ("p", 8), ("Z", 6), ("A", 8), ("X", 5), ("D", 4), ("p", 9), ("S", 4), ("p", 10), ("Z", 7), ("A", 9),
+    ("X", 6), ("D", 5), ("p", 11), ("S", 5), ("Z", 8), ("X", 7), ("D", 6), ("S", 6), ("Z", 9), ("Z", 10), ("X", 8),
+    ("D", 7), ("S", 7), ("p", 12), ("a", 7), ("X", 9), ("D", 8), ("S", 8), ("b", 7), ("p", 13), ("a", 8), ("D", 9),
+    ("b", 8), ("c", 7), ("S", 9), ("p", 14), ("a", 9), ("b", 9), ("c", 8), ("d", 7), ("X", 10), ("S", 10), ("p", 15),
+    ("a", 10), ("a", 5), ("a", 6), ("c", 9), ("d", 8), ("e", 7), ("p", 16), ("b", 10), ("b", 5), ("a", 4), ("c", 10),
+    ("d", 9), ("e", 8), ("p", 17), ("p", 18), ("p", 19), ("b", 6), ("c", 5), ("d", 10), ("e", 9), ("f", 7), ("p", 20),
+    ("p", 21), ("p", 22), ("a", 1), ("b", 4), ("c", 6), ("d", 5), ("e", 10), ("p", 23), ("a", 2), ("p", 24), ("a", 3),
+    ("b", 1), ("c", 4), ("d", 6), ("e", 5), ("f", 8), ("p", 25), ("r", 1), ("p", 26), ("b", 2), ("c", 1), ("d", 4),
+    ("e", 6), ("p", 27), ("a", 0), ("r", 2), ("b", 3), ("c", 2), ("d", 1), ("e", 4), ("f", 9), ("f", 10), ("p", 28),
+    ("r", 3), ("b", 0), ("c", 3), ("d", 2), ("e", 1), ("f", 5), ("f", 6), ("r", 4), ("c", 0), ("d", 3), ("e", 2),
+    ("f", 1), ("f", 4), ("d", 0), ("e", 3), ("f", 2), ("e", 0), ("f", 3), ("f", 0),
 )
 VOC = 288
 SCORER = 19
@@ -403,7 +403,7 @@
 
     for m in (ELT, WQ, WK, WV, *GU):
         exchange(m)
-    first = (0,)
+    first = (0, 1,)
     for m in first:
         net.own(m)
         net.ag1(m)

time: 162 us -> 151 us (0.932)
  Pallas kernels: 161 us -> 150 us
    pallas_call x1, Pallas kernels: 159 us -> 148 us  [call(): pl.pallas_call(functools.partial(kernel, inner, (tokens, width, half, ffh...]
where the time goes in v4:
time: 151 us
  Pallas kernels  150 us (99%)
    pallas_call x1, Pallas kernels, call(): pl.pallas_call(functools.partial(kernel, inner, (tokens, width, half, ffh...  148 us

profile of v4, /device:TPU:1, one launch (start us, length us, event | category | flops | bytes accessed | tf_op | source)
XLA Modules:
  0.0 151.1 jit_solution(11605018853812117643)
XLA Ops:
  0.7 147.8 %shard_map.272 = (bf16[2,256,384]{2,1,0:T(8,128)(2,1)}, f32[24,512]{1,0:T(8,128)}, f32[24,768]{1,0:T(8,128)}, f32[24,768]{1,0:T(8,128)}, f32[24,768]{1,0:T(8,128...) custom-call(s32[2,1,512]{2,1,0:T(1,128)} %refs_0_.1, ...), custom_call_target="tpu_custom_call" | custom-call | tf_op jit(solution)/shard_map/pallas_call | solution.py:817
  148.5 2.4 %shard_map.273 = (bf16[2,1,256,384]{3,2,1,0:T(8,128)(2,1)}, f32[24,259]{1,0:T(8,128)}, f32[16,24]{1,0:T(8,128)}, f32[1,24]{1,0:T(1,128)}, f32[1,24]{1,0:T(1,128)...) custom-call(bf16[2,256,384]{2,1,0:T(8,128)(2,1)} %get-tuple-element., ...), custom_call_target="tpu_custom_call" | custom-call | tf_op jit(solution)/shard_map/pallas_call | solution.py:879

commit v5 on v4

--- a/solution.py
+++ b/solution.py
@@ -27,20 +27,20 @@
 PLANE_GATHER = (10,)
 PLANE_REDUCE = ()
 SCHEDULE = (
-    ("A", 10), ("Z", 0), ("A", 2), ("p", 0), ("p", 1), ("Z", 1), ("A", 3), ("X", 0), ("p", 2), ("Z", 2), ("A", 4),
-    ("X", 1), ("D", 0), ("S", 0), ("p", 3), ("Z", 3), ("A", 5), ("X", 2), ("D", 1), ("p", 4), ("S", 1), ("p", 5),
-    ("Z", 4), ("A", 6), ("X", 3), ("D", 2), ("S", 2), ("p", 6), ("Z", 5), ("A", 7), ("X", 4), ("D", 3), ("S", 3),
-    ("p", 7), ("p", 8), ("Z", 6), ("A", 8), ("X", 5), ("D", 4), ("p", 9), ("S", 4), ("p", 10), ("Z", 7), ("A", 9),
-    ("X", 6), ("D", 5), ("p", 11), ("S", 5), ("Z", 8), ("X", 7), ("D", 6), ("S", 6), ("Z", 9), ("Z", 10), ("X", 8),
-    ("D", 7), ("S", 7), ("p", 12), ("a", 7), ("X", 9), ("D", 8), ("S", 8), ("b", 7), ("p", 13), ("a", 8), ("D", 9),
-    ("b", 8), ("c", 7), ("S", 9), ("p", 14), ("a", 9), ("b", 9), ("c", 8), ("d", 7), ("X", 10), ("S", 10), ("p", 15),
-    ("a", 10), ("a", 5), ("a", 6), ("c", 9), ("d", 8), ("e", 7), ("p", 16), ("b", 10), ("b", 5), ("a", 4), ("c", 10),
-    ("d", 9), ("e", 8), ("p", 17), ("p", 18), ("p", 19), ("b", 6), ("c", 5), ("d", 10), ("e", 9), ("f", 7), ("p", 20),
-    ("p", 21), ("p", 22), ("a", 1), ("b", 4), ("c", 6), ("d", 5), ("e", 10), ("p", 23), ("a", 2), ("p", 24), ("a", 3),
-    ("b", 1), ("c", 4), ("d", 6), ("e", 5), ("f", 8), ("p", 25), ("r", 1), ("p", 26), ("b", 2), ("c", 1), ("d", 4),
-    ("e", 6), ("p", 27), ("a", 0), ("r", 2), ("b", 3), ("c", 2), ("d", 1), ("e", 4), ("f", 9), ("f", 10), ("p", 28),
-    ("r", 3), ("b", 0), ("c", 3), ("d", 2), ("e", 1), ("f", 5), ("f", 6), ("r", 4), ("c", 0), ("d", 3), ("e", 2),
-    ("f", 1), ("f", 4), ("d", 0), ("e", 3), ("f", 2), ("e", 0), ("f", 3), ("f", 0),
+    ("A", 10), ("Z", 0), ("A", 2), ("p", 0), ("Z", 1), ("A", 3), ("X", 0), ("Z", 2), ("A", 4), ("X", 1), ("D", 0),
+    ("S", 0), ("p", 3), ("Z", 3), ("A", 5), ("X", 2), ("D", 1), ("p", 4), ("S", 1), ("p", 5), ("Z", 4), ("A", 6),
+    ("X", 3), ("D", 2), ("S", 2), ("p", 6), ("Z", 5), ("A", 7), ("X", 4), ("D", 3), ("S", 3), ("p", 7), ("p", 8),
+    ("Z", 6), ("A", 8), ("X", 5), ("D", 4), ("p", 9), ("S", 4), ("p", 10), ("Z", 7), ("A", 9), ("X", 6), ("D", 5),
+    ("p", 11), ("S", 5), ("Z", 8), ("X", 7), ("D", 6), ("S", 6), ("Z", 9), ("Z", 10), ("X", 8), ("D", 7), ("S", 7),
+    ("p", 12), ("a", 7), ("X", 9), ("b", 7), ("D", 8), ("S", 8), ("p", 13), ("a", 8), ("D", 9), ("b", 8), ("S", 9),
+    ("c", 7), ("p", 14), ("a", 9), ("b", 9), ("c", 8), ("d", 7), ("X", 10), ("S", 10), ("p", 15), ("a", 10), ("a", 5),
+    ("a", 6), ("c", 9), ("b", 10), ("d", 8), ("e", 7), ("p", 16), ("b", 5), ("a", 4), ("c", 10), ("b", 6), ("d", 9),
+    ("e", 8), ("p", 17), ("p", 18), ("p", 19), ("c", 5), ("d", 10), ("e", 9), ("f", 7), ("p", 20), ("p", 21),
+    ("p", 22), ("a", 1), ("c", 6), ("b", 4), ("d", 5), ("e", 10), ("p", 23), ("a", 2), ("p", 24), ("a", 3), ("b", 1),
+    ("c", 4), ("d", 6), ("e", 5), ("f", 8), ("p", 25), ("r", 1), ("p", 26), ("b", 2), ("c", 1), ("d", 4), ("e", 6),
+    ("p", 27), ("a", 0), ("r", 2), ("b", 3), ("c", 2), ("d", 1), ("e", 4), ("f", 9), ("f", 10), ("p", 28), ("r", 3),
+    ("b", 0), ("c", 3), ("d", 2), ("e", 1), ("f", 5), ("f", 6), ("r", 4), ("c", 0), ("d", 3), ("e", 2), ("f", 1),
+    ("f", 4), ("d", 0), ("e", 3), ("f", 2), ("e", 0), ("f", 3), ("f", 0),
 )
 VOC = 288
 SCORER = 19
@@ -102,11 +102,13 @@
         self.zn = [(self.s, self.d + (zz - self.z) * 4 * inner) for zz in self.zz]
         self.sent = []
 
-    def hello(self):
+    def greet(self):
         barrier = pltpu.get_barrier_semaphore()
         for device in (self.sib, self.xn, self.yn, self.dn, *self.zn):
             pl.semaphore_signal(barrier, inc=1, device_id=device, device_id_type=MESH)
-        pl.semaphore_wait(barrier, 7)
+
+    def meet(self):
+        pl.semaphore_wait(pltpu.get_barrier_semaphore(), 7)
 
     def copy(self, src, dst, send, recv, device):
         return pltpu.make_async_remote_copy(
@@ -340,7 +342,8 @@
 
 
 def kernel(inner, sizes, *refs):
-    (byte_ids, lengths, groups, emb, lang, scorer, prenorm, midnorm, rel, wq, wk, wv, wo, wi0, wi1, wd, cot) = refs[:17]
+    (byte_ids, lengths, groups, emb, lang, scorer, prenorm, midnorm, rel) = refs[:9]
+    given = refs[9:17]
     (enc_out, g_elt, g_q, g_k, g_v, g_o, g_0, g_1, g_d, g_rel) = refs[17:27]
     rest = refs[27:]
     take = lambda k: rest[N * k : N * k + N]
@@ -348,12 +351,17 @@
     rest = rest[9 * N :]
     sems, rest = rest[:6], rest[6:]
     (pi, cb, prow, gthi, gtlo, rows_ref, hid, nrm, nrmt, qs, ks, vs, bvec, pmat, mixed, mixp, mid, sec_ref, sect,
-     acc, encb, dq, dk, dv, dvec, relbuf, relin, cp) = rest
+     acc, encb, dq, dk, dv, dvec, relbuf, relin, cp) = rest[:28]
+    held, arrived = rest[28:36], rest[36]
+    (wq, wk, wv, wo, wi0, wi1, wd, cot) = held
     tokens, width, half, ffh = sizes
     quarter = ffh // 4
     net = Net(inner, w, g, sb, x1, y1, zi, ch, tmp, fo, sems)
     s = net.s
-    net.hello()
+    net.greet()
+    fetches = [pltpu.make_async_copy(a, b, arrived.at[k]) for k, (a, b) in enumerate(zip(given, held))]
+    for fetch in fetches:
+        fetch.start()
 
     def lanes(ref, h, n):
         return ref[:, pl.ds(pl.multiple_of(h * n, 128), n)]
@@ -376,6 +384,11 @@
         spot = (row + at == iota((rows + more, 512), 1)) & (row < rows)
         return dot_tn(value.astype(BF), jnp.where(spot, 1.0, 0.0).astype(BF))
 
+    col = iota((1, width), 1)
+    chip = over(col, 2 * rows_d)
+    inside = col - chip * (2 * rows_d)
+    natural = jnp.where(inside < rows_d, chip * rows_d + inside, half + (chip - 1) * rows_d + inside)
+    pi[...] = jnp.where(iota((width, width), 0) == natural, 1.0, 0.0).astype(BF)
     vectors = jnp.concatenate([scorer[...], prenorm[...], midnorm[...]], axis=0)
     spread = jnp.where(iota((vocab, 512), 0) == iota((vocab, 512), 1), 1.0, 0.0).astype(BF)
     elt = dot(emb[...].astype(BF), spread) + turned(lang[...], vocab) + turned(vectors, 256 + SCORER)
@@ -400,27 +413,6 @@
             ch[m][s] = mine
         else:
             ch[m][pl.ds(s * rows_d, rows_d)] = mine
-
-    for m in (ELT, WQ, WK, WV, *GU):
-        exchange(m)
-    first = (0, 1,)
-    for m in first:
-        net.own(m)
-        net.ag1(m)
-
-    col = iota((1, width), 1)
-    chip = over(col, 2 * rows_d)
-    inside = col - chip * (2 * rows_d)
-    natural = jnp.where(inside < rows_d, chip * rows_d + inside, half + (chip - 1) * rows_d + inside)
-    pi[...] = jnp.where(iota((width, width), 0) == natural, 1.0, 0.0).astype(BF)
-    wide[WO] = dot(wo[...].astype(BF), pi[...])
-    down_p = dot(wd[...].astype(BF), pi[...])
-    wide[DNA], wide[DNB] = down_p[: wd.shape[0] // 2], down_p[wd.shape[0] // 2 :]
-    for m in (WO, *DN):
-        exchange(m)
-    for m in ALL:
-        if m not in first:
-            net.own(m)
 
     span = 2 * tokens
     heads, buckets = rel.shape
@@ -734,6 +726,27 @@
         "a": net.rs0, "b": net.rs1, "c": net.rs2, "d": net.rs3, "e": net.rs4, "f": last,
         "p": lambda k: pieces[k](), "r": rel_step,
     }
+    bias_lines()
+    count_blocks()
+    for fetch in fetches[:7]:
+        fetch.wait()
+    net.meet()
+    for m in (ELT, WQ, WK, WV, *GU):
+        exchange(m)
+    first = (0, 1,)
+    for m in first:
+        net.own(m)
+        net.ag1(m)
+
+    wide[WO] = dot(wo[...].astype(BF), pi[...])
+    down_p = dot(wd[...].astype(BF), pi[...])
+    wide[DNA], wide[DNB] = down_p[: wd.shape[0] // 2], down_p[wd.shape[0] // 2 :]
+    for m in (WO, *DN):
+        exchange(m)
+    for m in ALL:
+        if m not in first:
+            net.own(m)
+    fetches[7].wait()
     for kind, index in SCHEDULE:
         steps[kind](index)
     enc_copy.wait_recv()
@@ -807,6 +820,8 @@
         pltpu.VMEM((4, 16, 128), F32),
         pltpu.VMEM((6, 16, 128), F32),
         pltpu.VMEM(act, BF),
+        *[pltpu.VMEM(item.shape, item.dtype) for item in args[9:]],
+        dma((8,)),
     ]
     outs = [
         jax.ShapeDtypeStruct((MICRO, tokens, half), BF),
@@ -817,7 +832,7 @@
     return pl.pallas_call(
         functools.partial(kernel, inner, (tokens, width, half, ffh)),
         out_shape=outs,
-        in_specs=[VMEM] * len(args),
+        in_specs=[VMEM] * 9 + [pl.BlockSpec(memory_space=pl.ANY)] * 8,
         out_specs=[VMEM] * len(outs),
         scratch_shapes=scratch,
         compiler_params=pltpu.CompilerParams(

time: 151 us -> 150 us (level)
  no operation moved by 1% of the time
where the time goes in v5:
time: 150 us
  Pallas kernels  149 us (99%)
    pallas_call x1, Pallas kernels, call(): pl.pallas_call(functools.partial(kernel, inner, (tokens, width, half, ffh...  146 us

profile of v5, /device:TPU:1, one launch (start us, length us, event | category | flops | bytes accessed | tf_op | source)
XLA Modules:
  0.0 149.7 jit_solution(15858955356803655173)
XLA Ops:
  0.7 146.5 %shard_map.272 = (bf16[2,256,384]{2,1,0:T(8,128)(2,1)}, f32[24,512]{1,0:T(8,128)}, f32[24,768]{1,0:T(8,128)}, f32[24,768]{1,0:T(8,128)}, f32[24,768]{1,0:T(8,128...) custom-call(s32[2,1,512]{2,1,0:T(1,128)} %refs_0_.1, ...), custom_call_target="tpu_custom_call" | custom-call | tf_op jit(solution)/shard_map/pallas_call | solution.py:832
  147.1 2.4 %shard_map.273 = (bf16[2,1,256,384]{3,2,1,0:T(8,128)(2,1)}, f32[24,259]{1,0:T(8,128)}, f32[16,24]{1,0:T(8,128)}, f32[1,24]{1,0:T(1,128)}, f32[1,24]{1,0:T(1,128)...) custom-call(bf16[2,256,384]{2,1,0:T(8,128)(2,1)} %get-tuple-element., ...), custom_call_target="tpu_custom_call" | custom-call | tf_op jit(solution)/shard_map/pallas_call | solution.py:894

commit v6 on v5

--- a/solution.py
+++ b/solution.py
@@ -32,15 +32,15 @@
     ("X", 3), ("D", 2), ("S", 2), ("p", 6), ("Z", 5), ("A", 7), ("X", 4), ("D", 3), ("S", 3), ("p", 7), ("p", 8),
     ("Z", 6), ("A", 8), ("X", 5), ("D", 4), ("p", 9), ("S", 4), ("p", 10), ("Z", 7), ("A", 9), ("X", 6), ("D", 5),
     ("p", 11), ("S", 5), ("Z", 8), ("X", 7), ("D", 6), ("S", 6), ("Z", 9), ("Z", 10), ("X", 8), ("D", 7), ("S", 7),
-    ("p", 12), ("a", 7), ("X", 9), ("b", 7), ("D", 8), ("S", 8), ("p", 13), ("a", 8), ("D", 9), ("b", 8), ("S", 9),
-    ("c", 7), ("p", 14), ("a", 9), ("b", 9), ("c", 8), ("d", 7), ("X", 10), ("S", 10), ("p", 15), ("a", 10), ("a", 5),
-    ("a", 6), ("c", 9), ("b", 10), ("d", 8), ("e", 7), ("p", 16), ("b", 5), ("a", 4), ("c", 10), ("b", 6), ("d", 9),
-    ("e", 8), ("p", 17), ("p", 18), ("p", 19), ("c", 5), ("d", 10), ("e", 9), ("f", 7), ("p", 20), ("p", 21),
-    ("p", 22), ("a", 1), ("c", 6), ("b", 4), ("d", 5), ("e", 10), ("p", 23), ("a", 2), ("p", 24), ("a", 3), ("b", 1),
-    ("c", 4), ("d", 6), ("e", 5), ("f", 8), ("p", 25), ("r", 1), ("p", 26), ("b", 2), ("c", 1), ("d", 4), ("e", 6),
-    ("p", 27), ("a", 0), ("r", 2), ("b", 3), ("c", 2), ("d", 1), ("e", 4), ("f", 9), ("f", 10), ("p", 28), ("r", 3),
-    ("b", 0), ("c", 3), ("d", 2), ("e", 1), ("f", 5), ("f", 6), ("r", 4), ("c", 0), ("d", 3), ("e", 2), ("f", 1),
-    ("f", 4), ("d", 0), ("e", 3), ("f", 2), ("e", 0), ("f", 3), ("f", 0),
+    ("q", 0), ("q", 1), ("a", 7), ("X", 9), ("b", 7), ("D", 8), ("S", 8), ("q", 2), ("q", 3), ("a", 8), ("D", 9),
+    ("b", 8), ("S", 9), ("q", 4), ("c", 7), ("q", 5), ("a", 9), ("b", 9), ("c", 8), ("X", 10), ("S", 10), ("q", 6),
+    ("d", 7), ("q", 7), ("a", 10), ("a", 5), ("a", 6), ("c", 9), ("b", 10), ("d", 8), ("e", 7), ("p", 16), ("b", 5),
+    ("a", 4), ("c", 10), ("b", 6), ("d", 9), ("e", 8), ("p", 17), ("p", 18), ("p", 19), ("c", 5), ("d", 10), ("e", 9),
+    ("f", 7), ("p", 20), ("p", 21), ("p", 22), ("a", 1), ("c", 6), ("b", 4), ("d", 5), ("e", 10), ("p", 23), ("a", 2),
+    ("p", 24), ("a", 3), ("b", 1), ("c", 4), ("d", 6), ("e", 5), ("f", 8), ("p", 25), ("r", 1), ("p", 26), ("b", 2),
+    ("c", 1), ("d", 4), ("e", 6), ("p", 27), ("a", 0), ("r", 2), ("b", 3), ("c", 2), ("d", 1), ("e", 4), ("f", 9),
+    ("f", 10), ("p", 28), ("r", 3), ("b", 0), ("c", 3), ("d", 2), ("e", 1), ("f", 5), ("f", 6), ("r", 4), ("c", 0),
+    ("d", 3), ("e", 2), ("f", 1), ("f", 4), ("d", 0), ("e", 3), ("f", 2), ("e", 0), ("f", 3), ("f", 0),
 )
 VOC = 288
 SCORER = 19
@@ -344,7 +344,7 @@
 def kernel(inner, sizes, *refs):
     (byte_ids, lengths, groups, emb, lang, scorer, prenorm, midnorm, rel) = refs[:9]
     given = refs[9:17]
-    (enc_out, g_elt, g_q, g_k, g_v, g_o, g_0, g_1, g_d, g_rel) = refs[17:27]
+    enc_out, g_elt, *final, g_rel = refs[17:27]
     rest = refs[27:]
     take = lambda k: rest[N * k : N * k + N]
     w, g, sb, x1, y1, zi, ch, tmp, fo = (take(k) for k in range(9))
@@ -353,6 +353,8 @@
     (pi, cb, prow, gthi, gtlo, rows_ref, hid, nrm, nrmt, qs, ks, vs, bvec, pmat, mixed, mixp, mid, sec_ref, sect,
      acc, encb, dq, dk, dv, dvec, relbuf, relin, cp) = rest[:28]
     held, arrived = rest[28:36], rest[36]
+    made, written = rest[37:44], rest[44]
+    (g_q, g_k, g_v, g_o, g_0, g_1, g_d) = made
     (wq, wk, wv, wo, wi0, wi1, wd, cot) = held
     tokens, width, half, ffh = sizes
     quarter = ffh // 4
@@ -524,7 +526,9 @@
         acc[...] = jnp.zeros_like(acc)
         encb[...] = mid[...]
 
-    def feed(c):
+    def feed(k):
+        c, half_at = k // 2, k % 2
+
         def one(h, carry):
             wgu = w[GU0 + c][h].reshape(width, 2 * quarter)
             wdn = [
@@ -549,7 +553,7 @@
             acc[...] += dot_nt(delta, wgu)
             return carry
 
-        lax.fori_loop(0, 2, one, 0)
+        lax.fori_loop(half_at, half_at + 1, one, 0)
 
     def middle_back():
         middle = mid[...]
@@ -714,7 +718,7 @@
         *(functools.partial(project, *item) for item in ((WQ, qs), (WK, ks), (WV, vs))),
         *(functools.partial(forward_pairs, k) for k in range(pairs // 2)),
         make_middle,
-        *(functools.partial(feed, c) for c in range(4)),
+        *(None for c in range(4)),
         middle_back, mixed_back,
         *(functools.partial(backward_pairs, k) for k in range(pairs // 2)),
         relative_back,
@@ -724,7 +728,7 @@
     steps = {
         "A": net.ag1, "Z": net.ag2, "X": net.ag3, "D": net.ag4, "S": net.ag5,
         "a": net.rs0, "b": net.rs1, "c": net.rs2, "d": net.rs3, "e": net.rs4, "f": last,
-        "p": lambda k: pieces[k](), "r": rel_step,
+        "p": lambda k: pieces[k](), "q": feed, "r": rel_step,
     }
     bias_lines()
     count_blocks()
@@ -747,13 +751,24 @@
         if m not in first:
             net.own(m)
     fetches[7].wait()
+    groups_of = ((WQ,), (WK,), (WV,), (WO,), GU, GU, DN)
+    writes = [pltpu.make_async_copy(a, b, written.at[k]) for k, (a, b) in enumerate(zip(made, final))]
+    missing = set(ALL)
     for kind, index in SCHEDULE:
         steps[kind](index)
+        if kind == "f":
+            missing.discard(index)
+            for write, groups in zip(writes, groups_of):
+                if index in groups and not missing.intersection(groups):
+                    write.start()
     enc_copy.wait_recv()
     net.finish()
+    for write in writes:
+        write.wait()
 
 
 VMEM = pl.BlockSpec(memory_space=pltpu.VMEM)
+ANY = pl.BlockSpec(memory_space=pl.ANY)
 
 
 def call(inner, *args):
@@ -822,6 +837,8 @@
         pltpu.VMEM(act, BF),
         *[pltpu.VMEM(item.shape, item.dtype) for item in args[9:]],
         dma((8,)),
+        *[pltpu.VMEM(item.shape, F32) for item in args[9:16]],
+        dma((7,)),
     ]
     outs = [
         jax.ShapeDtypeStruct((MICRO, tokens, half), BF),
@@ -832,8 +849,8 @@
     return pl.pallas_call(
         functools.partial(kernel, inner, (tokens, width, half, ffh)),
         out_shape=outs,
-        in_specs=[VMEM] * 9 + [pl.BlockSpec(memory_space=pl.ANY)] * 8,
-        out_specs=[VMEM] * len(outs),
+        in_specs=[VMEM] * 9 + [ANY] * 8,
+        out_specs=[VMEM] * 2 + [ANY] * 7 + [VMEM],
         scratch_shapes=scratch,
         compiler_params=pltpu.CompilerParams(
             collective_id=0, has_side_effects=True, vmem_limit_bytes=63 * 2**20

time: 150 us -> 149 us (level)
  no operation moved by 1% of the time
where the time goes in v6:
time: 149 us
  Pallas kernels  148 us (99%)
    pallas_call x1, Pallas kernels, call(): pl.pallas_call(functools.partial(kernel, inner, (tokens, width, half, ffh...  145 us

profile of v6, /device:TPU:1, one launch (start us, length us, event | category | flops | bytes accessed | tf_op | source)
XLA Modules:
  0.0 148.5 jit_solution(12573591676260109614)
XLA Ops:
  0.7 145.3 %shard_map.272 = (bf16[2,256,384]{2,1,0:T(8,128)(2,1)}, f32[24,512]{1,0:T(8,128)}, f32[24,768]{1,0:T(8,128)}, f32[24,768]{1,0:T(8,128)}, f32[24,768]{1,0:T(8,128...) custom-call(s32[2,1,512]{2,1,0:T(1,128)} %refs_0_.1, ...), custom_call_target="tpu_custom_call" | custom-call | tf_op jit(solution)/shard_map/pallas_call | solution.py:849
  145.9 2.4 %shard_map.273 = (bf16[2,1,256,384]{3,2,1,0:T(8,128)(2,1)}, f32[24,259]{1,0:T(8,128)}, f32[16,24]{1,0:T(8,128)}, f32[1,24]{1,0:T(1,128)}, f32[1,24]{1,0:T(1,128)...) custom-call(bf16[2,256,384]{2,1,0:T(8,128)(2,1)} %get-tuple-element., ...), custom_call_target="tpu_custom_call" | custom-call | tf_op jit(solution)/shard_map/pallas_call | solution.py:911
